TPU v7x, 32 devices: a whole 2x2x4 slice. The times are simulated.
32 devices in a mesh: dp: 8 (over y, x, core), mod: 4 (over z).
Axes of the slice: x: 2, y: 2, z: 4, core: 2. Of those that a mesh axis runs over, the one named last changes fastest.
Arguments:
- block_input: bfloat16 [2, 16384, 768], P(None, ('dp', 'mod')), may hold values from -6 to 6
- grad_out: bfloat16 [2, 16384, 768], P(None, ('dp', 'mod')), may hold values from -6 to 6
- long_flag: int32 [2, 32], P(None, ('dp', 'mod')), may hold values from 0 to 1, as said below
- valid_mask: int32 [2, 16384], P(None, ('dp', 'mod')), may hold values from 0 to 1, as said below
- labels: int32 [2, 128], P(None, ('dp', 'mod')), may hold values from 0 to 999
- tsteps: int32 [2, 128], P(None, ('dp', 'mod')), may hold values from 0 to 999
- time_table: bfloat16 [1000, 768], replicated, may hold values from -5 to 5
- class_table: bfloat16 [1000, 768], replicated, may hold values from -5 to 5
- w_ada: bfloat16 [768, 4608], P(None, 'mod'), may hold values from -0.21875 to 0.21875
- b_ada: bfloat16 [4608], P('mod'), may hold values from -3 to 3
- w_qkv: bfloat16 [768, 2304], P('mod'), may hold values from -0.21875 to 0.21875
- qv_bias: bfloat16 [1536], P('mod'), may hold values from -2 to 2
- w_proj: bfloat16 [768, 768], P('mod'), may hold values from -0.875 to 0.875
- proj_bias: bfloat16 [768], P('mod'), may hold values from -2 to 2
- w_fc1: bfloat16 [768, 3072], P('mod'), may hold values from -0.21875 to 0.21875
- fc1_bias: bfloat16 [3072], P('mod'), may hold values from -2 to 2
- w_fc2: bfloat16 [3072, 768], P('mod'), may hold values from -0.109375 to 0.109375
- fc2_bias: bfloat16 [768], P('mod'), may hold values from -2 to 2
- rel_table: bfloat16 [12, 1023], P('mod'), may hold values from -5 to 5
Outputs:
- block_output: bfloat16 [2, 16384, 768], P(None, ('dp', 'mod'))
- grad_input: bfloat16 [2, 16384, 768], P(None, ('dp', 'mod'))
- grad_time_table: float32 [1000, 768], P('mod')
- grad_class_table: float32 [1000, 768], P('mod')
- grad_w_ada: float32 [768, 4608], P(None, 'mod')
- grad_b_ada: float32 [4608], P('mod')
- grad_w_qkv: float32 [768, 2304], P('mod')
- grad_qv_bias: float32 [1536], P('mod')
- grad_w_proj: float32 [768, 768], P('mod')
- grad_proj_bias: float32 [768], P('mod')
- grad_w_fc1: float32 [768, 3072], P('mod')
- grad_fc1_bias: float32 [3072], P('mod')
- grad_w_fc2: float32 [3072, 768], P('mod')
- grad_fc2_bias: float32 [768], P('mod')
- grad_rel_table: float32 [12, 1023], P('mod')
Inputs may be any that keep to these rules, and one draw needn't show every extreme that they name: `long_flag`: 1 marks a buffer holding one sample of 512 tokens; 0 a buffer holding 4 samples of 128 tokens. `valid_mask`: each segment of 128 tokens of a buffer is valid or padding as a whole; the first segment of every buffer is valid, and all of a buffer with long_flag 1 is valid.
All inputs are finite; a program needn't handle non-finite values.
Results may differ from a plain program's by a relative error of at most 0.015.
Values may be sent and summed in bfloat16 or wider, within the bound.
No kernel may reach another device: no remote copies, remote signals or barrier semaphores. Data moves between devices by JAX's collectives and lax.ppermute only.
A program may use at most 256 MiB of HBM per device.

v0:
```python
from functools import partial

import jax
import jax.numpy as jnp
from jax import lax
from jax.sharding import PartitionSpec as P

D = 768
H = 12
HD = 64
FF = 3072
NCLS = 1000
NT = 1000
LLONG = 512
LSHORT = 128
QB = 512
MICRO = 2
SEGS = 4


HIGH = lax.Precision.HIGHEST


def norm_parts(values):
    centred = values - jnp.mean(values, axis=1, keepdims=True)
    inverse_std = lax.rsqrt(jnp.mean(centred * centred, axis=1, keepdims=True) + 1e-06)
    return (centred * inverse_std, inverse_std)


def norm_backward(grad_norm, normed, inverse_std):
    return inverse_std * (
        grad_norm
        - jnp.mean(grad_norm, axis=1, keepdims=True)
        - normed * jnp.mean(grad_norm * normed, axis=1, keepdims=True)
    )


def bias_block(table, start_row, block_rows, length):
    heads = table.shape[0]
    padded = jnp.pad(table, ((0, 0), (0, 1)))
    width = block_rows + length
    tiled = jnp.broadcast_to(padded[:, None, :], (heads, block_rows, width))
    flat = tiled.reshape(heads, block_rows * width)[:, : block_rows * (width - 1)]
    skewed = flat.reshape(heads, block_rows, width - 1)
    return skewed[:, :, block_rows - 1 : block_rows - 1 + length]


def local(
    block_input,
    grad_out,
    long_flag,
    valid_mask,
    labels,
    tsteps,
    time_table,
    class_table,
    w_ada,
    b_ada,
    w_qkv,
    qv_bias,
    w_proj,
    proj_bias,
    w_fc1,
    fc1_bias,
    w_fc2,
    fc2_bias,
    rel_table,
):
    f32 = jnp.float32
    bf16 = jnp.bfloat16
    scale = HD ** (-0.5)
    mod_count = lax.axis_size("mod")
    mod_index = lax.axis_index("mod")
    (
        full_qkv,
        full_qv_bias,
        full_proj,
        full_proj_bias,
        full_fc1,
        full_fc1_bias,
        full_fc2,
        full_fc2_bias,
        full_table,
    ) = (
        lax.all_gather(w_qkv, "mod", axis=0, tiled=True),
        lax.all_gather(qv_bias, "mod", axis=0, tiled=True),
        lax.all_gather(w_proj, "mod", axis=0, tiled=True),
        lax.all_gather(proj_bias, "mod", axis=0, tiled=True),
        lax.all_gather(w_fc1, "mod", axis=0, tiled=True),
        lax.all_gather(fc1_bias, "mod", axis=0, tiled=True),
        lax.all_gather(w_fc2, "mod", axis=0, tiled=True),
        lax.all_gather(fc2_bias, "mod", axis=0, tiled=True),
        lax.all_gather(rel_table, "mod", axis=0, tiled=True),
    )
    qkv_bias = jnp.concatenate(
        [full_qv_bias[:D].astype(f32), jnp.zeros((D,), f32), full_qv_bias[D:].astype(f32)]
    )
    table_float = full_table.astype(f32)
    ada_bias = b_ada.astype(f32)
    ada_weight = w_ada.astype(f32)
    cond = time_table[tsteps].astype(f32) + class_table[labels].astype(f32)
    act_value, silu_pull = jax.vjp(jax.nn.silu, cond)
    act_low = act_value.astype(bf16)
    grad_qkv_w = jnp.zeros(full_qkv.shape, f32)
    grad_qkv_b = jnp.zeros((3 * D,), f32)
    grad_proj_w = jnp.zeros(full_proj.shape, f32)
    grad_proj_b = jnp.zeros((D,), f32)
    grad_fc1_w = jnp.zeros(full_fc1.shape, f32)
    grad_fc1_b = jnp.zeros((FF,), f32)
    grad_fc2_w = jnp.zeros(full_fc2.shape, f32)
    grad_fc2_b = jnp.zeros((D,), f32)
    grad_table = jnp.zeros(full_table.shape, f32)
    grad_ada_w = jnp.zeros(w_ada.shape, f32)
    grad_ada_b = jnp.zeros(b_ada.shape, f32)
    outputs = []
    input_grads = []
    cond_pieces = []
    positions = jnp.arange(LLONG)
    slots = jnp.arange(SEGS)
    for micro_step in range(MICRO):
        group_act = lax.all_gather(act_low[micro_step], "mod", axis=0, tiled=True)
        columns = jnp.dot(group_act, w_ada, preferred_element_type=f32) + ada_bias
        modulation = lax.all_to_all(columns, "mod", split_axis=0, concat_axis=1, tiled=True)
        is_long = long_flag[micro_step, 0]
        owner = jnp.where(is_long > 0, 0, slots)
        select = (owner[:, None] == slots[None, :]).astype(f32)
        mod_tok = jnp.repeat(jnp.dot(select, modulation, precision=HIGH), LSHORT, axis=0)
        shift1, scale1, gate1, shift2, scale2, gate2 = jnp.split(mod_tok, 6, axis=1)
        valid_row = valid_mask[micro_step]
        valid = valid_row.astype(f32)[:, None]
        sample = jnp.where(is_long > 0, 0, positions // LSHORT)
        allowed = (sample[:, None] == sample[None, :]) & (valid_row[None, :] > 0)
        tokens = block_input[micro_step].astype(f32)
        norm1, inverse1 = norm_parts(tokens)
        entry = (norm1 * (1.0 + scale1) + shift1).astype(bf16)
        qkv_low = (jnp.dot(entry, full_qkv, preferred_element_type=f32) + qkv_bias).astype(bf16)
        query = qkv_low[:, :D].reshape(LLONG, H, HD)
        keys_all = qkv_low[:, D : 2 * D].reshape(LLONG, H, HD)
        values_all = qkv_low[:, 2 * D :].reshape(LLONG, H, HD)

        def block_probs(start):
            scores = jnp.einsum("qhd,khd->hqk", query, keys_all, preferred_element_type=f32) * scale
            scores = scores + bias_block(table_float, start, QB, LLONG)
            scores = jnp.where(allowed[None], scores, -1e30)
            top = jnp.max(scores, axis=-1, keepdims=True)
            expo = jnp.exp(scores - top)
            return expo / jnp.sum(expo, axis=-1, keepdims=True)

        block = 0
        probs = block_probs(block * QB)
        attended_parts = jnp.einsum(
            "hqk,khd->qhd", probs.astype(bf16), values_all, preferred_element_type=f32
        )
        attended = attended_parts.reshape(LLONG, D).astype(bf16)
        attn = jnp.dot(attended, full_proj, preferred_element_type=f32) + full_proj_bias.astype(f32)
        hidden = tokens + valid * gate1 * attn
        norm2, inverse2 = norm_parts(hidden)
        m_in = (norm2 * (1.0 + scale2) + shift2).astype(bf16)
        upper = jnp.dot(m_in, full_fc1, preferred_element_type=f32) + full_fc1_bias.astype(f32)
        gelu_value, gelu_pull = jax.vjp(partial(jax.nn.gelu, approximate=True), upper)
        gelu_low = gelu_value.astype(bf16)
        mlp = jnp.dot(gelu_low, full_fc2, preferred_element_type=f32) + full_fc2_bias.astype(f32)
        outputs.append((hidden + valid * gate2 * mlp).astype(bf16))
        grad_y = grad_out[micro_step].astype(f32)
        grad_mlp = (grad_y * valid * gate2).astype(bf16)
        grad_gate2 = grad_y * valid * mlp
        grad_fc2_w = grad_fc2_w + jnp.dot(gelu_low.T, grad_mlp, preferred_element_type=f32)
        grad_fc2_b = grad_fc2_b + jnp.sum(grad_mlp.astype(f32), axis=0)
        grad_gelu = jnp.einsum("td,fd->tf", grad_mlp, full_fc2, preferred_element_type=f32)
        grad_upper = gelu_pull(grad_gelu)[0].astype(bf16)
        grad_fc1_w = grad_fc1_w + jnp.dot(m_in.T, grad_upper, preferred_element_type=f32)
        grad_fc1_b = grad_fc1_b + jnp.sum(grad_upper.astype(f32), axis=0)
        grad_min = jnp.einsum("tf,df->td", grad_upper, full_fc1, preferred_element_type=f32)
        grad_scale2 = grad_min * norm2
        grad_hidden = grad_y + norm_backward(grad_min * (1.0 + scale2), norm2, inverse2)
        grad_attn = (grad_hidden * valid * gate1).astype(bf16)
        grad_gate1 = grad_hidden * valid * attn
        grad_proj_w = grad_proj_w + jnp.dot(attended.T, grad_attn, preferred_element_type=f32)
        grad_proj_b = grad_proj_b + jnp.sum(grad_attn.astype(f32), axis=0)
        grad_attended = (
            jnp.einsum("te,de->td", grad_attn, full_proj, preferred_element_type=f32)
            .astype(bf16)
            .reshape(LLONG, H, HD)
        )
        block = 0
        start = block * QB
        probs = block_probs(start)
        grad_probs = jnp.einsum(
            "qhd,khd->hqk", grad_attended, values_all, preferred_element_type=f32
        )
        delta = jnp.sum(grad_probs * probs, axis=-1, keepdims=True)
        grad_scores = (probs * (grad_probs - delta)).astype(bf16)
        grad_query_parts = (
            jnp.einsum("hqk,khd->qhd", grad_scores, keys_all, preferred_element_type=f32) * scale
        )
        grad_keys = (
            jnp.einsum("hqk,qhd->khd", grad_scores, query, preferred_element_type=f32) * scale
        )
        grad_values = jnp.einsum(
            "hqk,qhd->khd", probs.astype(bf16), grad_attended, preferred_element_type=f32
        )
        bias_value, bias_pull = jax.vjp(
            partial(bias_block, start_row=start, block_rows=QB, length=LLONG), table_float
        )
        grad_table = grad_table + bias_pull(grad_scores.astype(f32))[0]
        grad_qkv = jnp.concatenate(
            [
                grad_query_parts.reshape(LLONG, D),
                grad_keys.reshape(LLONG, D),
                grad_values.reshape(LLONG, D),
            ],
            axis=1,
        ).astype(bf16)
        grad_qkv_w = grad_qkv_w + jnp.dot(entry.T, grad_qkv, preferred_element_type=f32)
        grad_qkv_b = grad_qkv_b + jnp.sum(grad_qkv.astype(f32), axis=0)
        grad_entry = jnp.einsum("te,de->td", grad_qkv, full_qkv, preferred_element_type=f32)
        grad_scale1 = grad_entry * norm1
        input_grads.append(
            (grad_hidden + norm_backward(grad_entry * (1.0 + scale1), norm1, inverse1)).astype(bf16)
        )
        grad_mod_tok = jnp.concatenate(
            [grad_entry, grad_scale1, grad_gate1, grad_min, grad_scale2, grad_gate2], axis=1
        )
        grad_mod_seg = jnp.sum(grad_mod_tok.reshape(SEGS, LSHORT, 6 * D), axis=1)
        grad_modulation = jnp.dot(select.T, grad_mod_seg, precision=HIGH)
        grad_columns = lax.all_to_all(
            grad_modulation.astype(jnp.bfloat16), "mod", split_axis=1, concat_axis=0, tiled=True
        ).astype(grad_modulation.dtype)
        grad_ada_w = grad_ada_w + jnp.dot(group_act.astype(f32).T, grad_columns, precision=HIGH)
        grad_ada_b = grad_ada_b + jnp.sum(grad_columns, axis=0)
        cond_share = jnp.dot(grad_columns, ada_weight.T, precision=HIGH)
        cond_pieces.append(
            lax.psum_scatter(
                cond_share.astype(jnp.bfloat16), "mod", scatter_dimension=0, tiled=True
            ).astype(jnp.float32)
        )
    grad_act = jnp.stack(cond_pieces, axis=0)
    grad_cond = silu_pull(grad_act)[0].reshape(MICRO * SEGS, D)
    time_onehot = (tsteps.reshape(MICRO * SEGS)[:, None] == jnp.arange(NT)[None, :]).astype(f32)
    class_onehot = (labels.reshape(MICRO * SEGS)[:, None] == jnp.arange(NCLS)[None, :]).astype(f32)
    grad_time = jnp.dot(time_onehot.T, grad_cond, precision=HIGH)
    grad_class = jnp.dot(class_onehot.T, grad_cond, precision=HIGH)
    grad_qv = jnp.concatenate([grad_qkv_b[:D], grad_qkv_b[2 * D :]])
    summed = lax.psum(
        (
            grad_time,
            grad_class,
            grad_qkv_w,
            grad_qv,
            grad_proj_w,
            grad_proj_b,
            grad_fc1_w,
            grad_fc1_b,
            grad_fc2_w,
            grad_fc2_b,
            grad_table,
        ),
        ("dp", "mod"),
    )
    shares = tuple(
        (
            lax.dynamic_slice_in_dim(
                whole, mod_index * (whole.shape[0] // mod_count), whole.shape[0] // mod_count, 0
            )
            for whole in summed
        )
    )
    ada_w_total, ada_b_total = (
        lax.psum(grad_ada_w.astype(jnp.bfloat16), "dp").astype(jnp.float32),
        lax.psum(grad_ada_b.astype(jnp.bfloat16), "dp").astype(jnp.float32),
    )
    return (
        jnp.stack(outputs, axis=0),
        jnp.stack(input_grads, axis=0),
        shares[0],
        shares[1],
        ada_w_total,
        ada_b_total,
        shares[2],
        shares[3],
        shares[4],
        shares[5],
        shares[6],
        shares[7],
        shares[8],
        shares[9],
        shares[10],
    )


def solution(mesh):
    in_specs = (
        P(None, ("dp", "mod"), None),
        P(None, ("dp", "mod"), None),
        P(None, ("dp", "mod")),
        P(None, ("dp", "mod")),
        P(None, ("dp", "mod")),
        P(None, ("dp", "mod")),
        P(),
        P(),
        P(None, "mod"),
        P("mod"),
        P("mod", None),
        P("mod"),
        P("mod", None),
        P("mod"),
        P("mod", None),
        P("mod"),
        P("mod", None),
        P("mod"),
        P("mod", None),
    )
    out_specs = (
        P(None, ("dp", "mod"), None),
        P(None, ("dp", "mod"), None),
        P("mod", None),
        P("mod", None),
        P(None, "mod"),
        P("mod"),
        P("mod", None),
        P("mod"),
        P("mod", None),
        P("mod"),
        P("mod", None),
        P("mod"),
        P("mod", None),
        P("mod"),
        P("mod", None),
    )
    return jax.shard_map(local, mesh=mesh, in_specs=in_specs, out_specs=out_specs, check_vma=False)
```

profile of v0, /device:TPU:0, one launch (start us, length us, event | category | flops | bytes accessed | tf_op | source)
XLA Modules:
  0.0 1603.6 jit_solution(13607103833708870394)
XLA Ops:
  16.0 15.2 all-gather.1
  42.9 12.5 all-reduce.12
  68.3 13.3 all-gather.3
  104.5 39.7 %copy.161 = f32[2,8,512,1024]{3,1,2,0:T(8,128)} copy(f32[2,8,512,1024]{3,2,1,0:T(8,128)S(1)} %bitcast.259) | data formatting | bytes 67108864
  144.2 22.8 %slice.108 = f32[12,523776]{1,0:T(8,128)} slice(f32[12,524288]{1,0:T(8,128)} %bitcast.262), slice={[0:12], [0:523776]} | slice | bytes 50282496 | tf_op jit(solution)/shard_map/slice | solution.py:43
  166.9 53.5 %reshape.401 = f32[12,512,1023]{2,1,0:T(8,128)} reshape(f32[12,523776]{1,0:T(8,128)} %slice.108) | data formatting | bytes 50282496 | tf_op jit(solution)/shard_map/reshape | solution.py:44
  220.4 13.4 slice.109
  233.9 12.8 copy.158
  247.9 13.2 all-gather.4
  261.7 13.4 all-gather
  327.0 15.2 fusion.146
  342.2 12.3 fusion.77
  466.1 15.2 fusion.147
  481.3 12.4 fusion.71
  536.1 12.3 fusion.74
  672.5 34.9 %reshape.419 = bf16[12,523776]{1,0:T(8,128)(2,1)} reshape(bf16[12,512,1023]{2,1,0:T(8,128)(2,1)} %pad.40.clone) | data formatting | bytes 25141248 | tf_op jit(solution)/shard_map/transpose(jvp())/reshape | solution.py:44
  716.0 36.1 %copy.163 = f32[2,8,512,1024]{3,2,1,0:T(8,128)} copy(f32[2,8,512,1024]{3,1,2,0:T(8,128)S(1)} %bitcast.260) | data formatting | bytes 67108864
  771.8 34.8 %reshape.416 = bf16[12,523776]{1,0:T(8,128)(2,1)} reshape(bf16[12,512,1023]{2,1,0:T(8,128)(2,1)} %pad.37.clone) | data formatting | bytes 25141248 | tf_op jit(solution)/shard_map/transpose(jvp())/reshape | solution.py:44
  815.2 35.8 %copy.162 = f32[2,8,512,1024]{3,2,1,0:T(8,128)} copy(f32[2,8,512,1024]{3,1,2,0:T(8,128)S(1)} %bitcast.261) | data formatting | bytes 67108864
  877.1 16.9 %all-reduce.11 = (bf16[16,768]{1,0:T(8,128)(2,1)S(1)}, bf16[16,768]{1,0:T(8,128)(2,1)S(1)}) all-reduce(bf16[16,768]{1,0:T(8,128)(2,1)S(1)} %convolution_convert_fusion.4, bf16[16,768]{1,0:T(8,128)(2,1)S(1)} %convolution_convert_fusion.5), channel_id=5, replica_groups=mesh['dp'=8,'mod'=4] {'mod'}, use_global_device_ids=true, to_apply=%region_25.26.clone | all-reduce | flops 24576 | bytes 98304
  905.4 82.6 %all-reduce.19.cloned.1.call-done = (f32[1536]{0:T(1024)}, f32[768]{0:T(1024)}, f32[3072]{0:T(1024)}, f32[768]{0:T(1024)}, f32[12,1023]{1,0:T(8,128)}) async-done(((f32[1536]{0:T(1024)}, f32[768]{0:T(1024)}, f32[3072]{0:T(1024)}, f32[768]{0:T(1024)}, f32[12,1023]{1,0:T(8,128)}), (f32[1536]{0:T(1024)}, f32[768]{0:T(1024)}, f32[3072]{0:T(1024)}, f32[768]{0:T(1024)}, ...) | async-done | bytes 73696 | tf_op jit(solution)/shard_map/psum | solution.py:244
  994.8 12.3 psum.94
  1007.8 44.8 %all-reduce.17.cloned.1.call-done = bf16[768,1152]{1,0:T(8,128)(2,1)} async-done(((bf16[768,1152]{1,0:T(8,128)(2,1)}), bf16[768,1152]{1,0:T(8,128)(2,1)}) %all-reduce.17.cloned.1.call-update) | async-done | bytes 1769488 | tf_op jit(solution)/shard_map/psum | solution.py:269
  1056.0 525.1 %all-reduce.21.cloned.1.call-done = (f32[1000,768]{1,0:T(8,128)}, f32[1000,768]{1,0:T(8,128)}, f32[768,2304]{1,0:T(8,128)}, f32[768,768]{1,0:T(8,128)}, f32[768,3072]{1,0:T(8,128)}, /*index=5*/f32[3072,768]{1,0:T(8,128)}) async-done(((f32[1000,768]{1,0:T(8,128)}, f32[1000,768]{1,0:T(8,128)}, f32[768,2304]{1,0:T(8,128)}, f32[768,768]{1,0:T(8,128)}, f32[768,3072]{1,0:T(8,128)}, ...) | async-done | bytes 34455568 | tf_op jit(solution)/shard_map/psum | solution.py:244
  (505 shorter events, 484.4 us)
Async XLA Ops:
  7.2 34.0 %copy-start.107 = (u32[32]{0:T(128)S(1)}, u32[32]{0:T(128)}, u32[]{:S(2)}) copy-start(u32[32]{0:T(128)} %constant.123) | copy-start | bytes 388
  7.2 31.6 %copy-start.112 = (s32[2,4]{1,0:T(2,128)S(1)}, s32[2,4]{1,0:T(2,128)}, u32[]{:S(2)}) copy-start(s32[2,4]{1,0:T(2,128)} %param.23) | copy-start | bytes 100
  7.2 30.9 %copy-start.111 = (s32[2,4]{1,0:T(2,128)S(1)}, s32[2,4]{1,0:T(2,128)}, u32[]{:S(2)}) copy-start(s32[2,4]{1,0:T(2,128)} %param.24) | copy-start | bytes 100
  7.2 32.2 %copy-start.109 = (s32[2,1]{0,1:T(1,128)S(1)}, s32[2,1]{0,1:T(1,128)}, u32[]{:S(2)}) copy-start(s32[2,1]{0,1:T(1,128)} %param.21) | copy-start | bytes 28
  7.2 35.2 %copy-start.116 = (bf16[192]{0:T(256)(128)(2,1)S(1)}, bf16[192]{0:T(256)(128)(2,1)}, u32[]{:S(2)}) copy-start(bf16[192]{0:T(256)(128)(2,1)} %param.32) | copy-start | bytes 1156
  7.3 35.4 %copy-start.117 = (bf16[192]{0:T(256)(128)(2,1)S(1)}, bf16[192]{0:T(256)(128)(2,1)}, u32[]{:S(2)}) copy-start(bf16[192]{0:T(256)(128)(2,1)} %param.36) | copy-start | bytes 1156
  7.3 48.1 %copy-start.8 = (bf16[2,512,768]{2,1,0:T(8,128)(2,1)S(1)}, bf16[2,512,768]{2,1,0:T(8,128)(2,1)}, u32[]{:S(2)}) copy-start(bf16[2,512,768]{2,1,0:T(8,128)(2,1)} %param.19) | copy-start | bytes 4718596
  7.3 295.3 %all-gather.10.cloned.1.call-start = ((), (), s32[]{:S(2)}) async-start(), calls=%async_computation.4 | async-start | bytes 4423680 | tf_op jit(solution)/shard_map/all_gather | solution.py:85
  8.0 346.5 %all-gather.12.cloned.1.call-start = ((), (), s32[]{:S(2)}) async-start(), calls=%async_computation.5 | async-start | bytes 1474560 | tf_op jit(solution)/shard_map/all_gather | solution.py:87
  8.8 47.5 %copy-start.110 = (bf16[384]{0:T(512)(128)(2,1)S(1)}, bf16[384]{0:T(512)(128)(2,1)}, u32[]{:S(2)}) copy-start(bf16[384]{0:T(512)(128)(2,1)} %param.30) | copy-start | bytes 2308
  8.8 59.5 %copy-start.102 = (bf16[3,1023]{1,0:T(4,128)(2,1)S(1)}, bf16[3,1023]{1,0:T(4,128)(2,1)}, u32[]{:S(2)}) copy-start(bf16[3,1023]{1,0:T(4,128)(2,1)} %param.37) | copy-start | bytes 18418
  8.8 356.3 %all-gather.14.cloned.1.call-start = ((), (), s32[]{:S(2)}) async-start(), calls=%async_computation.6 | async-start | bytes 5898240 | tf_op jit(solution)/shard_map/all_gather | solution.py:89
  32.8 249.4 %all-to-all-start.1 = ((f32[4,4,1152]{2,1,0:T(4,128)}), f32[4,4,1152]{2,1,0:T(4,128)S(1)}, u32[]{:S(2)}, u32[]{:S(2)}) async-start(f32[4,4,1152]{2,1,0:T(4,128)} %all_to_all.60), calls=%async_computation.1 | async-start | bytes 147456 | tf_op jit(solution)/shard_map/all_to_all | solution.py:123
  37.5 335.4 %all-gather.16.cloned.1.call-start = ((), (), s32[]{:S(2)}) async-start(), calls=%async_computation.7 | async-start | bytes 5898240 | tf_op jit(solution)/shard_map/all_gather | solution.py:91
  233.8 44.2 %copy-start.101 = (f32[512]{0:T(512)S(1)}, f32[512]{0:T(512)}, u32[]{:S(2)}) copy-start(f32[512]{0:T(512)} %get-tuple-element.24) | copy-start | bytes 6148
  279.7 113.7 %copy-start.87 = (f32[1,512]{1,0:T(1,128)}, f32[1,512]{1,0:T(1,128)S(1)}, u32[]{:S(2)}) copy-start(f32[1,512]{1,0:T(1,128)S(1)} %get-tuple-element.89) | copy-start | bytes 6148
  282.3 13.0 all-to-all-start
  360.8 32.6 %copy-start.84 = (f32[512]{0:T(512)}, f32[512]{0:T(512)S(1)}, u32[]{:S(2)}) copy-start(f32[512]{0:T(512)S(1)} %broadcast_multiply_fusion.8) | copy-start | bytes 6148
  361.9 31.5 %copy-start.89 = (f32[512]{0:T(512)}, f32[512]{0:T(512)S(1)}, u32[]{:S(2)}) copy-start(f32[512]{0:T(512)S(1)} %add_rsqrt_fusion) | copy-start | bytes 6148
  630.2 233.0 %all-to-all-start.3 = ((bf16[4,4,1152]{2,0,1:T(4,128)(2,1)}), bf16[4,4,1152]{2,0,1:T(4,128)(2,1)S(1)}, u32[]{:S(2)}, u32[]{:S(2)}) async-start(bf16[4,4,1152]{2,0,1:T(4,128)(2,1)} %bitcast.52), calls=%async_computation.3 | async-start | bytes 73728 | tf_op jit(solution)/shard_map/all_to_all | solution.py:226
  633.5 354.5 %all-reduce.19.cloned.1.call-start = ((), (), s32[]{:S(2)}) async-start(), calls=%async_computation.9 | async-start | bytes 188416 | tf_op jit(solution)/shard_map/psum | solution.py:244
  863.2 10.7 all-to-all-start.2
  868.2 184.3 %all-reduce.17.cloned.1.call-start = ((), (), s32[]{:S(2)}) async-start(), calls=%async_computation.8 | async-start | bytes 3538944 | tf_op jit(solution)/shard_map/psum | solution.py:269
  894.0 687.1 %all-reduce.21.cloned.1.call-start = ((), (), s32[]{:S(2)}) async-start(), calls=%async_computation.10 | async-start | bytes 68911104 | tf_op jit(solution)/shard_map/psum | solution.py:244
  (131 other events, 993.6 us)
Sparse Core Ops, SparseCore 0:
  9.7 75.3 all-gather.9
  86.7 29.2 all-gather.11
  117.5 88.5 all-gather.13
  207.5 90.2 all-gather.15
  863.3 124.5 all-reduce.18
  991.7 60.8 all-reduce.16
  1060.7 520.4 all-reduce.20
where the time goes:
time: 1610 us; the launch traced here: 1600 us
  waiting for transfers between devices  668 us (41%)
  local copies, waits for them, and re-layouts  421 us (26%)
  matrix products  242 us (15%)
  other arithmetic  127 us (8%)
  blocking collectives  109 us (7%)
  between operations  18.7 us (1%)
  starting transfers between devices  17.5 us (1%)
    psum x2, waiting for transfers between devices, local(): lax.psum((grad_time, grad_class, grad_qkv_w, grad_qv, grad_proj_w, grad_p...  608 us
    unnamed x305, local copies, waits for them, and re-layouts  182 us
    reshape x3, local copies, waits for them, and re-layouts, bias_block(): skewed = flat.reshape(heads, block_rows, width - 1)  123 us
    psum x1, waiting for transfers between devices, local(): lax.psum(grad_ada_w.astype(jnp.bfloat16), 'dp').astype(jnp.float32)  44.8 us
  transfers between devices with their start and end apart: 11, of which 5 were waited for; matrix products, arithmetic and copies ran while one was open for 32% of the time, Pallas kernels for 0%

commit v1 on v0

v1 whole, which is shorter than its diff:
```python
from functools import partial
import jax
import jax.numpy as jnp
from jax import lax
from jax.experimental import pallas as pl
from jax.experimental.pallas import tpu as pltpu
from jax.sharding import PartitionSpec as P

f32 = jnp.float32
bf16 = jnp.bfloat16
D = 768
H = 12
HD = 64
FF = 3072
L = 512
SEG = 128
NSEG = 4
MICRO = 2
T = MICRO * L
HALF = 384
FH = 1536
VMEM_LIMIT = 56 * 1024 * 1024


def params(*sem):
    return pltpu.CompilerParams(vmem_limit_bytes=VMEM_LIMIT, dimension_semantics=sem)


def dot(a, b, ca=1, cb=0):
    return lax.dot_general(a, b, (((ca,), (cb,)), ((), ())), preferred_element_type=f32)


def norm_of(values):
    centred = values - jnp.mean(values, axis=1, keepdims=True)
    inverse = lax.rsqrt(jnp.mean(centred * centred, axis=1, keepdims=True) + 1e-6)
    return centred * inverse, inverse


def norm_back(grad, normed, inverse):
    return inverse * (
        grad
        - jnp.mean(grad, axis=1, keepdims=True)
        - normed * jnp.mean(grad * normed, axis=1, keepdims=True)
    )


def qkv_first_body(x_ref, mod_ref, w_ref, b_ref, a_ref, qkv_ref):
    for s in range(NSEG):
        rows = pl.ds(s * SEG, SEG)
        norm, _ = norm_of(x_ref[rows, :].astype(f32))
        a_ref[rows, :] = (norm * (1.0 + mod_ref[s, 1:2, :]) + mod_ref[s, 0:1, :]).astype(bf16)
    qkv_ref[...] = (dot(a_ref[...], w_ref[...]) + b_ref[...]).astype(bf16)


def qkv_first(x, mods, w, b):
    return pl.pallas_call(
        qkv_first_body,
        grid=(MICRO,),
        in_specs=[
            pl.BlockSpec((L, D), lambda i: (i, 0)),
            pl.BlockSpec((NSEG, 6, D), lambda i: (i, 0, 0)),
            pl.BlockSpec((D, 3 * HALF), lambda i: (0, 0)),
            pl.BlockSpec((1, 3 * HALF), lambda i: (0, 0)),
        ],
        out_specs=[
            pl.BlockSpec((L, D), lambda i: (i, 0)),
            pl.BlockSpec((L, 3 * HALF), lambda i: (i, 0)),
        ],
        out_shape=[
            jax.ShapeDtypeStruct((T, D), bf16),
            jax.ShapeDtypeStruct((T, 3 * HALF), bf16),
        ],
        compiler_params=params("arbitrary"),
        cost_estimate=pl.CostEstimate(flops=2 * T * D * 3 * HALF, bytes_accessed=8_000_000, transcendentals=0),
        name="qkv_first",
    )(x, mods, w, b)


def qkv_second_body(a_ref, w_ref, b_ref, qkv_ref):
    qkv_ref[...] = (dot(a_ref[...], w_ref[...]) + b_ref[...]).astype(bf16)


def qkv_second(a, w, b):
    return pl.pallas_call(
        qkv_second_body,
        grid=(MICRO,),
        in_specs=[
            pl.BlockSpec((L, D), lambda i: (i, 0)),
            pl.BlockSpec((D, 3 * HALF), lambda i: (0, 0)),
            pl.BlockSpec((1, 3 * HALF), lambda i: (0, 0)),
        ],
        out_specs=pl.BlockSpec((L, 3 * HALF), lambda i: (i, 0)),
        out_shape=jax.ShapeDtypeStruct((T, 3 * HALF), bf16),
        compiler_params=params("arbitrary"),
        cost_estimate=pl.CostEstimate(flops=2 * T * D * 3 * HALF, bytes_accessed=6_000_000, transcendentals=0),
        name="qkv_second",
    )(a, w, b)


def attend_body(long_ref, valid_ref, q_ref, k_ref, v_ref, t_ref, o_ref, p_ref, bias_ref):
    b = pl.program_id(1)

    @pl.when(b == 0)
    def _():
        for h in range(2):
            for d in range(7):
                row = jnp.broadcast_to(t_ref[h, d : d + 1, :], (SEG, 2 * SEG))
                bias_ref[h, d] = pltpu.roll(row, SEG + 1, 1, stride=1, stride_axis=0)[:, :SEG]

    is_long = long_ref[b]
    lane = lax.broadcasted_iota(jnp.int32, (L, 2 * HD), 1)
    query = q_ref[...] * jnp.asarray(HD**-0.5, bf16)
    keys = k_ref[...]
    values_t = v_ref[...].T
    outs = []
    for h in range(2):
        mine = (lane < HD) if h == 0 else (lane >= HD)
        key_h = jnp.where(mine, keys, jnp.zeros_like(keys))
        for qb in range(NSEG):
            cols = pl.ds(qb * SEG, SEG)
            scores = dot(key_h, query[qb * SEG : (qb + 1) * SEG, :], 1, 1)
            parts = []
            for kb in range(NSEG):
                open_ = (valid_ref[b, kb] > 0) if kb == qb else ((valid_ref[b, kb] > 0) & (is_long > 0))
                shut = jnp.where(open_, 0.0, -1e30).astype(f32)
                parts.append(scores[kb * SEG : (kb + 1) * SEG, :] + (bias_ref[h, kb - qb + 3] + shut))
            scores = jnp.concatenate(parts, axis=0)
            top = jnp.max(scores, axis=0, keepdims=True)
            expo = jnp.exp(scores - top)
            total = jnp.sum(expo, axis=0, keepdims=True)
            p_ref[0, h, :, cols] = (expo * (1.0 / total)).astype(bf16)
        outs.append(dot(values_t[h * HD : (h + 1) * HD, :], p_ref[0, h]))
    o_ref[...] = jnp.concatenate(outs, axis=0).T.astype(bf16)


def attend(qkv, table, long_flag, valid_seg):
    pairs = 3
    return pl.pallas_call(
        attend_body,
        grid_spec=pltpu.PrefetchScalarGridSpec(
            num_scalar_prefetch=2,
            grid=(pairs, MICRO),
            in_specs=[
                pl.BlockSpec((L, 2 * HD), lambda g, b, *_: (b, g)),
                pl.BlockSpec((L, 2 * HD), lambda g, b, *_: (b, 3 + g)),
                pl.BlockSpec((L, 2 * HD), lambda g, b, *_: (b, 6 + g)),
                pl.BlockSpec((2, 8, 2 * SEG), lambda g, b, *_: (g, 0, 0)),
            ],
            out_specs=[
                pl.BlockSpec((L, 2 * HD), lambda g, b, *_: (b, g)),
                pl.BlockSpec((1, 2, L, L), lambda g, b, *_: (b, g, 0, 0)),
            ],
            scratch_shapes=[pltpu.VMEM((2, 7, SEG, SEG), f32)],
        ),
        out_shape=[
            jax.ShapeDtypeStruct((T, HALF), bf16),
            jax.ShapeDtypeStruct((MICRO, 6, L, L), bf16),
        ],
        compiler_params=params("arbitrary", "arbitrary"),
        cost_estimate=pl.CostEstimate(flops=16_000_000_000, bytes_accessed=10_000_000, transcendentals=0),
        name="attend",
    )(long_flag, valid_seg, qkv, qkv, qkv, table)


def middle_body(half_ref, o1_ref, o2_ref, w_ref, b_ref, x_ref, dy_ref, mod_ref,
                h_ref, m_ref, attn_ref, dmlp_ref, db_ref):
    first = pl.multiple_of(half_ref[0] * HALF, HALF)
    second = pl.multiple_of((1 - half_ref[0]) * HALF, HALF)
    attn = dot(o1_ref[...], w_ref[pl.ds(first, HALF), :]) + dot(o2_ref[...], w_ref[pl.ds(second, HALF), :])
    attn = attn + b_ref[...]
    attn_ref[...] = attn.astype(bf16)
    total = jnp.zeros((1, D), f32)
    for s in range(NSEG):
        rows = pl.ds(s * SEG, SEG)
        hidden = x_ref[rows, :].astype(f32) + mod_ref[s, 2:3, :] * attn[s * SEG : (s + 1) * SEG, :]
        h_ref[rows, :] = hidden
        norm, _ = norm_of(hidden)
        m_ref[rows, :] = (norm * (1.0 + mod_ref[s, 4:5, :]) + mod_ref[s, 3:4, :]).astype(bf16)
        dmlp = (dy_ref[rows, :].astype(f32) * mod_ref[s, 5:6, :]).astype(bf16)
        dmlp_ref[rows, :] = dmlp
        total = total + jnp.sum(dmlp.astype(f32), axis=0, keepdims=True)

    @pl.when(pl.program_id(0) == 0)
    def _():
        db_ref[...] = jnp.zeros_like(db_ref)

    db_ref[0:1, :] += total


def middle(half, o1, o2, w, b, x, dy, mods):
    row = lambda i, *_: (i, 0)
    zero = lambda i, *_: (0, 0)
    return pl.pallas_call(
        middle_body,
        grid_spec=pltpu.PrefetchScalarGridSpec(
            num_scalar_prefetch=1,
            grid=(MICRO,),
            in_specs=[
                pl.BlockSpec((L, HALF), row),
                pl.BlockSpec((L, HALF), row),
                pl.BlockSpec((D, D), zero),
                pl.BlockSpec((1, D), zero),
                pl.BlockSpec((L, D), row),
                pl.BlockSpec((L, D), row),
                pl.BlockSpec((NSEG, 6, D), lambda i, *_: (i, 0, 0)),
            ],
            out_specs=[
                pl.BlockSpec((L, D), row),
                pl.BlockSpec((L, D), row),
                pl.BlockSpec((L, D), row),
                pl.BlockSpec((L, D), row),
                pl.BlockSpec((8, D), zero),
            ],
        ),
        out_shape=[
            jax.ShapeDtypeStruct((T, D), f32),
            jax.ShapeDtypeStruct((T, D), bf16),
            jax.ShapeDtypeStruct((T, D), bf16),
            jax.ShapeDtypeStruct((T, D), bf16),
            jax.ShapeDtypeStruct((8, D), f32),
        ],
        compiler_params=params("arbitrary"),
        cost_estimate=pl.CostEstimate(flops=4 * T * D * D, bytes_accessed=16_000_000, transcendentals=0),
        name="middle",
    )(half, o1, o2, w, b, x, dy, mods)


FB = 512


def mlp_body(has_acc, m_ref, dmlp_ref, w1_ref, w2_ref, b_ref, *refs):
    if has_acc:
        acc_o, acc_d, out_o, out_d, dw1_ref, dw2_ref, db_ref, g_s, du_s = refs
    else:
        out_o, out_d, dw1_ref, dw2_ref, db_ref, g_s, du_s = refs
    f = pl.program_id(0)
    w1 = w1_ref[...]
    w2 = w2_ref[...]
    bias = b_ref[0:1, :]
    chunk = 256
    total = jnp.zeros((1, FB), f32)
    c0 = (2.0 / jnp.pi) ** 0.5
    for r in range(T // chunk):
        rows = pl.ds(r * chunk, chunk)
        u = dot(m_ref[rows, :], w1) + bias
        dg = dot(dmlp_ref[rows, :], w2, 1, 1)
        u2 = u * u
        th = jnp.tanh(u * (c0 + (c0 * 0.044715) * u2))
        half = 0.5 + 0.5 * th
        g_s[rows, :] = (u * half).astype(bf16)
        slope = half + u * (0.5 - 0.5 * th * th) * (c0 + (3.0 * c0 * 0.044715) * u2)
        du = (dg * slope).astype(bf16)
        du_s[rows, :] = du
        total = total + jnp.sum(du.astype(f32), axis=0, keepdims=True)
    db_ref[0:1, :] = total

    @pl.when(f == 0)
    def _():
        if has_acc:
            out_o[...] = acc_o[...] + dot(g_s[...], w2)
            out_d[...] = acc_d[...] + dot(du_s[...], w1, 1, 1)
        else:
            out_o[...] = dot(g_s[...], w2)
            out_d[...] = dot(du_s[...], w1, 1, 1)

    @pl.when(f > 0)
    def _():
        out_o[...] += dot(g_s[...], w2)
        out_d[...] += dot(du_s[...], w1, 1, 1)

    dw2_ref[...] = dot(g_s[...], dmlp_ref[...], 0, 0).astype(bf16)
    dw1_ref[...] = dot(m_ref[...], du_s[...], 0, 0).astype(bf16)


def mlp(m_in, dmlp, w1, w2, b1, acc=None):
    zero = lambda f: (0, 0)
    col = lambda f: (0, f)
    once = pl.Buffered(1)
    specs = [
        pl.BlockSpec((T, D), zero, pipeline_mode=once),
        pl.BlockSpec((T, D), zero, pipeline_mode=once),
        pl.BlockSpec((D, FB), col),
        pl.BlockSpec((FB, D), lambda f: (f, 0)),
        pl.BlockSpec((1, FB), col),
    ]
    args = [m_in, dmlp, w1, w2, b1]
    alias = {}
    if acc is not None:
        specs += [pl.BlockSpec((T, D), zero, pipeline_mode=once)] * 2
        args += list(acc)
    return pl.pallas_call(
        partial(mlp_body, acc is not None),
        grid=(FH // FB,),
        in_specs=specs,
        out_specs=[
            pl.BlockSpec((T, D), zero),
            pl.BlockSpec((T, D), zero),
            pl.BlockSpec((D, FB), col),
            pl.BlockSpec((FB, D), lambda f: (f, 0)),
            pl.BlockSpec((8, FB), col),
        ],
        out_shape=[
            jax.ShapeDtypeStruct((T, D), f32),
            jax.ShapeDtypeStruct((T, D), f32),
            jax.ShapeDtypeStruct((D, FH), bf16),
            jax.ShapeDtypeStruct((FH, D), bf16),
            jax.ShapeDtypeStruct((8, FH), f32),
        ],
        scratch_shapes=[pltpu.VMEM((T, FB), bf16), pltpu.VMEM((T, FB), bf16)],
        compiler_params=params("arbitrary"),
        cost_estimate=pl.CostEstimate(flops=12 * T * D * FH, bytes_accessed=24_000_000, transcendentals=0),
        name="mlp",
    )(*args)


def back_middle_body(half_ref, h_ref, dy_ref, mlp_ref, b2_ref, dm_ref, attn_ref, mod_ref, o1_ref, o2_ref, w_ref,
                     y_ref, dh_ref, do1_ref, do2_ref, dws_ref, dwk_ref, dmod_ref, db_ref, dattn_s, dw_s):
    i = pl.program_id(0)
    first = pl.multiple_of(half_ref[0] * HALF, HALF)
    second = pl.multiple_of((1 - half_ref[0]) * HALF, HALF)
    total = jnp.zeros((1, D), f32)
    for s in range(NSEG):
        rows = pl.ds(s * SEG, SEG)
        hidden = h_ref[rows, :]
        dy = dy_ref[rows, :].astype(f32)
        ff = mlp_ref[rows, :] + b2_ref[...]
        y_ref[rows, :] = (hidden + mod_ref[s, 5:6, :] * ff).astype(bf16)
        dmod_ref[s, 5:6, :] = jnp.sum(dy * ff, axis=0, keepdims=True)
        norm, inverse = norm_of(hidden)
        dm = dm_ref[rows, :]
        dmod_ref[s, 3:4, :] = jnp.sum(dm, axis=0, keepdims=True)
        dmod_ref[s, 4:5, :] = jnp.sum(dm * norm, axis=0, keepdims=True)
        dh = dy + norm_back(dm * (1.0 + mod_ref[s, 4:5, :]), norm, inverse)
        dh_ref[rows, :] = dh
        dmod_ref[s, 2:3, :] = jnp.sum(dh * attn_ref[rows, :].astype(f32), axis=0, keepdims=True)
        dattn = (dh * mod_ref[s, 2:3, :]).astype(bf16)
        dattn_s[rows, :] = dattn
        total = total + jnp.sum(dattn.astype(f32), axis=0, keepdims=True)
    dmod_ref[:, 0:2, :] = jnp.zeros((NSEG, 2, D), f32)
    dattn = dattn_s[...]
    do1_ref[...] = dot(dattn, w_ref[pl.ds(first, HALF), :], 1, 1).astype(bf16)
    do2_ref[...] = dot(dattn, w_ref[pl.ds(second, HALF), :], 1, 1).astype(bf16)

    @pl.when(i == 0)
    def _():
        db_ref[...] = jnp.zeros_like(db_ref)
        dw_s[...] = jnp.zeros_like(dw_s)

    db_ref[0:1, :] += total
    dw_s[pl.ds(first, HALF), :] += dot(o1_ref[...], dattn, 0, 0)
    dw_s[pl.ds(second, HALF), :] += dot(o2_ref[...], dattn, 0, 0)

    @pl.when(i == MICRO - 1)
    def _():
        dws_ref[...] = dw_s[:, pl.ds(first, HALF)].astype(bf16)
        dwk_ref[...] = dw_s[:, pl.ds(second, HALF)].astype(bf16)


def back_middle(half, h, dy, ff, b2, dm, attn, mods, o1, o2, w):
    row = lambda i, *_: (i, 0)
    zero = lambda i, *_: (0, 0)
    full = pl.BlockSpec((L, D), row)
    part = pl.BlockSpec((L, HALF), row)
    modspec = pl.BlockSpec((NSEG, 6, D), lambda i, *_: (i, 0, 0))
    return pl.pallas_call(
        back_middle_body,
        grid_spec=pltpu.PrefetchScalarGridSpec(
            num_scalar_prefetch=1,
            grid=(MICRO,),
            in_specs=[full, full, full, pl.BlockSpec((1, D), zero), full, full, modspec, part, part,
                      pl.BlockSpec((D, D), zero)],
            out_specs=[full, full, part, part, pl.BlockSpec((D, HALF), zero), pl.BlockSpec((D, HALF), zero),
                       modspec, pl.BlockSpec((8, D), zero)],
            scratch_shapes=[pltpu.VMEM((L, D), bf16), pltpu.VMEM((D, D), f32)],
        ),
        out_shape=[
            jax.ShapeDtypeStruct((T, D), bf16),
            jax.ShapeDtypeStruct((T, D), f32),
            jax.ShapeDtypeStruct((T, HALF), bf16),
            jax.ShapeDtypeStruct((T, HALF), bf16),
            jax.ShapeDtypeStruct((D, HALF), bf16),
            jax.ShapeDtypeStruct((D, HALF), bf16),
            jax.ShapeDtypeStruct((MICRO * NSEG, 6, D), f32),
            jax.ShapeDtypeStruct((8, D), f32),
        ],
        compiler_params=params("arbitrary"),
        cost_estimate=pl.CostEstimate(flops=8 * T * D * D, bytes_accessed=24_000_000, transcendentals=0),
        name="back_middle",
    )(half, h, dy, ff, b2, dm, attn, mods, o1, o2, w)


def attend_back_body(q_ref, k_ref, v_ref, p_ref, do_ref, o_ref, dq_ref, dk_ref, dv_ref, dt_ref, db_ref, acc_ref, ds_s):
    b = pl.program_id(1)

    @pl.when(b == 0)
    def _():
        acc_ref[...] = jnp.zeros_like(acc_ref)
        db_ref[...] = jnp.zeros_like(db_ref)

    lane = lax.broadcasted_iota(jnp.int32, (L, 2 * HD), 1)
    query = q_ref[...]
    keys_t = k_ref[...].T
    values = v_ref[...]
    dout = do_ref[...]
    prod = (dout.astype(f32) * o_ref[...].astype(f32)).T
    dqs, dks, dvs = [], [], []
    for h in range(2):
        mine = (lane < HD) if h == 0 else (lane >= HD)
        value_h = jnp.where(mine, values, jnp.zeros_like(values))
        delta = jnp.sum(prod[h * HD : (h + 1) * HD, :], axis=0, keepdims=True)
        for qb in range(NSEG):
            cols = slice(qb * SEG, (qb + 1) * SEG)
            dp = dot(value_h, dout[cols, :], 1, 1)
            ds = (p_ref[0, h, :, cols].astype(f32) * (dp - delta[:, cols])).astype(bf16)
            ds_s[h, :, cols] = ds
            for kb in range(NSEG):
                acc_ref[h, kb - qb + 3] += ds[kb * SEG : (kb + 1) * SEG, :].astype(f32)
        dvs.append(dot(p_ref[0, h], dout))
        dks.append(dot(ds_s[h], query))
        dqs.append(dot(keys_t[h * HD : (h + 1) * HD, :], ds_s[h]))
    low = lane < HD
    scale = HD**-0.5
    dq = (jnp.concatenate(dqs, axis=0).T * scale).astype(bf16)
    dk = (jnp.where(low, dks[0], dks[1]) * scale).astype(bf16)
    dv = jnp.where(low, dvs[0], dvs[1]).astype(bf16)
    dq_ref[...] = dq
    dk_ref[...] = dk
    dv_ref[...] = dv
    db_ref[0:1, :] += jnp.sum(dq.astype(f32), axis=0, keepdims=True)
    db_ref[1:2, :] += jnp.sum(dv.astype(f32), axis=0, keepdims=True)

    @pl.when(b == MICRO - 1)
    def _():
        for h in range(2):
            for d in range(7):
                wide = jnp.concatenate([acc_ref[h, d], jnp.zeros((SEG, SEG), f32)], axis=1)
                rows = SEG
                while rows > 1:
                    rows //= 2
                    wide = pltpu.roll(wide[:rows], rows, 1) + wide[rows:]
                dt_ref[h, d : d + 1, :] = wide
            dt_ref[h, 7:8, :] = jnp.zeros((1, 2 * SEG), f32)


def attend_back(qkv, p, dout, out):
    col = lambda g, b: (b, g)
    part = pl.BlockSpec((L, 2 * HD), col)
    return pl.pallas_call(
        attend_back_body,
        grid=(3, MICRO),
        in_specs=[
            part,
            pl.BlockSpec((L, 2 * HD), lambda g, b: (b, 3 + g)),
            pl.BlockSpec((L, 2 * HD), lambda g, b: (b, 6 + g)),
            pl.BlockSpec((1, 2, L, L), lambda g, b: (b, g, 0, 0)),
            part,
            part,
        ],
        out_specs=[part, part, part, pl.BlockSpec((2, 8, 2 * SEG), lambda g, b: (g, 0, 0)),
                   pl.BlockSpec((8, 2 * HD), lambda g, b: (0, g))],
        out_shape=[jax.ShapeDtypeStruct((T, HALF), bf16)] * 3
        + [jax.ShapeDtypeStruct((6, 8, 2 * SEG), f32), jax.ShapeDtypeStruct((8, HALF), f32)],
        scratch_shapes=[pltpu.VMEM((2, 7, SEG, SEG), f32), pltpu.VMEM((2, L, L), bf16)],
        compiler_params=params("arbitrary", "arbitrary"),
        cost_estimate=pl.CostEstimate(flops=24_000_000_000, bytes_accessed=12_000_000, transcendentals=0),
        name="attend_back",
    )(qkv, qkv, qkv, p, dout, out)


def qkv_weight_body(a_ref, dq_ref, dk_ref, dv_ref, out_ref):
    a = a_ref[...]
    out_ref[:, 0:HALF] = dot(a, dq_ref[...], 0, 0).astype(bf16)
    out_ref[:, HALF : 2 * HALF] = dot(a, dk_ref[...], 0, 0).astype(bf16)
    out_ref[:, 2 * HALF : 3 * HALF] = dot(a, dv_ref[...], 0, 0).astype(bf16)


def qkv_weight(a, dq, dk, dv):
    return pl.pallas_call(
        qkv_weight_body,
        out_shape=jax.ShapeDtypeStruct((D, 3 * HALF), bf16),
        compiler_params=params(),
        cost_estimate=pl.CostEstimate(flops=2 * T * D * 3 * HALF, bytes_accessed=6_000_000, transcendentals=0),
        name="qkv_weight",
    )(a, dq, dk, dv)


def back_entry_body(dq1, dk1, dv1, dq2, dk2, dv2, w1_ref, w2_ref, x_ref, dh_ref, mod_ref, dx_ref, dmod_ref):
    da = dot(dq1[...], w1_ref[:, 0:HALF], 1, 1)
    da += dot(dk1[...], w1_ref[:, HALF : 2 * HALF], 1, 1)
    da += dot(dv1[...], w1_ref[:, 2 * HALF : 3 * HALF], 1, 1)
    da += dot(dq2[...], w2_ref[:, 0:HALF], 1, 1)
    da += dot(dk2[...], w2_ref[:, HALF : 2 * HALF], 1, 1)
    da += dot(dv2[...], w2_ref[:, 2 * HALF : 3 * HALF], 1, 1)
    for s in range(NSEG):
        rows = pl.ds(s * SEG, SEG)
        piece = da[s * SEG : (s + 1) * SEG, :]
        norm, inverse = norm_of(x_ref[rows, :].astype(f32))
        dmod_ref[s, 0:1, :] = jnp.sum(piece, axis=0, keepdims=True)
        dmod_ref[s, 1:2, :] = jnp.sum(piece * norm, axis=0, keepdims=True)
        dx_ref[rows, :] = (
            dh_ref[rows, :] + norm_back(piece * (1.0 + mod_ref[s, 1:2, :]), norm, inverse)
        ).astype(bf16)


def back_entry(parts, w1, w2, x, dh, mods):
    row = lambda i: (i, 0)
    zero = lambda i: (0, 0)
    full = pl.BlockSpec((L, D), row)
    part = pl.BlockSpec((L, HALF), row)
    return pl.pallas_call(
        back_entry_body,
        grid=(MICRO,),
        in_specs=[part] * 6 + [pl.BlockSpec((D, 3 * HALF), zero)] * 2 + [full, full, pl.BlockSpec((NSEG, 6, D), lambda i: (i, 0, 0))],
        out_specs=[full, pl.BlockSpec((NSEG, 2, D), lambda i: (i, 0, 0))],
        out_shape=[jax.ShapeDtypeStruct((T, D), bf16), jax.ShapeDtypeStruct((MICRO * NSEG, 2, D), f32)],
        compiler_params=params("arbitrary"),
        cost_estimate=pl.CostEstimate(flops=4 * T * D * 3 * HALF, bytes_accessed=16_000_000, transcendentals=0),
        name="back_entry",
    )(*parts, w1, w2, x, dh, mods)


def place_body(order, idx_ref, own_ref, near_ref, far_ref, out_ref, sems):
    count = near_ref.shape[1] + 1
    rows, piece = own_ref.shape[0], near_ref.shape[2]
    me, spot = idx_ref[0], idx_ref[1]
    copies = [pltpu.make_async_copy(own_ref, out_ref.at[pl.ds(pl.multiple_of(me * rows, rows), rows), :], sems.at[0])]
    first, second = order
    for k in range(1, count):
        base = lax.rem(me + count - k, count) * rows
        for n, (ref, slot, other) in enumerate(
            ((near_ref, 0, 0), (near_ref, 1, first), (far_ref, 0, second), (far_ref, 1, first + second))
        ):
            start = pl.multiple_of(base + lax.bitwise_xor(spot, other) * piece, 16)
            copies.append(
                pltpu.make_async_copy(
                    ref.at[slot, k - 1], out_ref.at[pl.ds(start, piece), :], sems.at[1 + 4 * (k - 1) + n]
                )
            )
    for copy in copies:
        copy.start()
    for copy in copies:
        copy.wait()


def place(idx, own, near, far, order):
    count = near.shape[1] + 1
    rows, width = own.shape
    anywhere = pl.BlockSpec(memory_space=pl.ANY)
    return pl.pallas_call(
        partial(place_body, order),
        in_specs=[pl.BlockSpec(memory_space=pltpu.SMEM), anywhere, anywhere, anywhere],
        out_specs=anywhere,
        out_shape=jax.ShapeDtypeStruct((count * rows, width), own.dtype),
        scratch_shapes=[pltpu.SemaphoreType.DMA((1 + 4 * (count - 1),))],
        compiler_params=pltpu.CompilerParams(vmem_limit_bytes=8 * 1024 * 1024),
        cost_estimate=pl.CostEstimate(flops=0, bytes_accessed=4 * count * rows * width, transcendentals=0),
        name="place",
    )(idx, own, near, far)


def finish_ff_body(idx_ref, mine_ref, peer_ref, fc1_ref, fc2_ref):
    spot, core = idx_ref[1], idx_ref[2]
    for source, half in ((mine_ref, core), (peer_ref, 1 - core)):
        for j in range(4):
            place_at = lax.bitwise_xor(spot, j)
            low, high = lax.rem(place_at, 2), lax.div(place_at, 2)
            row = pl.multiple_of((2 * low + high) * 48, 16)
            for z in range(4):
                source_rows = pl.ds(48 * (z // 2), 48)
                block = source[j, source_rows, (z % 2) * HALF : (z % 2 + 1) * HALF]
                column = pl.multiple_of((2 * z + half) * HALF, 128)
                fc1_ref[pl.ds(row, 48), pl.ds(column, HALF)] = block.astype(f32)
            row = pl.multiple_of(half * HALF + (2 * high + low) * 96, 16)
            fc2_ref[pl.ds(row, 96), :] = source[j, 96:192, :].astype(f32)


def finish_ff(idx, mine, peer):
    vmem = pl.BlockSpec(memory_space=pltpu.VMEM)
    return pl.pallas_call(
        finish_ff_body,
        in_specs=[pl.BlockSpec(memory_space=pltpu.SMEM), vmem, vmem],
        out_specs=[vmem, vmem],
        out_shape=[jax.ShapeDtypeStruct((D // 4, FF), f32), jax.ShapeDtypeStruct((FF // 4, D), f32)],
        compiler_params=params(),
        cost_estimate=pl.CostEstimate(flops=0, bytes_accessed=8_000_000, transcendentals=0),
        name="finish_ff",
    )(idx, mine, peer)


def finish_attn_body(idx_ref, mine_ref, peer_ref, qkv_ref, proj_ref):
    spot, core = idx_ref[1], idx_ref[2]
    for source, half in ((mine_ref, core), (peer_ref, 1 - core)):
        column = half * HALF
        for j in range(4):
            place_at = lax.bitwise_xor(spot, j)
            low, high = lax.rem(place_at, 2), lax.div(place_at, 2)
            row0 = pl.multiple_of((2 * low + high) * 48, 16)
            row1 = pl.multiple_of((2 * high + low) * 48, 16)
            for t in range(4):
                block = source[j, 48 * (t // 2) : 48 * (t // 2 + 1), (t % 2) * HALF : (t % 2 + 1) * HALF].astype(f32)
                row = row0 if t < 2 else row1
                if t < 3:
                    qkv_ref[pl.ds(row, 48), pl.ds(pl.multiple_of(t * D + column, 128), HALF)] = block
                else:
                    proj_ref[pl.ds(row, 48), pl.ds(pl.multiple_of(column, 128), HALF)] = block


def finish_attn(idx, mine, peer):
    vmem = pl.BlockSpec(memory_space=pltpu.VMEM)
    return pl.pallas_call(
        finish_attn_body,
        in_specs=[pl.BlockSpec(memory_space=pltpu.SMEM), vmem, vmem],
        out_specs=[vmem, vmem],
        out_shape=[jax.ShapeDtypeStruct((D // 4, 3 * D), f32), jax.ShapeDtypeStruct((D // 4, D), f32)],
        compiler_params=params(),
        cost_estimate=pl.CostEstimate(flops=0, bytes_accessed=5_000_000, transcendentals=0),
        name="finish_attn",
    )(idx, mine, peer)


def swap(array, bit):
    count = lax.axis_size("dp")
    return lax.ppermute(array, "dp", [(i, i ^ bit) for i in range(count)])


def shift(array, step):
    count = lax.axis_size("mod")
    return lax.ppermute(array, "mod", [(i, (i + step) % count) for i in range(count)])


def take(array, index, size, axis=0):
    return lax.dynamic_slice_in_dim(array, index * size, size, axis)


def gather_half(own, spot, order):
    piece = take(own, spot, own.shape[0] // 4)
    near = jnp.stack([shift(piece, k) for k in range(1, lax.axis_size("mod"))])
    near = jnp.stack([near, swap(near, 2 * order[0])])
    far = swap(near, 2 * order[1])
    return near, far


def halve(grad, spot, bit):
    size = grad.shape[1] // 2
    side = (spot // bit) % 2
    arrived = swap(take(grad, 1 - side, size, 1), 2 * bit)
    return (take(grad, side, size, 1).astype(f32) + arrived.astype(f32)).astype(bf16)


def spread_chips(grad):
    bit = 8
    while bit < lax.axis_size("dp"):
        grad = (grad.astype(f32) + swap(grad, bit).astype(f32)).astype(bf16)
        bit *= 2
    return grad


def scatter_mod(grad, me):
    count = lax.axis_size("mod")
    total = lax.dynamic_index_in_dim(grad, me, 0, keepdims=False).astype(f32)
    for k in range(1, count):
        piece = lax.dynamic_index_in_dim(grad, (me + k) % count, 0, keepdims=False)
        total = total + shift(piece, k).astype(f32)
    return total.astype(bf16)


def gather_chips(piece):
    mine = jnp.stack([piece, swap(piece, 2), swap(piece, 4), swap(piece, 6)])
    return mine, swap(mine, 1)


def local(
    block_input,
    grad_out,
    long_flag,
    valid_mask,
    labels,
    tsteps,
    time_table,
    class_table,
    w_ada,
    b_ada,
    w_qkv,
    qv_bias,
    w_proj,
    proj_bias,
    w_fc1,
    fc1_bias,
    w_fc2,
    fc2_bias,
    rel_table,
):
    mods_n = lax.axis_size("mod")
    me = lax.axis_index("mod")
    place_dp = lax.axis_index("dp")
    core = place_dp % 2
    spot = (place_dp // 2) % 4
    idx = jnp.stack([me, spot, core]).astype(jnp.int32)
    first = 1 - core
    slots_n = MICRO * NSEG

    step_flat = tsteps.reshape(slots_n)
    label_flat = labels.reshape(slots_n)
    cond = time_table[step_flat].astype(f32) + class_table[label_flat].astype(f32)
    sigma = jax.nn.sigmoid(cond)
    act = (cond * sigma).astype(bf16)
    slope = sigma * (1.0 + cond * (1.0 - sigma))
    digits = jnp.stack([step_flat // 32, step_flat % 32, label_flat // 32, label_flat % 32], axis=1).astype(bf16)
    digits = jnp.pad(digits, ((0, 0), (0, 124)))
    rel_shape = rel_table.shape
    small = jnp.concatenate(
        [qv_bias, proj_bias, fc1_bias, fc2_bias, jnp.pad(rel_table, ((0, 0), (0, 1))).reshape(-1)]
    ).reshape(slots_n, -1)
    small_n = small.shape[1]
    packet = jnp.concatenate([act, digits, small], axis=1)
    group = jnp.stack([packet] + [shift(packet, k) for k in range(1, mods_n)])
    group_act = group[:, :, :D].reshape(mods_n * slots_n, D)
    columns = jnp.dot(group_act, w_ada, preferred_element_type=f32) + b_ada.astype(f32)
    columns = columns.reshape(mods_n, slots_n, -1)
    back = [columns[0]] + [shift(columns[k], mods_n - k) for k in range(1, mods_n)]
    turn = (mods_n - me) % mods_n
    modulation = lax.dynamic_slice_in_dim(jnp.stack(back + back), turn, mods_n, 0)
    modulation = modulation.transpose(1, 0, 2).reshape(MICRO, NSEG, 6, D)
    long_one = long_flag.reshape(MICRO)
    is_long = long_one[:, None, None, None] > 0
    seg_mod = jnp.where(is_long, modulation[:, :1], modulation)
    valid_seg = valid_mask.reshape(MICRO, NSEG, SEG)[:, :, 0]
    valid = valid_seg.astype(f32)[:, :, None, None]
    is_gate = (jnp.arange(6) % 3 == 2)[None, None, :, None]
    mods = jnp.where(is_gate, seg_mod * valid, seg_mod).reshape(slots_n, 6, D)

    rows_small = jnp.stack([group[k, :, D + 128 :] for k in range(mods_n)])
    rows_small = rows_small[::-1]
    rows_small = lax.dynamic_slice_in_dim(jnp.concatenate([rows_small, rows_small]), (mods_n - 1 - me) % mods_n, mods_n, 0)
    rows_small = rows_small.reshape(mods_n, -1).astype(f32)
    sizes = [qv_bias.shape[0], proj_bias.shape[0], fc1_bias.shape[0], fc2_bias.shape[0]]
    cuts = [0]
    for n in sizes:
        cuts.append(cuts[-1] + n)
    full_qv = rows_small[:, cuts[0] : cuts[1]].reshape(-1)
    full_proj_b = rows_small[:, cuts[1] : cuts[2]].reshape(1, -1)
    full_fc1_b = rows_small[:, cuts[2] : cuts[3]].reshape(mods_n, 2, HALF)
    full_fc2_b = rows_small[:, cuts[3] : cuts[4]].reshape(1, -1)
    full_rel = rows_small[:, cuts[4] :].reshape(H, 2 * L)
    windows = jnp.stack([full_rel[:, SEG * n : SEG * n + 2 * SEG] for n in range(7)], axis=1)
    windows = jnp.pad(windows[:, :, 254::-1], ((0, 0), (0, 1), (0, 1)))
    bias_thirds = jnp.concatenate([full_qv[:D], jnp.zeros((D,), f32), full_qv[D:]]).reshape(3, 2, HALF)

    def half_bias(which):
        return lax.dynamic_index_in_dim(bias_thirds, which, 1, keepdims=False).reshape(1, 3 * HALF)

    qkv_own = w_qkv.reshape(D // mods_n, 3, 2, HALF)
    proj_own = w_proj.reshape(D // mods_n, 2, HALF)
    fc1_own = w_fc1.reshape(D // mods_n, mods_n, 2, HALF)

    def halves(array, axis, shape):
        return tuple(
            lax.dynamic_index_in_dim(array, which, axis, keepdims=False).reshape(shape) for which in (first, core)
        )

    fetch = {}
    for name, (own, order) in dict(
        qkv=(halves(qkv_own, 2, (D // mods_n, 3 * HALF)), (1, 2)),
        proj=(halves(proj_own, 1, (D // mods_n, HALF)), (2, 1)),
        fc1=(halves(fc1_own, 2, (D // mods_n, FH)), (2, 1)),
        fc2=(halves(w_fc2.reshape(2, HALF, D), 0, (HALF, D)), (1, 2)),
        ada=(halves(w_ada.reshape(2, HALF, -1), 0, (HALF, w_ada.shape[1])), (2, 1)),
    ).items():
        near, far = gather_half(own[0], spot, order)
        fetch[name] = (
            place(idx, own[0], near, far, order),
            place(idx, own[1], swap(near, 1), swap(far, 1), order),
        )

    x = block_input.reshape(T, D)
    dy = grad_out.reshape(T, D)
    a, qkv1 = qkv_first(x, mods, fetch["qkv"][0], half_bias(first))
    qkv2 = qkv_second(a, fetch["qkv"][1], half_bias(core))
    o1, p1 = attend(qkv1, take(windows, first, H // 2), long_one, valid_seg)
    o2, p2 = attend(qkv2, take(windows, core, H // 2), long_one, valid_seg)
    half = first.reshape(1).astype(jnp.int32)
    swapped = core > 0
    proj_pair = fetch["proj"]
    proj_full = jnp.where(
        swapped,
        jnp.concatenate(proj_pair, axis=1),
        jnp.concatenate(proj_pair[::-1], axis=1),
    )
    hidden, m_in, attn, d_mlp, db_fc2 = middle(half, o1, o2, proj_full, full_proj_b, x, dy, mods)
    fc1_b = [lax.dynamic_index_in_dim(full_fc1_b, which, 1, keepdims=False).reshape(1, FH) for which in (first, core)]
    acc_o, acc_d, dw1_send, dw2_send, db1_first = mlp(m_in, d_mlp, fetch["fc1"][0], fetch["fc2"][0], fc1_b[0])
    ff, dm, dw1_keep, dw2_keep, db1_second = mlp(
        m_in, d_mlp, fetch["fc1"][1], fetch["fc2"][1], fc1_b[1], (acc_o, acc_d)
    )

    def pair_sum(keep, send):
        return (keep.astype(f32) + swap(send, 1).astype(f32)).astype(bf16)

    c1 = pair_sum(dw1_keep, dw1_send).reshape(mods_n, D // mods_n, FH)
    c2 = pair_sum(dw2_keep, dw2_send).reshape(mods_n, HALF, D)
    c1 = halve(c1, spot, 1)
    c2 = halve(c2, spot, 2)
    c1 = spread_chips(halve(c1, spot, 2))
    c2 = spread_chips(halve(c2, spot, 1))
    ff_part = scatter_mod(jnp.concatenate([c1[:, :, :D], c1[:, :, D:], c2], axis=1), me)
    grad_fc1, grad_fc2 = finish_ff(idx, *gather_chips(ff_part))

    y, d_h, do1, do2, dwp_send, dwp_keep, dmod_mid, db_proj = back_middle(
        half, hidden, dy, ff, full_fc2_b, dm, attn, mods, o1, o2, proj_full
    )
    dq1, dk1, dv1, dt1, dbq1 = attend_back(qkv1, p1, do1, o1)
    dwq_send = qkv_weight(a, dq1, dk1, dv1)
    dq2, dk2, dv2, dt2, dbq2 = attend_back(qkv2, p2, do2, o2)
    dwq_keep = qkv_weight(a, dq2, dk2, dv2)
    c3 = jnp.concatenate([pair_sum(dwq_keep, dwq_send), pair_sum(dwp_keep, dwp_send)], axis=1)
    c3 = c3.reshape(mods_n, D // mods_n, FH)
    left = spread_chips(halve(halve(c3[:, :, :D], spot, 1), spot, 2))
    right = spread_chips(halve(halve(c3[:, :, D:], spot, 2), spot, 1))
    attn_part = scatter_mod(jnp.concatenate([left, right], axis=1), me)
    grad_qkv, grad_proj = finish_attn(idx, *gather_chips(attn_part))

    dx, dmod_entry = back_entry(
        (dq1, dk1, dv1, dq2, dk2, dv2), fetch["qkv"][0], fetch["qkv"][1], x, d_h, mods
    )

    d_seg = jnp.concatenate([dmod_entry, dmod_mid[:, 2:, :]], axis=1).reshape(MICRO, NSEG, 6, D)
    d_seg = jnp.where(is_gate, d_seg * valid, d_seg)
    whole = jnp.sum(d_seg, axis=1, keepdims=True)
    lead = (jnp.arange(NSEG) == 0)[None, :, None, None]
    d_mod = jnp.where(is_long, jnp.where(lead, whole, 0.0), d_seg).reshape(slots_n, mods_n, -1).astype(bf16)
    ada_pair = fetch["ada"]
    width = w_ada.shape[1]

    def ada_half(which):
        weight = ada_pair[which].reshape(mods_n, HALF, width)
        return jnp.einsum("smc,mrc->sr", d_mod, weight, preferred_element_type=f32)

    one, two = ada_half(0), ada_half(1)
    d_act = jnp.where(swapped, jnp.concatenate([one, two], axis=1), jnp.concatenate([two, one], axis=1))
    d_cond = (d_act * slope).astype(bf16)

    def both(one_half, two_half, axis):
        pair = jnp.stack([one_half, two_half], axis=axis)
        return jnp.where(swapped, pair, jnp.flip(pair, axis))

    g_qv = both(
        jnp.stack([dbq1[0], dbq1[1]]), jnp.stack([dbq2[0], dbq2[1]]), 1
    ).reshape(mods_n, -1)
    g_fc1 = both(db1_first[0].reshape(mods_n, HALF), db1_second[0].reshape(mods_n, HALF), 1).reshape(mods_n, -1)
    dt = both(dt1, dt2, 0).reshape(H, 8, 2 * SEG)[:, :7, 254::-1]
    g_rel = sum(
        jnp.pad(dt[:, n], ((0, 0), (SEG * n, 2 * L - 255 - SEG * n))) for n in range(7)
    )
    g_small = jnp.concatenate(
        [g_qv, db_proj[0].reshape(mods_n, -1), g_fc1, db_fc2[0].reshape(mods_n, -1), g_rel.reshape(mods_n, -1)],
        axis=1,
    ).astype(bf16).reshape(mods_n, slots_n, small_n)

    def outgoing(k):
        target = (me + k) % mods_n
        return jnp.concatenate(
            [
                lax.dynamic_index_in_dim(d_mod, target, 1, keepdims=False),
                d_cond,
                lax.dynamic_index_in_dim(g_small, target, 0, keepdims=False),
            ],
            axis=1,
        )

    arrived = jnp.stack([outgoing(0)] + [shift(outgoing(k), k) for k in range(1, mods_n)])
    small_sum = jnp.sum(arrived[:, :, width + D :].astype(f32), axis=0).astype(bf16)
    body = jnp.concatenate([arrived[:, :, : width + D], group[:, :, : D + 128]], axis=2).reshape(mods_n * slots_n, -1)
    small_sum = jnp.pad(small_sum, ((0, 0), (0, body.shape[1] - small_n)))
    everyone = lax.all_gather(jnp.concatenate([body, small_sum]), "dp", axis=0, tiled=False)
    small_all = jnp.sum(everyone[:, mods_n * slots_n :, :small_n].astype(f32), axis=0).reshape(-1)
    everyone = everyone[:, : mods_n * slots_n].reshape(-1, body.shape[1])
    d_mod_all = everyone[:, :width]
    d_cond_all = everyone[:, width : width + D]
    act_all = everyone[:, width + D : width + 2 * D]
    digits_all = everyone[:, width + 2 * D : width + 2 * D + 4].astype(jnp.int32)
    grad_ada = lax.dot_general(act_all, d_mod_all, (((0,), (0,)), ((), ())), preferred_element_type=f32)
    grad_ada_b = jnp.sum(d_mod_all.astype(f32), axis=0)

    def table_grad(high, low, rows):
        share = rows // mods_n
        index = digits_all[:, high] * 32 + digits_all[:, low]
        hot = (index[None, :] == me * share + jnp.arange(share)[:, None]).astype(bf16)
        return jnp.dot(hot, d_cond_all, preferred_element_type=f32)

    grad_time = table_grad(0, 1, time_table.shape[0])
    grad_class = table_grad(2, 3, class_table.shape[0])
    return (
        y.reshape(block_input.shape),
        dx.reshape(block_input.shape),
        grad_time,
        grad_class,
        grad_ada,
        grad_ada_b,
        grad_qkv,
        small_all[cuts[0] : cuts[1]],
        grad_proj,
        small_all[cuts[1] : cuts[2]],
        grad_fc1,
        small_all[cuts[2] : cuts[3]],
        grad_fc2,
        small_all[cuts[3] : cuts[4]],
        small_all[cuts[4] :].reshape(rel_shape[0], 2 * L)[:, : rel_shape[1]],
    )


def solution(mesh):
    in_specs = (
        P(None, ("dp", "mod"), None),
        P(None, ("dp", "mod"), None),
        P(None, ("dp", "mod")),
        P(None, ("dp", "mod")),
        P(None, ("dp", "mod")),
        P(None, ("dp", "mod")),
        P(),
        P(),
        P(None, "mod"),
        P("mod"),
        P("mod", None),
        P("mod"),
        P("mod", None),
        P("mod"),
        P("mod", None),
        P("mod"),
        P("mod", None),
        P("mod"),
        P("mod", None),
    )
    out_specs = (
        P(None, ("dp", "mod"), None),
        P(None, ("dp", "mod"), None),
        P("mod", None),
        P("mod", None),
        P(None, "mod"),
        P("mod"),
        P("mod", None),
        P("mod"),
        P("mod", None),
        P("mod"),
        P("mod", None),
        P("mod"),
        P("mod", None),
        P("mod"),
        P("mod", None),
    )
    return jax.shard_map(local, mesh=mesh, in_specs=in_specs, out_specs=out_specs, check_vma=False)
```

time: 1610 us -> 588 us (0.37)
  the two profiles are of different devices: /device:TPU:0 before, /device:TPU:9 now
where the time goes in v1:
time: 588 us; the launch traced here: 578 us
  Pallas kernels  186 us (32%)
  waiting for transfers between devices  149 us (25%)
  local copies, waits for them, and re-layouts  107 us (18%)
  starting transfers between devices  82.1 us (14%)
  other arithmetic  29.1 us (5%)
  between operations  16.1 us (3%)
  matrix products  8.85 us (2%)
    ppermute x40, waiting for transfers between devices, swap(): return lax.ppermute(array, 'dp', [(i, i ^ bit) for i in range(count)])  94.6 us
    ppermute x30, waiting for transfers between devices, shift(): lax.ppermute(array, 'mod', [(i, (i + step) % count) for i in range(count)])  54 us
    ppermute x40, starting transfers between devices, swap(): return lax.ppermute(array, 'dp', [(i, i ^ bit) for i in range(count)])  52.9 us
    pallas_call x2, Pallas kernels, mlp(): pl.pallas_call(partial(mlp_body, acc is not None), grid=(FH // FB,), in_s...  46.2 us
    unnamed x140, local copies, waits for them, and re-layouts  34.7 us
    ppermute x30, starting transfers between devices, shift(): lax.ppermute(array, 'mod', [(i, (i + step) % count) for i in range(count)])  29.2 us
    pallas_call x2, Pallas kernels, attend(): pl.pallas_call(attend_body, grid_spec=pltpu.PrefetchScalarGridSpec(num_sc...  26.9 us
    pallas_call x2, Pallas kernels, attend_back(): pl.pallas_call(attend_back_body, grid=(3, MICRO), in_specs=[part, pl.Bloc...  26.9 us
  transfers between devices with their start and end apart: 71, of which 25 were waited for; matrix products, arithmetic and copies ran while one was open for 21% of the time, Pallas kernels for 31%

profile of v1, /device:TPU:9, one launch (start us, length us, event | category | flops | bytes accessed | tf_op | source)
XLA Modules:
  0.0 577.7 jit_solution(16359728502413518722)
XLA Ops:
  10.8 8.2 %dynamic-slice_reduce_fusion = (bf16[192,4,384]{2,1,0:T(4,128)(2,1)S(1)}, bf16[192,4,384]{2,1,0:T(4,128)(2,1)}) fusion(bf16[192,4,2,384]{3,2,1,0:T(2,128)(2,1)S(1)} %reshape.550, s32[]{:T(128)S(6)} %select_n.359, s32[]{:T(128)S(6)} %select_n.364), kind=kLoop, calls=%fused_computation.19 | loop fusion | bytes 2359304 | tf_op jit(solution)/shard_map/jit(dynamic_index_in_dim)/dynamic_slice | solution.py:758
  39.2 6.3 %dynamic-slice_reduce_fusion.2 = (bf16[192,3,384]{2,1,0:T(4,128)(2,1)}, bf16[192,3,384]{2,1,0:T(4,128)(2,1)S(1)}) fusion(bf16[192,3,2,384]{3,2,1,0:T(2,128)(2,1)S(1)} %reshape.541, s32[]{:T(128)S(6)} %select_n.364, s32[]{:T(128)S(6)} %select_n.359), kind=kLoop, calls=%fused_computation.27 | loop fusion | bytes 1769480 | tf_op jit(solution)/shard_map/jit(dynamic_index_in_dim)/dynamic_slice | solution.py:758
  67.8 6.3 %collective-permute-done.3 = f32[8,1152]{1,0:T(8,128)S(1)} collective-permute-done((f32[8,1152]{1,0:T(8,128)S(1)}, f32[8,1152]{1,0:T(8,128)S(1)}, u32[]{:S(2)}, u32[]{:S(2)}) %collective-permute-start.3) | collective-permute-done | bytes 36896 | tf_op jit(solution)/shard_map/ppermute | solution.py:628
  100.5 7.4 %collective-permute-done.29 = bf16[96,768]{1,0:T(8,128)(2,1)S(1)} collective-permute-done((bf16[96,768]{1,0:T(8,128)(2,1)S(1)}, bf16[96,768]{1,0:T(8,128)(2,1)S(1)}, u32[]{:S(2)}, u32[]{:S(2)}) %collective-permute-start.29) | collective-permute-done | bytes 147488 | tf_op jit(solution)/shard_map/ppermute | solution.py:628
  109.2 7.5 %collective-permute-done.34 = bf16[96,1152]{1,0:T(8,128)(2,1)S(1)} collective-permute-done((bf16[96,1152]{1,0:T(8,128)(2,1)S(1)}, bf16[96,1152]{1,0:T(8,128)(2,1)S(1)}, u32[]{:S(2)}, u32[]{:S(2)}) %collective-permute-start.34) | collective-permute-done | bytes 221216 | tf_op jit(solution)/shard_map/ppermute | solution.py:628
  133.1 6.2 %collective-permute-start.11 = (bf16[2,3,48,1152]{3,2,1,0:T(8,128)(2,1)S(1)}, bf16[2,3,48,1152]{3,2,1,0:T(8,128)(2,1)S(1)}, u32[]{:S(2)}, u32[]{:S(2)}) collective-permute-start(bf16[2,3,48,1152]{3,2,1,0:T(8,128)(2,1)S(1)} %pad_maximum_fusion.6.near_ref), channel_id=1, source_target_pairs={{0,4},{4,0},{8,12},{12,8},{16,20},{20,16},{24,28},{28,24},{1,5},{5... | collective-permute-start | bytes 1990664 | tf_op jit(solution)/shard_map/ppermute | solution.py:623
  147.6 11.8 %collective-permute-done.10.far_ref = bf16[2,3,48,1152]{3,2,1,0:T(8,128)(2,1)S(1)} collective-permute-done((bf16[2,3,48,1152]{3,2,1,0:T(8,128)(2,1)S(1)}, bf16[2,3,48,1152]{3,2,1,0:T(8,128)(2,1)S(1)}, u32[]{:S(2)}, u32[]{:S(2)}) %collective-permute-start.10) | collective-permute-done | bytes 663584 | tf_op jit(solution)/shard_map/ppermute | solution.py:623
  163.3 5.9 %qkv_first.1 = (bf16[1024,768]{1,0:T(8,128)(2,1)}, bf16[1024,1152]{1,0:T(8,128)(2,1)}) custom-call(bf16[1024,768]{1,0:T(8,128)(2,1)} %bitcast.329, f32[8,6,768]{2,1,0:T(8,128)} %multiply_select_fusion.1.mod_ref, bf16[768,1152]{1,0:T(8,128)(2,1)} %copy-done.10, f32[1,1152]{1,0:T(1,128)} %bitcast.324), custom_call_target="tpu_custom_call" | custom-call | flops 1811939328 | bytes 8000000 | tf_op jit(solution)/shard_map/qkv_first/pallas_call | solution.py:56
  175.0 13.5 %attend.2 = (bf16[1024,384]{1,0:T(8,128)(2,1)}, bf16[2,6,512,512]{3,2,1,0:T(8,128)(2,1)}) custom-call(s32[2]{0:T(128)} %bitcast.332, s32[2,4]{1,0:T(2,128)} %bitcast.325, bf16[1024,1152]{1,0:T(8,128)(2,1)} %get-tuple-element.60.q_ref.k_ref.v_ref, bf16[1024,1152]{1,0:T(8,128)(2,1)} %get-tuple-element.60.q_ref.k_ref.v_ref, ...), custom_call_target="tpu_custom_call" | custom-call | flops 16000000000 | bytes 10000000 | tf_op jit(solution)/shard_map/attend/pallas_call | solution.py:138
  205.9 13.4 %attend.3 = (bf16[1024,384]{1,0:T(8,128)(2,1)}, bf16[2,6,512,512]{3,2,1,0:T(8,128)(2,1)}) custom-call(s32[2]{0:T(128)} %bitcast.333, s32[2,4]{1,0:T(2,128)} %bitcast.326, bf16[1024,1152]{1,0:T(8,128)(2,1)} %qkv_second.1.q_ref.k_ref.v_ref, bf16[1024,1152]{1,0:T(8,128)(2,1)} %qkv_second.1.q_ref.k_ref.v_ref, bf16[1024,1152]{1,0:T(8,128)(2,1)} %qkv_second.1.q_ref.k_ref.v_ref, ...), custom_call_target="tpu_custom_call" | custom-call | flops 16000000000 | bytes 10000000 | tf_op jit(solution)/shard_map/attend/pallas_call | solution.py:138
  219.3 7.5 %middle.1 = (f32[1024,768]{1,0:T(8,128)}, bf16[1024,768]{1,0:T(8,128)(2,1)}, bf16[1024,768]{1,0:T(8,128)(2,1)}, bf16[1024,768]{1,0:T(8,128)(2,1)}, f32[8,768]{1,0:T(8,128)}) custom-call(s32[1]{0:T(128)} %bitcast.half_ref, bf16[1024,384]{1,0:T(8,128)(2,1)} %get-tuple-element.61.o1_ref.o_ref, bf16[1024,384]{1,0:T(8,128)(2,1)} %get-tuple-element.63.o2_ref.o_ref, ...), custom_call_target="tpu_custom_call" | custom-call | flops 2415919104 | bytes 16000000 | tf_op jit(solution)/shard_map/middle/pallas_call | solution.py:193
  226.9 22.4 %mlp.2 = (f32[1024,768]{1,0:T(8,128)}, f32[1024,768]{1,0:T(8,128)}, bf16[768,1536]{1,0:T(8,128)(2,1)}, bf16[1536,768]{1,0:T(8,128)(2,1)}, f32[8,1536]{1,0:T(8,128)}) custom-call(bf16[1024,768]{1,0:T(8,128)(2,1)} %get-tuple-element.65.m_ref, bf16[1024,768]{1,0:T(8,128)(2,1)} %get-tuple-element.66.dmlp_ref, bf16[768,1536]{1,0:T(8,128)(2,1)} %copy-done.6, ...), custom_call_target="tpu_custom_call" | custom-call | flops 14495514624 | bytes 24000000 | tf_op jit(solution)/shard_map/mlp/pallas_call | solution.py:291
  264.5 23.8 %mlp.3 = (f32[1024,768]{1,0:T(8,128)}, f32[1024,768]{1,0:T(8,128)}, bf16[768,1536]{1,0:T(8,128)(2,1)}, bf16[1536,768]{1,0:T(8,128)(2,1)}, f32[8,1536]{1,0:T(8,128)}) custom-call(bf16[1024,768]{1,0:T(8,128)(2,1)} %get-tuple-element.65.m_ref, bf16[1024,768]{1,0:T(8,128)(2,1)} %get-tuple-element.66.dmlp_ref, bf16[768,1536]{1,0:T(8,128)(2,1)} %copy-done.8, ...), custom_call_target="tpu_custom_call" | custom-call | flops 14495514624 | bytes 24000000 | tf_op jit(solution)/shard_map/mlp/pallas_call | solution.py:291
  288.3 13.6 %back_middle.1 = (bf16[1024,768]{1,0:T(8,128)(2,1)}, f32[1024,768]{1,0:T(8,128)}, bf16[1024,384]{1,0:T(8,128)(2,1)}, bf16[1024,384]{1,0:T(8,128)(2,1)}, bf16[768...) custom-call(s32[1]{0:T(128)} %bitcast.half_ref, ...), custom_call_target="tpu_custom_call" | custom-call | flops 4831838208 | bytes 24000000 | tf_op jit(solution)/shard_map/back_middle/pallas_call | solution.py:365
  302.3 13.3 %attend_back.3 = (bf16[1024,384]{1,0:T(8,128)(2,1)}, bf16[1024,384]{1,0:T(8,128)(2,1)}, bf16[1024,384]{1,0:T(8,128)(2,1)}, f32[6,8,256]{2,1,0:T(8,128)}, f32[8,384]{1,0:T(8,128)}) custom-call(bf16[1024,1152]{1,0:T(8,128)(2,1)} %qkv_second.1.q_ref.k_ref.v_ref, bf16[1024,1152]{1,0:T(8,128)(2,1)} %qkv_second.1.q_ref.k_ref.v_ref, ...), custom_call_target="tpu_custom_call" | custom-call | flops 24000000000 | bytes 12000000 | tf_op jit(solution)/shard_map/attend_back/pallas_call | solution.py:448
  315.7 13.5 %attend_back.2 = (bf16[1024,384]{1,0:T(8,128)(2,1)}, bf16[1024,384]{1,0:T(8,128)(2,1)}, bf16[1024,384]{1,0:T(8,128)(2,1)}, f32[6,8,256]{2,1,0:T(8,128)}, f32[8,384]{1,0:T(8,128)}) custom-call(bf16[1024,1152]{1,0:T(8,128)(2,1)} %get-tuple-element.60.q_ref.k_ref.v_ref, bf16[1024,1152]{1,0:T(8,128)(2,1)} %get-tuple-element.60.q_ref.k_ref.v_ref, ...), custom_call_target="tpu_custom_call" | custom-call | flops 24000000000 | bytes 12000000 | tf_op jit(solution)/shard_map/attend_back/pallas_call | solution.py:448
  375.5 12.1 %back_entry.1 = (bf16[1024,768]{1,0:T(8,128)(2,1)}, f32[8,2,768]{2,1,0:T(2,128)}) custom-call(bf16[1024,384]{1,0:T(8,128)(2,1)} %get-tuple-element.75.dq1.dq_ref, bf16[1024,384]{1,0:T(8,128)(2,1)} %get-tuple-element.76.dk1.dk_ref, bf16[1024,384]{1,0:T(8,128)(2,1)} %get-tuple-element.77.dv1.dv_ref, bf16[1024,384]{1,0:T(8,128)(2,1)} %get-tuple-element.80.dq2.dq_ref, ...), custom_call_target="tpu_custom_call" | custom-call | flops 3623878656 | bytes 16000000 | tf_op jit(solution)/shard_map/back_entry/pallas_call | solution.py:510
  395.4 6.0 %qkv_weight.3 = bf16[768,1152]{1,0:T(8,128)(2,1)} custom-call(bf16[1024,768]{1,0:T(8,128)(2,1)} %get-tuple-element.62.a_ref, bf16[1024,384]{1,0:T(8,128)(2,1)} %get-tuple-element.75.dq1.dq_ref, bf16[1024,384]{1,0:T(8,128)(2,1)} %get-tuple-element.76.dk1.dk_ref, bf16[1024,384]{1,0:T(8,128)(2,1)} %get-tuple-element.77.dv1.dv_ref), custom_call_target="tpu_custom_call" | custom-call | flops 1811939328 | bytes 6000000 | tf_op jit(solution)/shard_map/qkv_weight/pallas_call | solution.py:478
  424.1 14.5 %collective-permute-done.48 = bf16[4,96,768]{2,1,0:T(8,128)(2,1)S(1)} collective-permute-done((bf16[4,96,768]{2,1,0:T(8,128)(2,1)S(1)}, bf16[4,96,768]{2,1,0:T(8,128)(2,1)S(1)}, u32[]{:S(2)}, u32[]{:S(2)}) %collective-permute-start.48) | collective-permute-done | bytes 589856 | tf_op jit(solution)/shard_map/ppermute | solution.py:623
  438.8 24.6 %collective-permute-done.46 = bf16[4,96,768]{2,1,0:T(8,128)(2,1)S(1)} collective-permute-done((bf16[4,96,768]{2,1,0:T(8,128)(2,1)S(1)}, bf16[4,96,768]{2,1,0:T(8,128)(2,1)S(1)}, u32[]{:S(2)}, u32[]{:S(2)}) %collective-permute-start.46) | collective-permute-done | bytes 589856 | tf_op jit(solution)/shard_map/ppermute | solution.py:623
  482.2 16.3 %collective-permute-done.61 = bf16[4,192,768]{2,1,0:T(8,128)(2,1)S(1)} collective-permute-done((bf16[4,192,768]{2,1,0:T(8,128)(2,1)S(1)}, bf16[4,192,768]{2,1,0:T(8,128)(2,1)S(1)}, u32[]{:S(2)}, u32[]{:S(2)}) %collective-permute-start.61) | collective-permute-done | bytes 1179680 | tf_op jit(solution)/shard_map/ppermute | solution.py:623
  499.1 12.0 %collective-permute-done.59 = bf16[4,48,1536]{2,1,0:T(8,128)(2,1)S(1)} collective-permute-done((bf16[4,48,1536]{2,1,0:T(8,128)(2,1)S(1)}, bf16[4,48,1536]{2,1,0:T(8,128)(2,1)S(1)}, u32[]{:S(2)}, u32[]{:S(2)}) %collective-permute-start.59) | collective-permute-done | bytes 589856 | tf_op jit(solution)/shard_map/ppermute | solution.py:623
  519.3 13.6 %collective-permute-done.64 = bf16[192,768]{1,0:T(8,128)(2,1)S(1)} collective-permute-done((bf16[192,768]{1,0:T(8,128)(2,1)S(1)}, bf16[192,768]{1,0:T(8,128)(2,1)S(1)}, u32[]{:S(2)}, u32[]{:S(2)}) %collective-permute-start.64) | collective-permute-done | bytes 294944 | tf_op jit(solution)/shard_map/ppermute | solution.py:628
  544.6 7.3 %collective-permute-done.68 = bf16[192,768]{1,0:T(8,128)(2,1)S(1)} collective-permute-done((bf16[192,768]{1,0:T(8,128)(2,1)S(1)}, bf16[192,768]{1,0:T(8,128)(2,1)S(1)}, u32[]{:S(2)}, u32[]{:S(2)}) %collective-permute-start.68) | collective-permute-done | bytes 294944 | tf_op jit(solution)/shard_map/ppermute | solution.py:623
  (468 shorter events, 274.7 us)
Async XLA Ops:
  7.2 548.3 %all-gather.3.cloned.1.call-start = ((), (), s32[]{:S(2)}) async-start(), calls=%async_computation | async-start | bytes 2027520 | tf_op jit(solution)/shard_map/all_gather | solution.py:874
  19.8 71.5 %collective-permute-start.20 = (bf16[48,1536]{1,0:T(8,128)(2,1)}, bf16[48,1536]{1,0:T(8,128)(2,1)}, u32[]{:S(2)}, u32[]{:S(2)}) collective-permute-start(bf16[48,1536]{1,0:T(8,128)(2,1)} %constant_dynamic-slice_fusion.18), channel_id=1, source_target_pairs={{0,1},{1,2},{2,3},{3,0},{4,5},{5,6},{6,7},{7,4},{8,9},{9,10},{10,1... | collective-permute-start | bytes 442376 | tf_op jit(solution)/shard_map/ppermute | solution.py:628
  21.1 70.3 %collective-permute-start.21 = (bf16[48,1536]{1,0:T(8,128)(2,1)}, bf16[48,1536]{1,0:T(8,128)(2,1)}, u32[]{:S(2)}, u32[]{:S(2)}) collective-permute-start(bf16[48,1536]{1,0:T(8,128)(2,1)} %constant_dynamic-slice_fusion.18), channel_id=1, source_target_pairs={{0,2},{1,3},{2,0},{3,1},{4,6},{5,7},{6,4},{7,5},{8,10},{9,11},{10,... | collective-permute-start | bytes 442376 | tf_op jit(solution)/shard_map/ppermute | solution.py:628
  133.1 62.9 %collective-permute-start.11 = (bf16[2,3,48,1152]{3,2,1,0:T(8,128)(2,1)S(1)}, bf16[2,3,48,1152]{3,2,1,0:T(8,128)(2,1)S(1)}, u32[]{:S(2)}, u32[]{:S(2)}) collective-permute-start(bf16[2,3,48,1152]{3,2,1,0:T(8,128)(2,1)S(1)} %pad_maximum_fusion.6.near_ref), channel_id=1, source_target_pairs={{0,4},{4,0},{8,12},{12,8},{16,20},{20,16},{24,28},{28,24},{1,5},{5... | collective-permute-start | bytes 1990664 | tf_op jit(solution)/shard_map/ppermute | solution.py:623
  139.3 49.2 %collective-permute-start.25 = (bf16[2,3,48,1536]{3,2,1,0:T(8,128)(2,1)}, bf16[2,3,48,1536]{3,2,1,0:T(8,128)(2,1)}, u32[]{:S(2)}, u32[]{:S(2)}) collective-permute-start(bf16[2,3,48,1536]{3,2,1,0:T(8,128)(2,1)} %pad_maximum_fusion.4.near_ref), channel_id=1, source_target_pairs={{0,8},{4,12},{8,0},{12,4},{16,24},{20,28},{24,16},{28,20},{1,9},{5... | collective-permute-start | bytes 2654216 | tf_op jit(solution)/shard_map/ppermute | solution.py:623
  142.0 114.4 %collective-permute-start.24 = (bf16[2,3,48,1536]{3,2,1,0:T(8,128)(2,1)}, bf16[2,3,48,1536]{3,2,1,0:T(8,128)(2,1)}, u32[]{:S(2)}, u32[]{:S(2)}) collective-permute-start(bf16[2,3,48,1536]{3,2,1,0:T(8,128)(2,1)} %pad_maximum_fusion.4.near_ref), channel_id=1, source_target_pairs={{0,4},{4,0},{8,12},{12,8},{16,20},{20,16},{24,28},{28,24},{1,5},{5... | collective-permute-start | bytes 2654216 | tf_op jit(solution)/shard_map/ppermute | solution.py:623
  145.2 45.7 %collective-permute-start.32 = (bf16[2,3,96,768]{3,2,1,0:T(8,128)(2,1)}, bf16[2,3,96,768]{3,2,1,0:T(8,128)(2,1)}, u32[]{:S(2)}, u32[]{:S(2)}) collective-permute-start(bf16[2,3,96,768]{3,2,1,0:T(8,128)(2,1)} %pad_maximum_fusion.5.near_ref), channel_id=1, source_target_pairs={{0,16},{4,20},{8,24},{12,28},{16,0},{20,4},{24,8},{28,12},{1,17},{... | collective-permute-start | bytes 2654216 | tf_op jit(solution)/shard_map/ppermute | solution.py:623
  188.5 72.2 %collective-permute-start.31 = (bf16[2,3,96,768]{3,2,1,0:T(8,128)(2,1)}, bf16[2,3,96,768]{3,2,1,0:T(8,128)(2,1)}, u32[]{:S(2)}, u32[]{:S(2)}) collective-permute-start(bf16[2,3,96,768]{3,2,1,0:T(8,128)(2,1)} %pad_maximum_fusion.5.near_ref), channel_id=1, source_target_pairs={{0,4},{4,0},{8,12},{12,8},{16,20},{20,16},{24,28},{28,24},{1,5},{5... | collective-permute-start | bytes 2654216 | tf_op jit(solution)/shard_map/ppermute | solution.py:623
  190.9 61.2 %collective-permute-start.38 = (bf16[2,3,96,1152]{3,2,1,0:T(8,128)(2,1)}, bf16[2,3,96,1152]{3,2,1,0:T(8,128)(2,1)}, u32[]{:S(2)}, u32[]{:S(2)}) collective-permute-start(bf16[2,3,96,1152]{3,2,1,0:T(8,128)(2,1)} %pad_maximum_fusion.1.near_ref), channel_id=1, source_target_pairs={{0,8},{4,12},{8,0},{12,4},{16,24},{20,28},{24,16},{28,20},{1,9},{5... | collective-permute-start | bytes 3981320 | tf_op jit(solution)/shard_map/ppermute | solution.py:623
  196.0 60.6 %collective-permute-start.26 = (bf16[2,3,48,1536]{3,2,1,0:T(8,128)(2,1)}, bf16[2,3,48,1536]{3,2,1,0:T(8,128)(2,1)}, u32[]{:S(2)}, u32[]{:S(2)}) collective-permute-start(bf16[2,3,48,1536]{3,2,1,0:T(8,128)(2,1)} %collective-permute-done.25.far_ref), channel_id=1, source_target_pairs={{0,4},{4,0},{8,12},{12,8},{16,20},{20,16},{24,28},{28,24},{1,5},{5... | collective-permute-start | bytes 2654216 | tf_op jit(solution)/shard_map/ppermute | solution.py:623
  196.8 64.1 %collective-permute-start.33 = (bf16[2,3,96,768]{3,2,1,0:T(8,128)(2,1)}, bf16[2,3,96,768]{3,2,1,0:T(8,128)(2,1)}, u32[]{:S(2)}, u32[]{:S(2)}) collective-permute-start(bf16[2,3,96,768]{3,2,1,0:T(8,128)(2,1)} %collective-permute-done.32.far_ref), channel_id=1, source_target_pairs={{0,4},{4,0},{8,12},{12,8},{16,20},{20,16},{24,28},{28,24},{1,5},{5... | collective-permute-start | bytes 2654216 | tf_op jit(solution)/shard_map/ppermute | solution.py:623
  252.1 149.3 %collective-permute-start.39 = (bf16[2,3,96,1152]{3,2,1,0:T(8,128)(2,1)}, bf16[2,3,96,1152]{3,2,1,0:T(8,128)(2,1)}, u32[]{:S(2)}, u32[]{:S(2)}) collective-permute-start(bf16[2,3,96,1152]{3,2,1,0:T(8,128)(2,1)} %pad_maximum_fusion.1.near_ref), channel_id=1, source_target_pairs={{0,4},{4,0},{8,12},{12,8},{16,20},{20,16},{24,28},{28,24},{1,5},{5... | collective-permute-start | bytes 3981320 | tf_op jit(solution)/shard_map/ppermute | solution.py:623
  256.4 157.6 %collective-permute-start.57 = (bf16[768,1536]{1,0:T(8,128)(2,1)}, bf16[768,1536]{1,0:T(8,128)(2,1)}, u32[]{:S(2)}, u32[]{:S(2)}) collective-permute-start(bf16[768,1536]{1,0:T(8,128)(2,1)} %get-tuple-element.100), channel_id=1, source_target_pairs={{0,4},{4,0},{8,12},{12,8},{16,20},{20,16},{24,28},{28,24},{1,5},{5... | collective-permute-start | bytes 7077896 | tf_op jit(solution)/shard_map/ppermute | solution.py:623
  256.5 165.2 %collective-permute-start.60 = (bf16[1536,768]{1,0:T(8,128)(2,1)}, bf16[1536,768]{1,0:T(8,128)(2,1)}, u32[]{:S(2)}, u32[]{:S(2)}) collective-permute-start(bf16[1536,768]{1,0:T(8,128)(2,1)} %get-tuple-element.102), channel_id=1, source_target_pairs={{0,4},{4,0},{8,12},{12,8},{16,20},{20,16},{24,28},{28,24},{1,5},{5... | collective-permute-start | bytes 7077896 | tf_op jit(solution)/shard_map/ppermute | solution.py:623
  260.7 140.7 %collective-permute-start.40 = (bf16[2,3,96,1152]{3,2,1,0:T(8,128)(2,1)}, bf16[2,3,96,1152]{3,2,1,0:T(8,128)(2,1)}, u32[]{:S(2)}, u32[]{:S(2)}) collective-permute-start(bf16[2,3,96,1152]{3,2,1,0:T(8,128)(2,1)} %collective-permute-done.38.far_ref), channel_id=1, source_target_pairs={{0,4},{4,0},{8,12},{12,8},{16,20},{20,16},{24,28},{28,24},{1,5},{5... | collective-permute-start | bytes 3981320 | tf_op jit(solution)/shard_map/ppermute | solution.py:623
  301.9 106.7 %collective-permute-start.45 = (bf16[768,384]{1,0:T(8,128)(2,1)}, bf16[768,384]{1,0:T(8,128)(2,1)}, u32[]{:S(2)}, u32[]{:S(2)}) collective-permute-start(bf16[768,384]{1,0:T(8,128)(2,1)} %get-tuple-element.96), channel_id=1, source_target_pairs={{0,4},{4,0},{8,12},{12,8},{16,20},{20,16},{24,28},{28,24},{1,5},{5... | collective-permute-start | bytes 1769480 | tf_op jit(solution)/shard_map/ppermute | solution.py:623
  416.4 55.4 %collective-permute-start.58 = (bf16[4,96,1536]{2,1,0:T(8,128)(2,1)S(1)}, bf16[4,96,1536]{2,1,0:T(8,128)(2,1)S(1)}, u32[]{:S(2)}, u32[]{:S(2)}) collective-permute-start(bf16[4,96,1536]{2,1,0:T(8,128)(2,1)S(1)} %constant_dynamic-slice_fusion.3), channel_id=1, source_target_pairs={{0,8},{4,12},{8,0},{12,4},{16,24},{20,28},{24,16},{28,20},{1,9},{5... | collective-permute-start | bytes 3538952 | tf_op jit(solution)/shard_map/ppermute | solution.py:623
  421.4 42.0 %collective-permute-start.46 = (bf16[4,96,768]{2,1,0:T(8,128)(2,1)S(1)}, bf16[4,96,768]{2,1,0:T(8,128)(2,1)S(1)}, u32[]{:S(2)}, u32[]{:S(2)}) collective-permute-start(bf16[4,96,768]{2,1,0:T(8,128)(2,1)S(1)} %constant_dynamic-slice_fusion.7), channel_id=1, source_target_pairs={{0,8},{4,12},{8,0},{12,4},{16,24},{20,28},{24,16},{28,20},{1,9},{5... | collective-permute-start | bytes 1769480 | tf_op jit(solution)/shard_map/ppermute | solution.py:623
  438.8 31.0 %collective-permute-start.49 = (bf16[4,48,768]{2,1,0:T(8,128)(2,1)S(1)}, bf16[4,48,768]{2,1,0:T(8,128)(2,1)S(1)}, u32[]{:S(2)}, u32[]{:S(2)}) collective-permute-start(bf16[4,48,768]{2,1,0:T(8,128)(2,1)S(1)} %constant_dynamic-slice_fusion.4), channel_id=1, source_target_pairs={{0,8},{4,12},{8,0},{12,4},{16,24},{20,28},{24,16},{28,20},{1,9},{5... | collective-permute-start | bytes 884744 | tf_op jit(solution)/shard_map/ppermute | solution.py:623
  465.0 33.5 %collective-permute-start.61 = (bf16[4,192,768]{2,1,0:T(8,128)(2,1)S(1)}, bf16[4,192,768]{2,1,0:T(8,128)(2,1)S(1)}, u32[]{:S(2)}, u32[]{:S(2)}) collective-permute-start(bf16[4,192,768]{2,1,0:T(8,128)(2,1)S(1)} %constant_dynamic-slice_fusion.1), channel_id=1, source_target_pairs={{0,16},{4,20},{8,24},{12,28},{16,0},{20,4},{24,8},{28,12},{1,17},{... | collective-permute-start | bytes 3538952 | tf_op jit(solution)/shard_map/ppermute | solution.py:623
  472.2 38.9 %collective-permute-start.59 = (bf16[4,48,1536]{2,1,0:T(8,128)(2,1)S(1)}, bf16[4,48,1536]{2,1,0:T(8,128)(2,1)S(1)}, u32[]{:S(2)}, u32[]{:S(2)}) collective-permute-start(bf16[4,48,1536]{2,1,0:T(8,128)(2,1)S(1)} %constant_dynamic-slice_fusion.2), channel_id=1, source_target_pairs={{0,16},{4,20},{8,24},{12,28},{16,0},{20,4},{24,8},{28,12},{1,17},{... | collective-permute-start | bytes 1769480 | tf_op jit(solution)/shard_map/ppermute | solution.py:623
  479.5 32.4 %collective-permute-start.53 = (bf16[96,768]{1,0:T(8,128)(2,1)S(1)}, bf16[96,768]{1,0:T(8,128)(2,1)S(1)}, u32[]{:S(2)}, u32[]{:S(2)}) collective-permute-start(bf16[96,768]{1,0:T(8,128)(2,1)S(1)} %fusion.13), channel_id=1, source_target_pairs={{0,8},{4,12},{8,0},{12,4},{16,24},{20,28},{24,16},{28,20},{1,9},{5... | collective-permute-start | bytes 442376 | tf_op jit(solution)/shard_map/ppermute | solution.py:623
  479.8 34.5 %collective-permute-start.54 = (bf16[96,768]{1,0:T(8,128)(2,1)S(1)}, bf16[96,768]{1,0:T(8,128)(2,1)S(1)}, u32[]{:S(2)}, u32[]{:S(2)}) collective-permute-start(bf16[96,768]{1,0:T(8,128)(2,1)S(1)} %fusion.13), channel_id=1, source_target_pairs={{0,16},{4,20},{8,24},{12,28},{16,0},{20,4},{24,8},{28,12},{1,17},{... | collective-permute-start | bytes 442376 | tf_op jit(solution)/shard_map/ppermute | solution.py:623
  481.0 33.2 %collective-permute-start.55 = (bf16[96,768]{1,0:T(8,128)(2,1)S(1)}, bf16[96,768]{1,0:T(8,128)(2,1)S(1)}, u32[]{:S(2)}, u32[]{:S(2)}) collective-permute-start(bf16[96,768]{1,0:T(8,128)(2,1)S(1)} %fusion.13), channel_id=1, source_target_pairs={{0,24},{4,28},{8,16},{12,20},{16,8},{20,12},{24,0},{28,4},{1,25},{... | collective-permute-start | bytes 442376 | tf_op jit(solution)/shard_map/ppermute | solution.py:623
  (99 other events, 1508.8 us)
Sparse Core Ops, SparseCore 0:
  414.1 33.9 all-gather.2

commit v2 on v1

v2 whole, which is shorter than its diff:
```python
from functools import partial
import jax
import jax.numpy as jnp
from jax import lax
from jax.experimental import pallas as pl
from jax.experimental.pallas import tpu as pltpu
from jax.sharding import PartitionSpec as P

f32 = jnp.float32
bf16 = jnp.bfloat16
D = 768
H = 12
HD = 64
FF = 3072
L = 512
SEG = 128
NSEG = 4
MICRO = 2
T = MICRO * L
HALF = 384
FH = 1536
VMEM_LIMIT = 56 * 1024 * 1024


LONG = pl.CostEstimate(flops=30_000_000_000, bytes_accessed=1_000_000, transcendentals=0)
SHORT = pl.CostEstimate(flops=1, bytes_accessed=1, transcendentals=0)


def params(*sem):
    return pltpu.CompilerParams(vmem_limit_bytes=VMEM_LIMIT, dimension_semantics=sem)


def dot(a, b, ca=1, cb=0):
    return lax.dot_general(a, b, (((ca,), (cb,)), ((), ())), preferred_element_type=f32)


def norm_of(values):
    centred = values - jnp.mean(values, axis=1, keepdims=True)
    inverse = lax.rsqrt(jnp.mean(centred * centred, axis=1, keepdims=True) + 1e-6)
    return centred * inverse, inverse


def norm_back(grad, normed, inverse):
    return inverse * (
        grad
        - jnp.mean(grad, axis=1, keepdims=True)
        - normed * jnp.mean(grad * normed, axis=1, keepdims=True)
    )


UR = 48
ANY = pl.BlockSpec(memory_space=pl.ANY)
SMEM = pl.BlockSpec(memory_space=pltpu.SMEM)
VMEM = pl.BlockSpec(memory_space=pltpu.VMEM)


def whole(shape):
    return pl.BlockSpec(shape, lambda *_: (0,) * len(shape))


def bring(copies, sems):
    made = [pltpu.make_async_copy(source, target, sems.at[n]) for n, (source, target) in enumerate(copies)]
    return made


def go(made):
    for copy in made:
        copy.start()


def ready(made):
    for copy in made:
        copy.wait()


def quarters(idx_ref, sources):
    me, spot = idx_ref[0], idx_ref[1]
    for ref, lead, other in sources:
        for k in range(1, 4):
            yield (
                ref.at[k - 1] if lead is None else ref.at[lead, k - 1],
                lax.rem(me + 4 - k, 4),
                lax.bitwise_xor(spot, other),
            )


def pick_entry_body(idx_ref, w_ref, proj_ref, own_ref, piece_ref):
    spot, core = idx_ref[1], idx_ref[2]
    for n, half in enumerate((1 - core, core)):
        for u in range(3):
            column = pl.multiple_of((2 * u + half) * HALF, HALF)
            own_ref[n, u] = w_ref[:, pl.ds(column, HALF)].reshape(4, UR, HALF)
        own_ref[n, 3] = proj_ref[:, pl.ds(pl.multiple_of(half * HALF, HALF), HALF)].reshape(4, UR, HALF)
    for u in range(4):
        piece_ref[u] = own_ref[0, u, spot]


def pick_entry(idx, w, proj):
    return pl.pallas_call(
        pick_entry_body,
        in_specs=[SMEM, VMEM, VMEM],
        out_specs=[VMEM, VMEM],
        out_shape=[jax.ShapeDtypeStruct((2, 4, 4, UR, HALF), bf16), jax.ShapeDtypeStruct((4, UR, HALF), bf16)],
        compiler_params=params(),
        cost_estimate=SHORT,
        name="pick_entry",
    )(idx, w, proj)


def pick_ff_body(idx_ref, fc1_ref, fc2_ref, own1_ref, own2_ref, piece_ref):
    spot, core = idx_ref[1], idx_ref[2]
    for n, half in enumerate((1 - core, core)):
        for z in range(4):
            column = pl.multiple_of((2 * z + half) * HALF, HALF)
            own1_ref[n, z] = fc1_ref[:, pl.ds(column, HALF)].reshape(4, UR, HALF)
        for j in range(2):
            for i in range(2):
                row = pl.multiple_of(half * HALF + i * 192, 192)
                own2_ref[n, 2 * j + i] = fc2_ref[pl.ds(row, 192), j * HALF : (j + 1) * HALF].reshape(4, UR, HALF)
    for n, q in enumerate((spot, lax.bitwise_xor(spot, 3))):
        for u in range(4):
            piece_ref[n, u] = own1_ref[0, u, q]
            piece_ref[n, 4 + u] = own2_ref[0, u, q]


def pick_ff(idx, fc1, fc2):
    return pl.pallas_call(
        pick_ff_body,
        in_specs=[SMEM, VMEM, VMEM],
        out_specs=[VMEM] * 3,
        out_shape=[
            jax.ShapeDtypeStruct((2, 4, 4, UR, HALF), bf16),
            jax.ShapeDtypeStruct((2, 4, 4, UR, HALF), bf16),
            jax.ShapeDtypeStruct((2, 8, UR, HALF), bf16),
        ],
        compiler_params=params(),
        cost_estimate=SHORT,
        name="pick_ff",
    )(idx, fc1, fc2)


def pick_ada_body(idx_ref, w_ref, own_ref, piece_ref):
    spot, core = idx_ref[1], idx_ref[2]
    for n, half in enumerate((1 - core, core)):
        for c in range(3):
            for i in range(2):
                row = pl.multiple_of(half * HALF + i * 192, 192)
                own_ref[n, 2 * c + i] = w_ref[pl.ds(row, 192), c * HALF : (c + 1) * HALF].reshape(4, UR, HALF)
    for u in range(6):
        piece_ref[u] = own_ref[0, u, spot]


def pick_ada(idx, w):
    return pl.pallas_call(
        pick_ada_body,
        in_specs=[SMEM, VMEM],
        out_specs=[VMEM, VMEM],
        out_shape=[jax.ShapeDtypeStruct((2, 6, 4, UR, HALF), bf16), jax.ShapeDtypeStruct((6, UR, HALF), bf16)],
        compiler_params=params(),
        cost_estimate=SHORT,
        name="pick_ada",
    )(idx, w)


def entry_copies(idx_ref, own, half, sources, held):
    return [(own.at[half, pl.ds(0, 3)], held.at[:, idx_ref[0]])] + [
        (ref.at[pl.ds(0, 3)], held.at[:, z, q]) for ref, z, q in quarters(idx_ref, sources)
    ]


def stacked(ref):
    return [(ref, n, n) for n in range(4)]


def proj_copies(idx_ref, own, half, at, sources, held):
    return [(own.at[half, 3], held.at[at, idx_ref[0]])] + [
        (ref.at[3], held.at[at, z, q]) for ref, z, q in quarters(idx_ref, sources)
    ]


def fc1_copies(idx_ref, own, half, sources, held):
    return [(own.at[half], held.at[:, idx_ref[0]])] + [
        (ref.at[pl.ds(0, 4)], held.at[:, z, q]) for ref, z, q in quarters(idx_ref, sources)
    ]


def fc2_copies(idx_ref, own, half, sources, held):
    return [(own.at[half, pl.ds(2 * j, 2)], held.at[j, idx_ref[0]]) for j in range(2)] + [
        (ref.at[pl.ds(4 + 2 * j, 2)], held.at[j, z, :, q]) for ref, z, q in quarters(idx_ref, sources) for j in range(2)
    ]


def ada_copies(idx_ref, own, half, sources, held):
    return [(own.at[half, pl.ds(2 * c, 2)], held.at[idx_ref[0], c]) for c in range(3)] + [
        (ref.at[pl.ds(2 * c, 2)], held.at[z, c, :, q]) for ref, z, q in quarters(idx_ref, sources) for c in range(3)
    ]


def entry_weight(held):
    return jnp.concatenate([held[u].reshape(D, HALF) for u in range(3)], axis=1)


def proj_weight(held):
    return jnp.concatenate([held[n].reshape(D, HALF) for n in range(2)], axis=1)


ENTRY_HELD = (3, 4, 4, UR, HALF)


def qkv_first_body(idx_ref, x_ref, mod_ref, b_ref, own, fetched, a_ref, qkv_ref, held, sems):
    i = pl.program_id(0)
    copies = bring(entry_copies(idx_ref, own, 0, stacked(fetched), held), sems)

    @pl.when(i == 0)
    def _():
        go(copies)

    for s in range(NSEG):
        rows = pl.ds(s * SEG, SEG)
        at = pl.ds(i * NSEG + s, 1)
        norm, _ = norm_of(x_ref[rows, :].astype(f32))
        a_ref[rows, :] = (norm * (1.0 + mod_ref[1, at, :]) + mod_ref[0, at, :]).astype(bf16)

    @pl.when(i == 0)
    def _():
        ready(copies)

    qkv_ref[...] = (dot(a_ref[...], entry_weight(held)) + b_ref[...]).astype(bf16)


def qkv_first(idx, x, mods, b, own, near):
    return pl.pallas_call(
        qkv_first_body,
        grid=(MICRO,),
        in_specs=[
            SMEM,
            pl.BlockSpec((L, D), lambda i: (i, 0)),
            whole((6, MICRO * NSEG, D)),
            whole((1, 3 * HALF)),
            ANY, ANY,
        ],
        out_specs=[
            pl.BlockSpec((L, D), lambda i: (i, 0)),
            pl.BlockSpec((L, 3 * HALF), lambda i: (i, 0)),
        ],
        out_shape=[
            jax.ShapeDtypeStruct((T, D), bf16),
            jax.ShapeDtypeStruct((T, 3 * HALF), bf16),
        ],
        scratch_shapes=[pltpu.VMEM(ENTRY_HELD, bf16), pltpu.SemaphoreType.DMA((13,))],
        compiler_params=params("arbitrary"),
        cost_estimate=SHORT,
        name="qkv_first",
    )(idx, x, mods, b, own, near)


def qkv_second_body(idx_ref, a_ref, b_ref, own, fetched, qkv_ref, held, sems):
    copies = bring(entry_copies(idx_ref, own, 1, stacked(fetched), held), sems)

    @pl.when(pl.program_id(0) == 0)
    def _():
        go(copies)
        ready(copies)

    qkv_ref[...] = (dot(a_ref[...], entry_weight(held)) + b_ref[...]).astype(bf16)


def qkv_second(idx, a, b, own, near):
    return pl.pallas_call(
        qkv_second_body,
        grid=(MICRO,),
        in_specs=[
            SMEM,
            pl.BlockSpec((L, D), lambda i: (i, 0)),
            whole((1, 3 * HALF)),
            ANY, ANY,
        ],
        out_specs=pl.BlockSpec((L, 3 * HALF), lambda i: (i, 0)),
        out_shape=jax.ShapeDtypeStruct((T, 3 * HALF), bf16),
        scratch_shapes=[pltpu.VMEM(ENTRY_HELD, bf16), pltpu.SemaphoreType.DMA((13,))],
        compiler_params=params("arbitrary"),
        cost_estimate=SHORT,
        name="qkv_second",
    )(idx, a, b, own, near)


def lane_reverse(rows):
    at = lax.broadcasted_iota(jnp.int32, (2 * SEG, 2 * SEG), 0) + lax.broadcasted_iota(jnp.int32, (2 * SEG, 2 * SEG), 1)
    turn = (at == 2 * SEG - 2).astype(f32)
    return lax.dot_general(
        rows, turn, (((1,), (0,)), ((), ())), precision=lax.Precision.HIGHEST, preferred_element_type=f32
    )


def attend_body(long_ref, valid_ref, q_ref, k_ref, v_ref, t_ref, o_ref, p_ref, bias_ref):
    b = pl.program_id(1)

    @pl.when(b == 0)
    def _():
        windows = [t_ref[0, h : h + 1, d * SEG : (d + 2) * SEG] for h in range(2) for d in range(7)]
        windows = lane_reverse(jnp.concatenate(windows + windows[:2], axis=0))
        for h in range(2):
            for d in range(7):
                row = jnp.broadcast_to(windows[h * 7 + d : h * 7 + d + 1, :], (SEG, 2 * SEG))
                bias_ref[h, d] = pltpu.roll(row, SEG + 1, 1, stride=1, stride_axis=0)[:, :SEG]

    is_long = long_ref[b]
    lane = lax.broadcasted_iota(jnp.int32, (L, 2 * HD), 1)
    query = q_ref[...] * jnp.asarray(HD**-0.5, bf16)
    keys = k_ref[...]
    values_t = v_ref[...].T
    outs = []
    for h in range(2):
        mine = (lane < HD) if h == 0 else (lane >= HD)
        key_h = jnp.where(mine, keys, jnp.zeros_like(keys))
        for qb in range(NSEG):
            cols = pl.ds(qb * SEG, SEG)
            scores = dot(key_h, query[qb * SEG : (qb + 1) * SEG, :], 1, 1)
            parts = []
            for kb in range(NSEG):
                open_ = (valid_ref[b, kb] > 0) if kb == qb else ((valid_ref[b, kb] > 0) & (is_long > 0))
                shut = jnp.where(open_, 0.0, -1e30).astype(f32)
                parts.append(scores[kb * SEG : (kb + 1) * SEG, :] + (bias_ref[h, kb - qb + 3] + shut))
            scores = jnp.concatenate(parts, axis=0)
            top = jnp.max(scores, axis=0, keepdims=True)
            expo = jnp.exp(scores - top)
            total = jnp.sum(expo, axis=0, keepdims=True)
            p_ref[0, h, :, cols] = (expo * (1.0 / total)).astype(bf16)
        outs.append(dot(values_t[h * HD : (h + 1) * HD, :], p_ref[0, h]))
    o_ref[...] = jnp.concatenate(outs, axis=0).T.astype(bf16)


def attend(qkv, table, long_flag, valid_seg):
    pairs = 3
    return pl.pallas_call(
        attend_body,
        grid_spec=pltpu.PrefetchScalarGridSpec(
            num_scalar_prefetch=2,
            grid=(pairs, MICRO),
            in_specs=[
                pl.BlockSpec((L, 2 * HD), lambda g, b, *_: (b, g)),
                pl.BlockSpec((L, 2 * HD), lambda g, b, *_: (b, 3 + g)),
                pl.BlockSpec((L, 2 * HD), lambda g, b, *_: (b, 6 + g)),
                pl.BlockSpec((1, 2, 2 * L), lambda g, b, *_: (g, 0, 0)),
            ],
            out_specs=[
                pl.BlockSpec((L, 2 * HD), lambda g, b, *_: (b, g)),
                pl.BlockSpec((1, 2, L, L), lambda g, b, *_: (b, g, 0, 0)),
            ],
            scratch_shapes=[pltpu.VMEM((2, 7, SEG, SEG), f32)],
        ),
        out_shape=[
            jax.ShapeDtypeStruct((T, HALF), bf16),
            jax.ShapeDtypeStruct((MICRO, 6, L, L), bf16),
        ],
        compiler_params=params("arbitrary", "arbitrary"),
        cost_estimate=SHORT,
        name="attend",
    )(long_flag, valid_seg, qkv, qkv, qkv, table)


def middle_body(idx_ref, o1_ref, o2_ref, b_ref, x_ref, dy_ref, mod_ref, own, fetched, peer,
                h_ref, m_ref, attn_ref, dmlp_ref, db_ref, held, w_ref, sems):
    core = idx_ref[2]
    i = pl.program_id(0)

    @pl.when(i == 0)
    def _():
        copies = bring(
            proj_copies(idx_ref, own, 0, 1 - core, stacked(fetched), held)
            + proj_copies(idx_ref, own, 1, core, stacked(peer), held),
            sems,
        )
        go(copies)
        ready(copies)
        w_ref[...] = proj_weight(held)

    first = pl.multiple_of((1 - core) * HALF, HALF)
    second = pl.multiple_of(core * HALF, HALF)
    attn = dot(o1_ref[...], w_ref[pl.ds(first, HALF), :]) + dot(o2_ref[...], w_ref[pl.ds(second, HALF), :])
    attn = attn + b_ref[...]
    attn_ref[...] = attn.astype(bf16)
    total = jnp.zeros((1, D), f32)
    for s in range(NSEG):
        rows = pl.ds(s * SEG, SEG)
        at = pl.ds(i * NSEG + s, 1)
        hidden = x_ref[rows, :].astype(f32) + mod_ref[2, at, :] * attn[s * SEG : (s + 1) * SEG, :]
        h_ref[rows, :] = hidden
        norm, _ = norm_of(hidden)
        m_ref[rows, :] = (norm * (1.0 + mod_ref[4, at, :]) + mod_ref[3, at, :]).astype(bf16)
        dmlp = (dy_ref[rows, :].astype(f32) * mod_ref[5, at, :]).astype(bf16)
        dmlp_ref[rows, :] = dmlp
        total = total + jnp.sum(dmlp.astype(f32), axis=0, keepdims=True)

    @pl.when(pl.program_id(0) == 0)
    def _():
        db_ref[...] = jnp.zeros_like(db_ref)

    db_ref[0:1, :] += total


def middle(idx, o1, o2, b, x, dy, mods, own, one, two):
    row = lambda i: (i, 0)
    return pl.pallas_call(
        middle_body,
        grid=(MICRO,),
        in_specs=[
            SMEM,
            pl.BlockSpec((L, HALF), row),
            pl.BlockSpec((L, HALF), row),
            whole((1, D)),
            pl.BlockSpec((L, D), row),
            pl.BlockSpec((L, D), row),
            whole((6, MICRO * NSEG, D)),
        ] + [ANY] * 3,
        out_specs=[
            pl.BlockSpec((L, D), row),
            pl.BlockSpec((L, D), row),
            pl.BlockSpec((L, D), row),
            pl.BlockSpec((L, D), row),
            whole((8, D)),
        ],
        out_shape=[
            jax.ShapeDtypeStruct((T, D), f32),
            jax.ShapeDtypeStruct((T, D), bf16),
            jax.ShapeDtypeStruct((T, D), bf16),
            jax.ShapeDtypeStruct((T, D), bf16),
            jax.ShapeDtypeStruct((8, D), f32),
        ],
        scratch_shapes=[
            pltpu.VMEM((2, 4, 4, UR, HALF), bf16),
            pltpu.VMEM((D, D), bf16),
            pltpu.SemaphoreType.DMA((26,)),
        ],
        compiler_params=params("arbitrary"),
        cost_estimate=LONG,
        name="middle",
    )(idx, o1, o2, b, x, dy, mods, own, one, two)


FB = 768


def mlp_body(has_acc, idx_ref, m_ref, dmlp_ref, b_ref, own1, own2, fetched, *refs):
    if has_acc:
        acc_o, acc_d, out_o, out_d, dw1_ref, dw2_ref, db_ref, g_s, du_s, held1, held2, sems = refs
    else:
        out_o, out_d, dw1_ref, dw2_ref, db_ref, g_s, du_s, held1, held2, sems = refs
    f = pl.program_id(0)
    half_index = 1 if has_acc else 0

    @pl.when(f == 0)
    def _():
        copies = bring(
            fc1_copies(idx_ref, own1, half_index, stacked(fetched), held1)
            + fc2_copies(idx_ref, own2, half_index, stacked(fetched), held2),
            sems,
        )
        go(copies)
        ready(copies)

    w1 = jnp.concatenate([held1[2 * f + n].reshape(D, HALF) for n in range(2)], axis=1)
    w2 = jnp.concatenate([held2[j, pl.ds(2 * f, 2)].reshape(D, HALF) for j in range(2)], axis=1)
    bias = b_ref[0:1, :]
    chunk = 256
    total = jnp.zeros((1, FB), f32)
    c0 = (2.0 / jnp.pi) ** 0.5
    for r in range(T // chunk):
        rows = pl.ds(r * chunk, chunk)
        u = dot(m_ref[rows, :], w1) + bias
        dg = dot(dmlp_ref[rows, :], w2, 1, 1)
        u2 = u * u
        th = jnp.tanh(u * (c0 + (c0 * 0.044715) * u2))
        half = 0.5 + 0.5 * th
        g_s[rows, :] = (u * half).astype(bf16)
        slope = half + u * (0.5 - 0.5 * th * th) * (c0 + (3.0 * c0 * 0.044715) * u2)
        du = (dg * slope).astype(bf16)
        du_s[rows, :] = du
        total = total + jnp.sum(du.astype(f32), axis=0, keepdims=True)
    db_ref[0:1, :] = total

    @pl.when(f == 0)
    def _():
        if has_acc:
            out_o[...] = acc_o[...] + dot(g_s[...], w2)
            out_d[...] = acc_d[...] + dot(du_s[...], w1, 1, 1)
        else:
            out_o[...] = dot(g_s[...], w2)
            out_d[...] = dot(du_s[...], w1, 1, 1)

    @pl.when(f > 0)
    def _():
        out_o[...] += dot(g_s[...], w2)
        out_d[...] += dot(du_s[...], w1, 1, 1)

    dw2_ref[...] = dot(g_s[...], dmlp_ref[...], 0, 0).astype(bf16)
    dw1_ref[...] = dot(m_ref[...], du_s[...], 0, 0).astype(bf16)


def mlp(idx, m_in, dmlp, b1, own1, own2, fetched, acc=None):
    zero = lambda f: (0, 0)
    col = lambda f: (0, f)
    once = pl.Buffered(1)
    specs = [
        SMEM,
        pl.BlockSpec((T, D), zero, pipeline_mode=once),
        pl.BlockSpec((T, D), zero, pipeline_mode=once),
        pl.BlockSpec((1, FB), col),
    ] + [ANY] * 3
    args = [idx, m_in, dmlp, b1, own1, own2, fetched]
    if acc is not None:
        specs += [pl.BlockSpec((T, D), zero, pipeline_mode=once)] * 2
        args += list(acc)
    return pl.pallas_call(
        partial(mlp_body, acc is not None),
        grid=(FH // FB,),
        in_specs=specs,
        out_specs=[
            pl.BlockSpec((T, D), zero),
            pl.BlockSpec((T, D), zero),
            pl.BlockSpec((D, FB), col),
            pl.BlockSpec((FB, D), lambda f: (f, 0)),
            pl.BlockSpec((8, FB), col),
        ],
        out_shape=[
            jax.ShapeDtypeStruct((T, D), f32),
            jax.ShapeDtypeStruct((T, D), f32),
            jax.ShapeDtypeStruct((D, FH), bf16),
            jax.ShapeDtypeStruct((FH, D), bf16),
            jax.ShapeDtypeStruct((8, FH), f32),
        ],
        scratch_shapes=[
            pltpu.VMEM((T, FB), bf16),
            pltpu.VMEM((T, FB), bf16),
            pltpu.VMEM((4, 4, 4, UR, HALF), bf16),
            pltpu.VMEM((2, 4, 2, 4, UR, HALF), bf16),
            pltpu.SemaphoreType.DMA((39,)),
        ],
        compiler_params=params("arbitrary"),
        cost_estimate=LONG,
        name="mlp",
    )(*args)


def back_middle_body(idx_ref, h_ref, dy_ref, mlp_ref, b2_ref, dm_ref, attn_ref, mod_ref, o1_ref, o2_ref,
                     own, fetched, peer,
                     y_ref, dh_ref, do1_ref, do2_ref, dws_ref, dwk_ref, dmod_ref, db_ref,
                     dattn_s, dw_s, held, w_ref, sems):
    i = pl.program_id(0)
    core = idx_ref[2]
    first = pl.multiple_of((1 - core) * HALF, HALF)
    second = pl.multiple_of(core * HALF, HALF)
    copies = bring(
        proj_copies(idx_ref, own, 0, 1 - core, stacked(fetched), held)
        + proj_copies(idx_ref, own, 1, core, stacked(peer), held),
        sems,
    )

    @pl.when(i == 0)
    def _():
        go(copies)

    total = jnp.zeros((1, D), f32)
    for s in range(NSEG):
        rows = pl.ds(s * SEG, SEG)
        at = pl.ds(i * NSEG + s, 1)
        hidden = h_ref[rows, :]
        dy = dy_ref[rows, :].astype(f32)
        ff = mlp_ref[rows, :] + b2_ref[...]
        y_ref[rows, :] = (hidden + mod_ref[5, at, :] * ff).astype(bf16)
        dmod_ref[5, at, :] = jnp.sum(dy * ff, axis=0, keepdims=True)
        norm, inverse = norm_of(hidden)
        dm = dm_ref[rows, :]
        dmod_ref[3, at, :] = jnp.sum(dm, axis=0, keepdims=True)
        dmod_ref[4, at, :] = jnp.sum(dm * norm, axis=0, keepdims=True)
        dh = dy + norm_back(dm * (1.0 + mod_ref[4, at, :]), norm, inverse)
        dh_ref[rows, :] = dh
        dmod_ref[2, at, :] = jnp.sum(dh * attn_ref[rows, :].astype(f32), axis=0, keepdims=True)
        dattn = (dh * mod_ref[2, at, :]).astype(bf16)
        dattn_s[rows, :] = dattn
        total = total + jnp.sum(dattn.astype(f32), axis=0, keepdims=True)
    dattn = dattn_s[...]

    @pl.when(i == 0)
    def _():
        ready(copies)
        w_ref[...] = proj_weight(held)

    do1_ref[...] = dot(dattn, w_ref[pl.ds(first, HALF), :], 1, 1).astype(bf16)
    do2_ref[...] = dot(dattn, w_ref[pl.ds(second, HALF), :], 1, 1).astype(bf16)

    @pl.when(i == 0)
    def _():
        db_ref[...] = jnp.zeros_like(db_ref)
        dmod_ref[0:2] = jnp.zeros((2, MICRO * NSEG, D), f32)
        dw_s[...] = jnp.zeros_like(dw_s)

    db_ref[0:1, :] += total
    dw_s[pl.ds(first, HALF), :] += dot(o1_ref[...], dattn, 0, 0)
    dw_s[pl.ds(second, HALF), :] += dot(o2_ref[...], dattn, 0, 0)

    @pl.when(i == MICRO - 1)
    def _():
        dws_ref[...] = dw_s[:, pl.ds(first, HALF)].astype(bf16)
        dwk_ref[...] = dw_s[:, pl.ds(second, HALF)].astype(bf16)


def back_middle(idx, h, dy, ff, b2, dm, attn, mods, o1, o2, own, one, two):
    row = lambda i: (i, 0)
    full = pl.BlockSpec((L, D), row)
    part = pl.BlockSpec((L, HALF), row)
    modspec = whole((6, MICRO * NSEG, D))
    return pl.pallas_call(
        back_middle_body,
        grid=(MICRO,),
        in_specs=[SMEM, full, full, full, whole((1, D)), full, full, modspec, part, part] + [ANY] * 3,
        out_specs=[full, full, part, part, whole((D, HALF)), whole((D, HALF)), modspec, whole((8, D))],
        scratch_shapes=[
            pltpu.VMEM((L, D), bf16),
            pltpu.VMEM((D, D), f32),
            pltpu.VMEM((2, 4, 4, UR, HALF), bf16),
            pltpu.VMEM((D, D), bf16),
            pltpu.SemaphoreType.DMA((26,)),
        ],
        out_shape=[
            jax.ShapeDtypeStruct((T, D), bf16),
            jax.ShapeDtypeStruct((T, D), f32),
            jax.ShapeDtypeStruct((T, HALF), bf16),
            jax.ShapeDtypeStruct((T, HALF), bf16),
            jax.ShapeDtypeStruct((D, HALF), bf16),
            jax.ShapeDtypeStruct((D, HALF), bf16),
            jax.ShapeDtypeStruct((6, MICRO * NSEG, D), f32),
            jax.ShapeDtypeStruct((8, D), f32),
        ],
        compiler_params=params("arbitrary"),
        cost_estimate=LONG,
        name="back_middle",
    )(idx, h, dy, ff, b2, dm, attn, mods, o1, o2, own, one, two)


def attend_back_body(q_ref, k_ref, v_ref, p_ref, do_ref, o_ref, dq_ref, dk_ref, dv_ref, dt_ref, db_ref, acc_ref, ds_s):
    b = pl.program_id(1)

    @pl.when(b == 0)
    def _():
        acc_ref[...] = jnp.zeros_like(acc_ref)
        db_ref[...] = jnp.zeros_like(db_ref)

    lane = lax.broadcasted_iota(jnp.int32, (L, 2 * HD), 1)
    query = q_ref[...]
    keys_t = k_ref[...].T
    values = v_ref[...]
    dout = do_ref[...]
    prod = (dout.astype(f32) * o_ref[...].astype(f32)).T
    dqs, dks, dvs = [], [], []
    for h in range(2):
        mine = (lane < HD) if h == 0 else (lane >= HD)
        value_h = jnp.where(mine, values, jnp.zeros_like(values))
        delta = jnp.sum(prod[h * HD : (h + 1) * HD, :], axis=0, keepdims=True)
        for qb in range(NSEG):
            cols = slice(qb * SEG, (qb + 1) * SEG)
            dp = dot(value_h, dout[cols, :], 1, 1)
            ds = (p_ref[0, h, :, cols].astype(f32) * (dp - delta[:, cols])).astype(bf16)
            ds_s[h, :, cols] = ds
            for kb in range(NSEG):
                acc_ref[h, kb - qb + 3] += ds[kb * SEG : (kb + 1) * SEG, :].astype(f32)
        dvs.append(dot(p_ref[0, h], dout))
        dks.append(dot(ds_s[h], query))
        dqs.append(dot(keys_t[h * HD : (h + 1) * HD, :], ds_s[h]))
    low = lane < HD
    scale = HD**-0.5
    dq = (jnp.concatenate(dqs, axis=0).T * scale).astype(bf16)
    dk = (jnp.where(low, dks[0], dks[1]) * scale).astype(bf16)
    dv = jnp.where(low, dvs[0], dvs[1]).astype(bf16)
    dq_ref[...] = dq
    dk_ref[...] = dk
    dv_ref[...] = dv
    db_ref[0:1, :] += jnp.sum(dq.astype(f32), axis=0, keepdims=True)
    db_ref[1:2, :] += jnp.sum(dv.astype(f32), axis=0, keepdims=True)

    @pl.when(b == MICRO - 1)
    def _():
        sums = []
        for h in range(2):
            for d in range(7):
                wide = jnp.concatenate([acc_ref[h, d], jnp.zeros((SEG, SEG), f32)], axis=1)
                rows = SEG
                while rows > 1:
                    rows //= 2
                    wide = pltpu.roll(wide[:rows], rows, 1) + wide[rows:]
                sums.append(wide)
        sums = lane_reverse(jnp.concatenate(sums + sums[:2], axis=0))
        dt_ref[...] = jnp.zeros_like(dt_ref)
        for h in range(2):
            for d in range(7):
                dt_ref[0, h : h + 1, d * SEG : (d + 2) * SEG] += sums[h * 7 + d : h * 7 + d + 1, :]


def attend_back(qkv, p, dout, out, cost):
    col = lambda g, b: (b, g)
    part = pl.BlockSpec((L, 2 * HD), col)
    return pl.pallas_call(
        attend_back_body,
        grid=(3, MICRO),
        in_specs=[
            part,
            pl.BlockSpec((L, 2 * HD), lambda g, b: (b, 3 + g)),
            pl.BlockSpec((L, 2 * HD), lambda g, b: (b, 6 + g)),
            pl.BlockSpec((1, 2, L, L), lambda g, b: (b, g, 0, 0)),
            part,
            part,
        ],
        out_specs=[part, part, part, pl.BlockSpec((1, 8, 2 * L), lambda g, b: (g, 0, 0)),
                   pl.BlockSpec((8, 2 * HD), lambda g, b: (0, g))],
        out_shape=[jax.ShapeDtypeStruct((T, HALF), bf16)] * 3
        + [jax.ShapeDtypeStruct((3, 8, 2 * L), f32), jax.ShapeDtypeStruct((8, HALF), f32)],
        scratch_shapes=[pltpu.VMEM((2, 7, SEG, SEG), f32), pltpu.VMEM((2, L, L), bf16)],
        compiler_params=params("arbitrary", "arbitrary"),
        cost_estimate=cost,
        name="attend_back",
    )(qkv, qkv, qkv, p, dout, out)


def qkv_weight_body(a_ref, dq_ref, dk_ref, dv_ref, out_ref):
    a = a_ref[...]
    out_ref[:, 0:HALF] = dot(a, dq_ref[...], 0, 0).astype(bf16)
    out_ref[:, HALF : 2 * HALF] = dot(a, dk_ref[...], 0, 0).astype(bf16)
    out_ref[:, 2 * HALF : 3 * HALF] = dot(a, dv_ref[...], 0, 0).astype(bf16)


def qkv_weight(a, dq, dk, dv, cost):
    return pl.pallas_call(
        qkv_weight_body,
        out_shape=jax.ShapeDtypeStruct((D, 3 * HALF), bf16),
        compiler_params=params(),
        cost_estimate=cost,
        name="qkv_weight",
    )(a, dq, dk, dv)


def back_entry_body(idx_ref, dq1, dk1, dv1, dq2, dk2, dv2, x_ref, dh_ref, mod_ref, own, fetched, peer,
                    dx_ref, dmod_ref, held1, held2, sems):
    i = pl.program_id(0)

    @pl.when(i == 0)
    def _():
        copies = bring(
            entry_copies(idx_ref, own, 0, stacked(fetched), held1)
            + entry_copies(idx_ref, own, 1, stacked(peer), held2),
            sems,
        )
        go(copies)
        ready(copies)

    one = jnp.concatenate([dq1[...], dk1[...], dv1[...]], axis=1)
    two = jnp.concatenate([dq2[...], dk2[...], dv2[...]], axis=1)
    da = dot(one, entry_weight(held1), 1, 1) + dot(two, entry_weight(held2), 1, 1)
    for s in range(NSEG):
        rows = pl.ds(s * SEG, SEG)
        at = pl.ds(i * NSEG + s, 1)
        piece = da[s * SEG : (s + 1) * SEG, :]
        norm, inverse = norm_of(x_ref[rows, :].astype(f32))
        dmod_ref[0, at, :] = jnp.sum(piece, axis=0, keepdims=True)
        dmod_ref[1, at, :] = jnp.sum(piece * norm, axis=0, keepdims=True)
        dx_ref[rows, :] = (
            dh_ref[rows, :] + norm_back(piece * (1.0 + mod_ref[1, at, :]), norm, inverse)
        ).astype(bf16)


def back_entry(idx, parts, x, dh, mods, own, near, peer):
    row = lambda i: (i, 0)
    full = pl.BlockSpec((L, D), row)
    part = pl.BlockSpec((L, HALF), row)
    return pl.pallas_call(
        back_entry_body,
        grid=(MICRO,),
        in_specs=[SMEM] + [part] * 6 + [full, full, whole((6, MICRO * NSEG, D))] + [ANY] * 3,
        out_specs=[full, whole((2, MICRO * NSEG, D))],
        out_shape=[jax.ShapeDtypeStruct((T, D), bf16), jax.ShapeDtypeStruct((2, MICRO * NSEG, D), f32)],
        scratch_shapes=[
            pltpu.VMEM(ENTRY_HELD, bf16),
            pltpu.VMEM(ENTRY_HELD, bf16),
            pltpu.SemaphoreType.DMA((26,)),
        ],
        compiler_params=params("arbitrary"),
        cost_estimate=SHORT,
        name="back_entry",
    )(idx, *parts, x, dh, mods, own, near, peer)


def pack_small_body(idx_ref, q1, q2, proj_ref, u1, u2, fc2_ref, t1, t2, out_ref):
    core = idx_ref[2]
    for z in range(4):
        half = z // 2
        tail = []
        for t in range(3):
            n = (z % 2) * 3 + t
            row = jnp.where(core == half, t2[n // 2, n % 2 : n % 2 + 1, :], t1[n // 2, n % 2 : n % 2 + 1, :])
            out_ref[z, t : t + 1, :] = row[:, :D]
            tail.append(row[:, D:])
        out_ref[z, 3:4, :] = jnp.concatenate(tail, axis=1)
        for h in range(2):
            block = slice(z * HALF, (z + 1) * HALF)
            out_ref[z, 4:5, h * HALF : (h + 1) * HALF] = jnp.where(core == h, u2[0:1, block], u1[0:1, block])
        half, kind = z % 2, z // 2
        out_ref[z, 5:6, 0:HALF] = jnp.where(core == half, q2[kind : kind + 1, :], q1[kind : kind + 1, :])
        out_ref[z, 5:6, HALF:] = jnp.zeros((1, HALF), f32)
        out_ref[z, 6:7, :] = proj_ref[0:1, :]
        out_ref[z, 7:8, :] = fc2_ref[0:1, :]


def pack_small(idx, *arrays):
    return pl.pallas_call(
        pack_small_body,
        in_specs=[SMEM] + [VMEM] * 8,
        out_specs=VMEM,
        out_shape=jax.ShapeDtypeStruct((4, 8, D), f32),
        compiler_params=params(),
        cost_estimate=SHORT,
        name="pack_small",
    )(idx, *arrays)


def back_cond_body(idx_ref, long_ref, valid_ref, mid_ref, entry_ref, slope_ref, own, fetched, peer,
                   out_ref, held1, held2, sems):
    copies = bring(
        ada_copies(idx_ref, own, 0, stacked(fetched), held1)
        + ada_copies(idx_ref, own, 1, stacked(peer), held2),
        sems,
    )
    go(copies)
    core = idx_ref[2]
    slots = MICRO * NSEG
    row = lax.broadcasted_iota(jnp.int32, (slots, 1), 0)
    upper = row < NSEG
    is_long = jnp.where(upper, long_ref[0], long_ref[1]) > 0
    valid = jnp.zeros((slots, 1), f32)
    for n in range(slots):
        valid = jnp.where(row == n, valid_ref[n // NSEG, n % NSEG].astype(f32), valid)
    lead = (row == 0) | (row == NSEG)
    blocks = []
    for j in range(6):
        value = entry_ref[j] if j < 2 else mid_ref[j]
        if j % 3 == 2:
            value = value * valid
        total = jnp.where(
            upper,
            jnp.sum(value[:NSEG], axis=0, keepdims=True),
            jnp.sum(value[NSEG:], axis=0, keepdims=True),
        )
        value = jnp.where(is_long, jnp.where(lead, total, 0.0), value).astype(bf16)
        blocks += [value[:, :HALF], value[:, HALF:]]
    ready(copies)
    for held, half in ((held1, 1 - core), (held2, core)):
        grad = jnp.zeros((slots, HALF), f32)
        for z in range(4):
            for c in range(3):
                grad += dot(blocks[3 * z + c], held[z, c].reshape(HALF, HALF), 1, 1)
        at = pl.ds(pl.multiple_of(half * HALF, HALF), HALF)
        out_ref[0, :, pl.ds(pl.multiple_of(3 * HALF + half * HALF, HALF), HALF)] = grad * slope_ref[:, at]
    for z in range(4):
        if z:
            out_ref[z, :, 3 * HALF :] = out_ref[0, :, 3 * HALF :]
        for c in range(3):
            out_ref[z, :, c * HALF : (c + 1) * HALF] = blocks[3 * z + c].astype(f32)


def back_cond(idx, long_flag, valid_seg, mid, entry, slope, own, near, peer):
    return pl.pallas_call(
        back_cond_body,
        in_specs=[SMEM, SMEM, SMEM, VMEM, VMEM, VMEM] + [ANY] * 3,
        out_specs=VMEM,
        out_shape=jax.ShapeDtypeStruct((4, MICRO * NSEG, 5 * HALF), f32),
        scratch_shapes=[
            pltpu.VMEM((4, 3, 2, 4, UR, HALF), bf16),
            pltpu.VMEM((4, 3, 2, 4, UR, HALF), bf16),
            pltpu.SemaphoreType.DMA((78,)),
        ],
        compiler_params=params(),
        cost_estimate=SHORT,
        name="back_cond",
    )(idx, long_flag, valid_seg, mid, entry, slope, own, near, peer)


def finish_ff_body(idx_ref, mine_ref, peer_ref, fc1_ref, fc2_ref):
    spot, core = idx_ref[1], idx_ref[2]
    for source, half in ((mine_ref, core), (peer_ref, 1 - core)):
        for j in range(4):
            place_at = lax.bitwise_xor(spot, j)
            low, high = lax.rem(place_at, 2), lax.div(place_at, 2)
            row = pl.multiple_of((2 * low + high) * 48, 16)
            for z in range(4):
                source_rows = pl.ds(48 * (z // 2), 48)
                block = source[j, source_rows, (z % 2) * HALF : (z % 2 + 1) * HALF]
                column = pl.multiple_of((2 * z + half) * HALF, 128)
                fc1_ref[pl.ds(row, 48), pl.ds(column, HALF)] = block.astype(f32)
            row = pl.multiple_of(half * HALF + (2 * high + low) * 96, 16)
            fc2_ref[pl.ds(row, 96), :] = source[j, 96:192, :].astype(f32)


def finish_ff(idx, mine, peer):
    vmem = pl.BlockSpec(memory_space=pltpu.VMEM)
    return pl.pallas_call(
        finish_ff_body,
        in_specs=[pl.BlockSpec(memory_space=pltpu.SMEM), vmem, vmem],
        out_specs=[vmem, vmem],
        out_shape=[jax.ShapeDtypeStruct((D // 4, FF), f32), jax.ShapeDtypeStruct((FF // 4, D), f32)],
        compiler_params=params(),
        cost_estimate=SHORT,
        name="finish_ff",
    )(idx, mine, peer)


def finish_attn_body(idx_ref, mine_ref, peer_ref, qkv_ref, proj_ref):
    spot, core = idx_ref[1], idx_ref[2]
    for source, half in ((mine_ref, core), (peer_ref, 1 - core)):
        column = half * HALF
        for j in range(4):
            place_at = lax.bitwise_xor(spot, j)
            low, high = lax.rem(place_at, 2), lax.div(place_at, 2)
            row0 = pl.multiple_of((2 * low + high) * 48, 16)
            row1 = pl.multiple_of((2 * high + low) * 48, 16)
            for t in range(4):
                block = source[j, 48 * (t // 2) : 48 * (t // 2 + 1), (t % 2) * HALF : (t % 2 + 1) * HALF].astype(f32)
                row = row0 if t < 2 else row1
                if t < 3:
                    qkv_ref[pl.ds(row, 48), pl.ds(pl.multiple_of(t * D + column, 128), HALF)] = block
                else:
                    proj_ref[pl.ds(row, 48), pl.ds(pl.multiple_of(column, 128), HALF)] = block


def finish_attn(idx, mine, peer):
    vmem = pl.BlockSpec(memory_space=pltpu.VMEM)
    return pl.pallas_call(
        finish_attn_body,
        in_specs=[pl.BlockSpec(memory_space=pltpu.SMEM), vmem, vmem],
        out_specs=[vmem, vmem],
        out_shape=[jax.ShapeDtypeStruct((D // 4, 3 * D), f32), jax.ShapeDtypeStruct((D // 4, D), f32)],
        compiler_params=params(),
        cost_estimate=SHORT,
        name="finish_attn",
    )(idx, mine, peer)


def swap(array, bit):
    count = lax.axis_size("dp")
    return lax.ppermute(array, "dp", [(i, i ^ bit) for i in range(count)])


def shift(array, step):
    count = lax.axis_size("mod")
    return lax.ppermute(array, "mod", [(i, (i + step) % count) for i in range(count)])


def take(array, index, size, axis=0):
    return lax.dynamic_slice_in_dim(array, index * size, size, axis)


def after(value, *earlier):
    return lax.optimization_barrier((value, *earlier))[0]


def fence(*values):
    return lax.optimization_barrier(values)


def around(piece):
    return [shift(piece, k) for k in range(1, 4)]


def three(near):
    return [near, swap(near, 2), swap(near, 4), swap(near, 6)]


def add(*terms):
    total = terms[0].astype(f32)
    for term in terms[1:]:
        total = total + term.astype(f32)
    return total.astype(bf16)


def spread_chips(grad):
    bit = 8
    while bit < lax.axis_size("dp"):
        grad = add(grad, swap(grad, bit))
        bit *= 2
    return grad


def pick_mod(grad, index):
    return lax.dynamic_index_in_dim(grad, index, 0, keepdims=False)


def local(
    block_input,
    grad_out,
    long_flag,
    valid_mask,
    labels,
    tsteps,
    time_table,
    class_table,
    w_ada,
    b_ada,
    w_qkv,
    qv_bias,
    w_proj,
    proj_bias,
    w_fc1,
    fc1_bias,
    w_fc2,
    fc2_bias,
    rel_table,
):
    mods_n = lax.axis_size("mod")
    me = lax.axis_index("mod")
    core = lax.axis_index("dp") % 2
    spot = (lax.axis_index("dp") // 2) % 4
    idx = jnp.stack([me, spot, core]).astype(jnp.int32)
    first = 1 - core
    slots_n = MICRO * NSEG

    own_a, piece_a = pick_entry(idx, w_qkv, w_proj)
    step_flat = tsteps.reshape(slots_n)
    label_flat = labels.reshape(slots_n)
    cond = time_table[step_flat].astype(f32) + class_table[label_flat].astype(f32)
    sigma = jax.nn.sigmoid(cond)
    act = (cond * sigma).astype(bf16)
    slope = sigma * (1.0 + cond * (1.0 - sigma))
    digits = jnp.stack([step_flat // 32, step_flat % 32, label_flat // 32, label_flat % 32], axis=1).astype(bf16)
    digits = jnp.pad(digits, ((0, 0), (0, 124)))
    rel_shape = rel_table.shape
    small = jnp.concatenate(
        [qv_bias, proj_bias, fc1_bias, fc2_bias, jnp.pad(rel_table, ((0, 0), (0, 1))).reshape(-1)]
    ).reshape(slots_n, -1)
    packet = jnp.concatenate([act, digits, small], axis=1)
    group = jnp.stack([packet] + [shift(packet, k) for k in range(1, mods_n)])
    near_a = jnp.stack(around(piece_a))
    group_act = group[:, :, :D].reshape(mods_n * slots_n, D)
    columns = jnp.dot(group_act, w_ada, preferred_element_type=f32) + b_ada.astype(f32)
    columns = columns.reshape(mods_n, slots_n, -1)
    own_1, own_2, piece_b = pick_ff(idx, w_fc1, w_fc2)
    near_a, columns, piece_b, group = fence(near_a, columns, piece_b, group)
    set_a = three(near_a)
    got_b = around(piece_b)
    back = [columns[0]] + [shift(columns[k], mods_n - k) for k in range(1, mods_n)]
    act_all = lax.all_gather(
        group[:, :, : D + 128].reshape(mods_n * slots_n, D + 128), "dp", axis=0, tiled=True
    )
    act_all, *rest = fence(act_all, *set_a, *back)
    set_a, back = jnp.stack(rest[:4]), rest[4:]
    turn = (mods_n - me) % mods_n
    modulation = lax.dynamic_slice_in_dim(jnp.stack(back + back), turn, mods_n, 0)
    modulation = modulation.transpose(1, 0, 2).reshape(MICRO, NSEG, 6, D)
    long_one = long_flag.reshape(MICRO)
    is_long = long_one[:, None, None, None] > 0
    seg_mod = jnp.where(is_long, modulation[:, :1], modulation)
    valid_seg = valid_mask.reshape(MICRO, NSEG, SEG)[:, :, 0]
    valid = valid_seg.astype(f32)[:, :, None, None]
    is_gate = (jnp.arange(6) % 3 == 2)[None, None, :, None]
    mods = jnp.where(is_gate, seg_mod * valid, seg_mod).reshape(slots_n, 6, D).transpose(1, 0, 2)

    rows_small = group[:, :, D + 128 :][::-1]
    rows_small = lax.dynamic_slice_in_dim(jnp.concatenate([rows_small, rows_small]), (mods_n - 1 - me) % mods_n, mods_n, 0)
    rows_small = rows_small.reshape(mods_n, -1).astype(f32)
    cuts = [0]
    for bias in (qv_bias, proj_bias, fc1_bias, fc2_bias):
        cuts.append(cuts[-1] + bias.shape[0])
    full_qv = rows_small[:, cuts[0] : cuts[1]].reshape(-1)
    full_proj_b = rows_small[:, cuts[1] : cuts[2]].reshape(1, -1)
    full_fc1_b = rows_small[:, cuts[2] : cuts[3]].reshape(mods_n, 2, HALF)
    full_fc2_b = rows_small[:, cuts[3] : cuts[4]].reshape(1, -1)
    full_rel = rows_small[:, cuts[4] :].reshape(2, H // 4, 2, 2 * L)
    bias_thirds = jnp.concatenate([full_qv[:D], jnp.zeros((D,), f32), full_qv[D:]]).reshape(3, 2, HALF)

    def by_half(array, axis):
        one, two = (lax.index_in_dim(array, n, axis, keepdims=False) for n in (0, 1))
        return jnp.where(core > 0, one, two), jnp.where(core > 0, two, one)

    qkv_b = [b.reshape(1, 3 * HALF) for b in by_half(bias_thirds, 1)]
    fc1_b = [b.reshape(1, FH) for b in by_half(full_fc1_b, 1)]
    rel = by_half(full_rel, 0)

    x = block_input.reshape(T, D)
    dy = grad_out.reshape(T, D)
    peer_a = swap(set_a, 1)
    a, qkv1 = qkv_first(idx, x, mods, qkv_b[0], own_a, set_a)
    o1, p1 = attend(qkv1, rel[0], long_one, valid_seg)
    a, o1, peer_a = fence(a, o1, peer_a)
    qkv2 = qkv_second(idx, a, qkv_b[1], own_a, peer_a)
    o2, p2 = attend(qkv2, rel[1], long_one, valid_seg)
    o2, *got_b = fence(o2, *got_b)
    near_b = jnp.stack([g[0] for g in got_b])
    diag_b = jnp.stack([g[1] for g in got_b])
    side_b = [swap(near_b, 2), swap(near_b, 4)]
    hidden, m_in, attn, d_mlp, db_fc2 = middle(idx, o1, o2, full_proj_b, x, dy, mods, own_a, set_a, peer_a)
    m_in, near_b, diag_b, *side_b = fence(m_in, near_b, diag_b, *side_b)
    set_b = jnp.stack([near_b, *side_b, diag_b])
    peer_b = swap(set_b, 1)
    own_c, piece_c = pick_ada(idx, w_ada)
    piece_c, m_in = fence(piece_c, m_in)
    got_c = around(piece_c)
    acc_o, acc_d, dw1_send, dw2_send, db1_first = mlp(idx, m_in, d_mlp, fc1_b[0], own_1, own_2, set_b)
    acc_o, peer_b, *got_c = fence(acc_o, peer_b, *got_c)
    near_c = jnp.stack(got_c)
    set_c = three(near_c)
    from_core = [swap(dw1_send, 1), swap(dw2_send, 1)]
    ff, dm, dw1_keep, dw2_keep, db1_second = mlp(
        idx, m_in, d_mlp, fc1_b[1], own_1, own_2, peer_b, (acc_o, acc_d)
    )
    ff, dw1_keep, dw2_keep, *rest = fence(ff, dw1_keep, dw2_keep, *from_core, *set_c)
    from_core, set_c = rest[:2], jnp.stack(rest[2:])

    side_x, side_y = spot % 2, spot // 2

    def cut(terms, side):
        size = terms[0].shape[1] // 2
        return [take(term, side, size, 1) for term in terms]

    terms_1 = [g.reshape(mods_n, D // mods_n, FH) for g in (dw1_keep, from_core[0])]
    terms_2 = [g.reshape(mods_n, HALF, D) for g in (dw2_keep, from_core[1])]
    in_1 = swap(add(*cut(terms_1, 1 - side_x)), 2)
    in_2 = swap(add(*cut(terms_2, 1 - side_y)), 4)
    y, d_h, do1, do2, dwp_send, dwp_keep, dmod_mid, db_proj = back_middle(
        idx, hidden, dy, ff, full_fc2_b, dm, attn, mods, o1, o2, own_a, set_a, peer_a
    )
    dq1, dk1, dv1, dt1, dbq1 = attend_back(qkv1, p1, do1, o1, SHORT)
    dwq_send = qkv_weight(a, dq1, dk1, dv1, SHORT)
    in_1, in_2, dwq_send, do2, set_c = fence(in_1, in_2, dwq_send, do2, set_c)
    terms_1 = cut(terms_1, side_x) + [in_1]
    terms_2 = cut(terms_2, side_y) + [in_2]
    far_in_1 = swap(add(*cut(terms_1, 1 - side_y)), 4)
    far_in_2 = swap(add(*cut(terms_2, 1 - side_x)), 2)
    peer_c = swap(set_c, 1)
    dwq_in = swap(dwq_send, 1)
    dwp_in = swap(dwp_send, 1)
    dq2, dk2, dv2, dt2, dbq2 = attend_back(qkv2, p2, do2, o2, LONG)
    dq2, dk2, dv2, dt2, dbq2, far_in_1, far_in_2, peer_c, dwq_in, dwp_in = fence(
        dq2, dk2, dv2, dt2, dbq2, far_in_1, far_in_2, peer_c, dwq_in, dwp_in
    )
    kept_1 = spread_chips(add(*cut(terms_1, side_y), far_in_1))
    kept_2 = spread_chips(add(*cut(terms_2, side_x), far_in_2))
    ff_parts = jnp.concatenate([kept_1[:, :, :D], kept_1[:, :, D:], kept_2], axis=1)

    def scatter_send(grad):
        return [shift(pick_mod(grad, (me + k) % mods_n), k) for k in range(1, mods_n)]

    ff_in = scatter_send(ff_parts)
    dwq_keep = qkv_weight(a, dq2, dk2, dv2, LONG)
    packed = pack_small(idx, dbq1, dbq2, db_proj, db1_first, db1_second, db_fc2, dt1, dt2).astype(bf16)
    packed = add(packed, swap(packed, 1))

    dwq = [dwq_keep, dwq_in]
    dwp = [g.reshape(mods_n, D // mods_n, HALF) for g in (dwp_keep, dwp_in)]
    left = [g[:, :D].reshape(mods_n, D // mods_n, D) for g in dwq]
    right = [g[:, D:].reshape(mods_n, D // mods_n, HALF) for g in dwq]

    def right_add(side):
        return jnp.concatenate([add(*cut(right, side)), add(*cut(dwp, side))], axis=2)

    in_l = swap(jnp.concatenate([add(*cut(left, 1 - side_x)), packed], axis=1), 2)
    in_r = swap(right_add(1 - side_y), 4)
    dx, dmod_entry = back_entry(
        idx, (dq1, dk1, dv1, dq2, dk2, dv2), x, after(d_h, dwq_keep), mods, own_a, set_a, peer_a
    )
    d_cond = back_cond(idx, long_one, valid_seg, dmod_mid, dmod_entry, slope, own_c, set_c, peer_c).astype(bf16)
    in_l, in_r, d_cond, dx, *ff_in = fence(in_l, in_r, d_cond, dx, *ff_in)
    rows = left[0].shape[1] // 2
    left = cut(left, side_x) + [in_l[:, :rows]]
    packed = add(packed, in_l[:, rows:])
    right_mid = [right_add(side_y), in_r]
    far_l = swap(jnp.concatenate([add(*cut(left, 1 - side_y)), packed], axis=1), 4)
    far_r = swap(add(*cut(right_mid, 1 - side_x)), 2)
    cond_in = scatter_send(d_cond)
    far_l, far_r, *cond_in = fence(far_l, far_r, *cond_in)
    packed = add(packed, far_l[:, rows // 2 :])
    attn_parts = spread_chips(
        jnp.concatenate(
            [add(*cut(left, side_y), far_l[:, : rows // 2]), add(*cut(right_mid, side_x), far_r), packed], axis=1
        )
    )
    attn_in = scatter_send(attn_parts)
    everyone = lax.all_gather(jnp.concatenate([pick_mod(d_cond, me), *cond_in]), "dp", axis=0, tiled=True)
    ff_part = add(pick_mod(ff_parts, me), *ff_in)
    attn_in[0], everyone = fence(attn_in[0], everyone)
    attn_part = add(pick_mod(attn_parts, me), *attn_in)

    def gather_chips(piece):
        mine = jnp.stack(three(piece))
        return mine, swap(mine, 1)

    grad_fc1, grad_fc2 = finish_ff(idx, *gather_chips(ff_part))
    grad_qkv, grad_proj = finish_attn(idx, *gather_chips(attn_part[:D // 8]))
    small_all = attn_part[D // 8 :].astype(f32)

    width = w_ada.shape[1]
    d_mod_all = everyone[:, :width]
    d_cond_all = everyone[:, width:]
    digits_all = act_all[:, D : D + 4].astype(jnp.int32)
    grad_ada = lax.dot_general(act_all[:, :D], d_mod_all, (((0,), (0,)), ((), ())), preferred_element_type=f32)
    grad_ada_b = jnp.sum(d_mod_all.astype(f32), axis=0)

    def table_grad(high, low, rows):
        share = rows // mods_n
        index = digits_all[:, high] * 32 + digits_all[:, low]
        hot = (index[None, :] == me * share + jnp.arange(share)[:, None]).astype(bf16)
        return jnp.dot(hot, d_cond_all, preferred_element_type=f32)

    grad_rel = jnp.concatenate([small_all[:3], small_all[3].reshape(3, 2 * L - D)], axis=1)
    return (
        y.reshape(block_input.shape),
        dx.reshape(block_input.shape),
        table_grad(0, 1, time_table.shape[0]),
        table_grad(2, 3, class_table.shape[0]),
        grad_ada,
        grad_ada_b,
        grad_qkv,
        small_all[5, : qv_bias.shape[0]],
        grad_proj,
        take(small_all[6], me, proj_bias.shape[0]),
        grad_fc1,
        small_all[4],
        grad_fc2,
        take(small_all[7], me, fc2_bias.shape[0]),
        grad_rel[:, : rel_shape[1]],
    )


def solution(mesh):
    in_specs = (
        P(None, ("dp", "mod"), None),
        P(None, ("dp", "mod"), None),
        P(None, ("dp", "mod")),
        P(None, ("dp", "mod")),
        P(None, ("dp", "mod")),
        P(None, ("dp", "mod")),
        P(),
        P(),
        P(None, "mod"),
        P("mod"),
        P("mod", None),
        P("mod"),
        P("mod", None),
        P("mod"),
        P("mod", None),
        P("mod"),
        P("mod", None),
        P("mod"),
        P("mod", None),
    )
    out_specs = (
        P(None, ("dp", "mod"), None),
        P(None, ("dp", "mod"), None),
        P("mod", None),
        P("mod", None),
        P(None, "mod"),
        P("mod"),
        P("mod", None),
        P("mod"),
        P("mod", None),
        P("mod"),
        P("mod", None),
        P("mod"),
        P("mod", None),
        P("mod"),
        P("mod", None),
    )
    return jax.shard_map(local, mesh=mesh, in_specs=in_specs, out_specs=out_specs, check_vma=False)
```

time: 588 us -> 415 us (0.71)
  the two profiles are of different devices: /device:TPU:9 before, /device:TPU:0 now
where the time goes in v2:
time: 415 us; the launch traced here: 409 us
  Pallas kernels  189 us (46%)
  starting transfers between devices  66.9 us (16%)
  local copies, waits for them, and re-layouts  50.4 us (12%)
  waiting for transfers between devices  35.5 us (9%)
  other arithmetic  32.3 us (8%)
  blocking collectives  28.3 us (7%)
  matrix products  5.28 us (1%)
    pallas_call x2, Pallas kernels, mlp(): pl.pallas_call(partial(mlp_body, acc is not None), grid=(FH // FB,), in_s...  47.2 us
    ppermute x24, starting transfers between devices, shift(): lax.ppermute(array, 'mod', [(i, (i + step) % count) for i in range(count)])  40.6 us
    pallas_call x2, Pallas kernels, attend(): pl.pallas_call(attend_body, grid_spec=pltpu.PrefetchScalarGridSpec(num_sc...  28.2 us
    pallas_call x2, Pallas kernels, attend_back(): pl.pallas_call(attend_back_body, grid=(3, MICRO), in_specs=[part, pl.Bloc...  26.9 us
    ppermute x32, starting transfers between devices, swap(): return lax.ppermute(array, 'dp', [(i, i ^ bit) for i in range(count)])  26.3 us
    ppermute x32, waiting for transfers between devices, swap(): return lax.ppermute(array, 'dp', [(i, i ^ bit) for i in range(count)])  21.3 us
    all_gather x1, blocking collectives, local(): lax.all_gather(group[:, :, :D + 128].reshape(mods_n * slots_n, D + 128),...  18.1 us
    convert_element_type x18, other arithmetic, add(): return total.astype(bf16)  18 us
  transfers between devices with their start and end apart: 56, of which 10 were waited for; matrix products, arithmetic and copies ran while one was open for 16% of the time, Pallas kernels for 43%

profile of v2, /device:TPU:0, one launch (start us, length us, event | category | flops | bytes accessed | tf_op | source)
XLA Modules:
  0.0 409.1 jit_solution(479744821537490201)
XLA Ops:
  3.8 5.0 %collective-permute-start.2 = (bf16[4,48,384]{2,1,0:T(8,128)(2,1)}, bf16[4,48,384]{2,1,0:T(8,128)(2,1)S(1)}, u32[]{:S(2)}, u32[]{:S(2)}) collective-permute-start(bf16[4,48,384]{2,1,0:T(8,128)(2,1)} %get-tuple-element.138), channel_id=1, source_target_pairs={{0,3},{1,0},{2,1},{3,2},{4,7},{5,4},{6,5},{7,6},{8,11},{9,8},{10,9... | collective-permute-start | bytes 442376 | tf_op jit(solution)/shard_map/ppermute | solution.py:952
  27.6 6.4 %collective-permute-done = bf16[4,48,384]{2,1,0:T(8,128)(2,1)S(1)} collective-permute-done((bf16[4,48,384]{2,1,0:T(8,128)(2,1)S(1)}, bf16[4,48,384]{2,1,0:T(8,128)(2,1)S(1)}, u32[]{:S(2)}, u32[]{:S(2)}) %collective-permute-start) | collective-permute-done | bytes 147488 | tf_op jit(solution)/shard_map/ppermute | solution.py:952
  39.4 4.2 %collective-permute-done.9 = f32[8,1152]{1,0:T(8,128)S(1)} collective-permute-done((f32[8,1152]{1,0:T(8,128)S(1)}, f32[8,1152]{1,0:T(8,128)S(1)}, u32[]{:S(2)}, u32[]{:S(2)}) %collective-permute-start.9) | collective-permute-done | bytes 36896 | tf_op jit(solution)/shard_map/ppermute | solution.py:952
  43.6 18.1 %all_gather.6 = bf16[256,896]{1,0:T(8,128)(2,1)} all-gather(bf16[32,896]{1,0:T(8,128)(2,1)S(1)} %slice_bitcast_fusion), channel_id=1, replica_groups=mesh['dp'=8,'mod'=4] {'dp'}, dimensions={0}, use_global_device_ids=true | all-gather | bytes 516096 | tf_op jit(solution)/shard_map/all_gather | solution.py:1047
  90.6 7.3 %qkv_first.1 = (bf16[1024,768]{1,0:T(8,128)(2,1)}, bf16[1024,1152]{1,0:T(8,128)(2,1)}) custom-call(s32[3]{0:T(128)} %pad_add_fusion.idx_ref, bf16[1024,768]{1,0:T(8,128)(2,1)} %bitcast.127, f32[6,8,768]{2,1,0:T(8,128)} %fusion.18.mod_ref, f32[1,1152]{1,0:T(1,128)} %bitcast.183, bf16[2,4,4,48,384]{4,3,2,1,0:T(8,128)(2,1)} %get-tuple-element.147.own, ...), custom_call_target="tpu_custom_call" | custom-call | flops 1 | bytes 1 | tf_op jit(solution)/shard_map/qkv_first/pallas_call | solution.py:232
  97.9 14.1 %attend.2 = (bf16[1024,384]{1,0:T(8,128)(2,1)}, bf16[2,6,512,512]{3,2,1,0:T(8,128)(2,1)}) custom-call(s32[2]{0:T(128)} %bitcast.187, s32[2,4]{1,0:T(2,128)} %bitcast.176, bf16[1024,1152]{1,0:T(8,128)(2,1)} %get-tuple-element.153.q_ref.k_ref.v_ref, bf16[1024,1152]{1,0:T(8,128)(2,1)} %get-tuple-element.153.q_ref.k_ref.v_ref, ...), custom_call_target="tpu_custom_call" | custom-call | flops 1 | bytes 1 | tf_op jit(solution)/shard_map/attend/pallas_call | solution.py:335
  113.2 6.2 %qkv_second.1.q_ref.k_ref.v_ref = bf16[1024,1152]{1,0:T(8,128)(2,1)} custom-call(s32[3]{0:T(128)} %pad_add_fusion.idx_ref, bf16[1024,768]{1,0:T(8,128)(2,1)} %get-tuple-element.156.a_ref, f32[1,1152]{1,0:T(1,128)} %bitcast.182, bf16[2,4,4,48,384]{4,3,2,1,0:T(8,128)(2,1)} %get-tuple-element.147.own, bf16[4,3,4,48,384]{4,3,2,1,0:T(8,128)(2,1)} %copy-done.4), custom_call_target="tpu_custom_call" | custom-call | flops 1 | bytes 1 | tf_op jit(solution)/shard_map/qkv_second/pallas_call | solution.py:269
  120.1 14.1 %attend.3 = (bf16[1024,384]{1,0:T(8,128)(2,1)}, bf16[2,6,512,512]{3,2,1,0:T(8,128)(2,1)}) custom-call(s32[2]{0:T(128)} %bitcast.188, s32[2,4]{1,0:T(2,128)} %bitcast.177, bf16[1024,1152]{1,0:T(8,128)(2,1)} %qkv_second.1.q_ref.k_ref.v_ref, bf16[1024,1152]{1,0:T(8,128)(2,1)} %qkv_second.1.q_ref.k_ref.v_ref, bf16[1024,1152]{1,0:T(8,128)(2,1)} %qkv_second.1.q_ref.k_ref.v_ref, ...), custom_call_target="tpu_custom_call" | custom-call | flops 1 | bytes 1 | tf_op jit(solution)/shard_map/attend/pallas_call | solution.py:335
  139.8 8.9 %middle.1 = (f32[1024,768]{1,0:T(8,128)}, bf16[1024,768]{1,0:T(8,128)(2,1)}, bf16[1024,768]{1,0:T(8,128)(2,1)}, bf16[1024,768]{1,0:T(8,128)(2,1)}, f32[8,768]{1,0:T(8,128)}) custom-call(s32[3]{0:T(128)} %pad_add_fusion.idx_ref, bf16[1024,384]{1,0:T(8,128)(2,1)} %get-tuple-element.155.o1_ref.o_ref, bf16[1024,384]{1,0:T(8,128)(2,1)} %get-tuple-element.160.o2_ref.o_ref, ...), custom_call_target="tpu_custom_call" | custom-call | flops 30000001024 | bytes 1000000 | tf_op jit(solution)/shard_map/middle/pallas_call | solution.py:404
  148.8 10.5 %collective-permute-done.16 = bf16[3,8,48,384]{3,2,1,0:T(8,128)(2,1)S(1)} collective-permute-done((bf16[3,8,48,384]{3,2,1,0:T(8,128)(2,1)S(1)}, bf16[3,8,48,384]{3,2,1,0:T(8,128)(2,1)S(1)}, u32[]{:S(2)}, u32[]{:S(2)}) %collective-permute-start.16) | collective-permute-done | bytes 884768 | tf_op jit(solution)/shard_map/ppermute | solution.py:947
  172.4 22.5 %mlp.2 = (f32[1024,768]{1,0:T(8,128)}, f32[1024,768]{1,0:T(8,128)}, bf16[768,1536]{1,0:T(8,128)(2,1)}, bf16[1536,768]{1,0:T(8,128)(2,1)}, f32[8,1536]{1,0:T(8,128)}) custom-call(s32[3]{0:T(128)} %pad_add_fusion.idx_ref, bf16[1024,768]{1,0:T(8,128)(2,1)} %get-tuple-element.168.m_ref, bf16[1024,768]{1,0:T(8,128)(2,1)} %get-tuple-element.169.dmlp_ref, ...), custom_call_target="tpu_custom_call" | custom-call | flops 30000001024 | bytes 1000000 | tf_op jit(solution)/shard_map/mlp/pallas_call | solution.py:514
  199.1 24.7 %mlp.3 = (f32[1024,768]{1,0:T(8,128)}, f32[1024,768]{1,0:T(8,128)}, bf16[768,1536]{1,0:T(8,128)(2,1)}, bf16[1536,768]{1,0:T(8,128)(2,1)}, f32[8,1536]{1,0:T(8,128)}) custom-call(s32[3]{0:T(128)} %pad_add_fusion.idx_ref, bf16[1024,768]{1,0:T(8,128)(2,1)} %get-tuple-element.168.m_ref, bf16[1024,768]{1,0:T(8,128)(2,1)} %get-tuple-element.169.dmlp_ref, ...), custom_call_target="tpu_custom_call" | custom-call | flops 30000001024 | bytes 1000000 | tf_op jit(solution)/shard_map/mlp/pallas_call | solution.py:514
  223.9 4.2 %collective-permute-done.25 = bf16[3,6,48,384]{3,2,1,0:T(8,128)(2,1)S(1)} collective-permute-done((bf16[3,6,48,384]{3,2,1,0:T(8,128)(2,1)S(1)}, bf16[3,6,48,384]{3,2,1,0:T(8,128)(2,1)S(1)}, u32[]{:S(2)}, u32[]{:S(2)}) %collective-permute-start.25) | collective-permute-done | bytes 663584 | tf_op jit(solution)/shard_map/ppermute | solution.py:947
  236.6 14.4 %back_middle.1 = (bf16[1024,768]{1,0:T(8,128)(2,1)}, f32[1024,768]{1,0:T(8,128)}, bf16[1024,384]{1,0:T(8,128)(2,1)}, bf16[1024,384]{1,0:T(8,128)(2,1)}, bf16[768...) custom-call(s32[3]{0:T(128)} %pad_add_fusion.idx_ref, ...), custom_call_target="tpu_custom_call" | custom-call | flops 30000001024 | bytes 1000000 | tf_op jit(solution)/shard_map/back_middle/pallas_call | solution.py:613
  251.0 13.4 %attend_back.2 = (bf16[1024,384]{1,0:T(8,128)(2,1)}, bf16[1024,384]{1,0:T(8,128)(2,1)}, bf16[1024,384]{1,0:T(8,128)(2,1)}, f32[3,8,1024]{2,1,0:T(8,128)}, f32[8,384]{1,0:T(8,128)}) custom-call(bf16[1024,1152]{1,0:T(8,128)(2,1)} %get-tuple-element.153.q_ref.k_ref.v_ref, bf16[1024,1152]{1,0:T(8,128)(2,1)} %get-tuple-element.153.q_ref.k_ref.v_ref, ...), custom_call_target="tpu_custom_call" | custom-call | flops 1 | bytes 1 | tf_op jit(solution)/shard_map/attend_back/pallas_call | solution.py:702
  264.4 5.9 %qkv_weight.2 = bf16[768,1152]{1,0:T(8,128)(2,1)} custom-call(bf16[1024,768]{1,0:T(8,128)(2,1)} %get-tuple-element.156.a_ref, bf16[1024,384]{1,0:T(8,128)(2,1)} %get-tuple-element.200.dq_ref.dq1, bf16[1024,384]{1,0:T(8,128)(2,1)} %get-tuple-element.201.dk_ref.dk1, bf16[1024,384]{1,0:T(8,128)(2,1)} %get-tuple-element.202.dv_ref.dv1), custom_call_target="tpu_custom_call" | custom-call | flops 1 | bytes 1 | tf_op jit(solution)/shard_map/qkv_weight/pallas_call | solution.py:732
  281.4 13.5 %attend_back.3 = (bf16[1024,384]{1,0:T(8,128)(2,1)}, bf16[1024,384]{1,0:T(8,128)(2,1)}, bf16[1024,384]{1,0:T(8,128)(2,1)}, f32[3,8,1024]{2,1,0:T(8,128)}, f32[8,384]{1,0:T(8,128)}) custom-call(bf16[1024,1152]{1,0:T(8,128)(2,1)} %qkv_second.1.q_ref.k_ref.v_ref, bf16[1024,1152]{1,0:T(8,128)(2,1)} %qkv_second.1.q_ref.k_ref.v_ref, ...), custom_call_target="tpu_custom_call" | custom-call | flops 30000001024 | bytes 1000000 | tf_op jit(solution)/shard_map/attend_back/pallas_call | solution.py:702
  298.5 5.9 %qkv_weight.3 = bf16[768,1152]{1,0:T(8,128)(2,1)} custom-call(bf16[1024,768]{1,0:T(8,128)(2,1)} %get-tuple-element.156.a_ref, bf16[1024,384]{1,0:T(8,128)(2,1)} %get-tuple-element.219.dq_ref.dq2, bf16[1024,384]{1,0:T(8,128)(2,1)} %get-tuple-element.220.dk_ref.dk2, bf16[1024,384]{1,0:T(8,128)(2,1)} %get-tuple-element.221.dv_ref.dv2), custom_call_target="tpu_custom_call" | custom-call | flops 30000001024 | bytes 1000000 | tf_op jit(solution)/shard_map/qkv_weight/pallas_call | solution.py:732
  321.8 11.6 %back_entry.1 = (bf16[1024,768]{1,0:T(8,128)(2,1)}, f32[2,8,768]{2,1,0:T(8,128)}) custom-call(s32[3]{0:T(128)} %pad_add_fusion.idx_ref, bf16[1024,384]{1,0:T(8,128)(2,1)} %get-tuple-element.200.dq_ref.dq1, bf16[1024,384]{1,0:T(8,128)(2,1)} %get-tuple-element.201.dk_ref.dk1, bf16[1024,384]{1,0:T(8,128)(2,1)} %get-tuple-element.202.dv_ref.dv1, ...), custom_call_target="tpu_custom_call" | custom-call | flops 1 | bytes 1 | tf_op jit(solution)/shard_map/back_entry/pallas_call | solution.py:774
  333.4 7.5 %back_cond.1 = f32[4,8,1920]{2,1,0:T(8,128)} custom-call(s32[3]{0:T(128)} %pad_add_fusion.idx_ref, s32[2]{0:T(128)} %bitcast.189, s32[2,4]{1,0:T(2,128)} %bitcast.178, f32[6,8,768]{2,1,0:T(8,128)} %get-tuple-element.233.mid_ref, f32[2,8,768]{2,1,0:T(8,128)} %get-tuple-element.236.entry_ref, f32[8,768]{1,0:T(8,128)} %get-tuple-element.301.slope_ref, ...), custom_call_target="tpu_custom_call" | custom-call | flops 1 | bytes 1 | tf_op jit(solution)/shard_map/back_cond/pallas_call | solution.py:869
  349.3 4.9 %collective-permute-done.54 = bf16[192,768]{1,0:T(8,128)(2,1)S(1)} collective-permute-done((bf16[192,768]{1,0:T(8,128)(2,1)S(1)}, bf16[192,768]{1,0:T(8,128)(2,1)S(1)}, u32[]{:S(2)}, u32[]{:S(2)}) %collective-permute-start.54) | collective-permute-done | bytes 294944 | tf_op jit(solution)/shard_map/ppermute | solution.py:947
  354.2 5.5 %collective-permute-start.42 = (bf16[8,1920]{1,0:T(8,128)(2,1)S(1)}, bf16[8,1920]{1,0:T(8,128)(2,1)S(1)}, u32[]{:S(2)}, u32[]{:S(2)}) collective-permute-start(bf16[8,1920]{1,0:T(8,128)(2,1)S(1)} %get-tuple-element.292), channel_id=1, source_target_pairs={{0,1},{1,2},{2,3},{3,0},{4,5},{5,6},{6,7},{7,4},{8,9},{9,10},{10,1... | collective-permute-start | bytes 92168 | tf_op jit(solution)/shard_map/ppermute | solution.py:952
  373.8 10.2 %all_gather.7 = bf16[256,1920]{1,0:T(8,128)(2,1)S(1)} all-gather(bf16[32,1920]{1,0:T(8,128)(2,1)S(1)} %pad_maximum_fusion.14), channel_id=1, replica_groups=mesh['dp'=8,'mod'=4] {'dp'}, dimensions={0}, use_global_device_ids=true | all-gather | bytes 1105920 | tf_op jit(solution)/shard_map/all_gather | solution.py:1183
  404.7 4.2 %finish_ff.1 = (f32[192,3072]{1,0:T(8,128)}, f32[768,768]{1,0:T(8,128)}) custom-call(s32[3]{0:T(128)} %pad_add_fusion.idx_ref, bf16[4,192,768]{2,1,0:T(8,128)(2,1)} %pad_maximum_fusion.4.mine_ref, bf16[4,192,768]{2,1,0:T(8,128)(2,1)} %collective-permute-done.55.peer_ref), custom_call_target="tpu_custom_call" | custom-call | flops 1 | bytes 1 | tf_op jit(solution)/shard_map/finish_ff/pallas_call | solution.py:903
  (303 shorter events, 164.2 us)
Async XLA Ops:
  35.0 27.7 %collective-permute-start.6 = (bf16[3,4,48,384]{3,2,1,0:T(8,128)(2,1)S(1)}, bf16[3,4,48,384]{3,2,1,0:T(8,128)(2,1)S(1)}, u32[]{:S(2)}, u32[]{:S(2)}) collective-permute-start(bf16[3,4,48,384]{3,2,1,0:T(8,128)(2,1)S(1)} %pad_maximum_fusion.12), channel_id=1, source_target_pairs={{0,8},{4,12},{8,0},{12,4},{16,24},{20,28},{24,16},{28,20},{1,9},{5... | collective-permute-start | bytes 1327112 | tf_op jit(solution)/shard_map/ppermute | solution.py:947
  36.6 29.9 %collective-permute-start.7 = (bf16[3,4,48,384]{3,2,1,0:T(8,128)(2,1)S(1)}, bf16[3,4,48,384]{3,2,1,0:T(8,128)(2,1)S(1)}, u32[]{:S(2)}, u32[]{:S(2)}) collective-permute-start(bf16[3,4,48,384]{3,2,1,0:T(8,128)(2,1)S(1)} %pad_maximum_fusion.12), channel_id=1, source_target_pairs={{0,16},{4,20},{8,24},{12,28},{16,0},{20,4},{24,8},{28,12},{1,17},{... | collective-permute-start | bytes 1327112 | tf_op jit(solution)/shard_map/ppermute | solution.py:947
  38.1 28.4 %collective-permute-start.8 = (bf16[3,4,48,384]{3,2,1,0:T(8,128)(2,1)S(1)}, bf16[3,4,48,384]{3,2,1,0:T(8,128)(2,1)S(1)}, u32[]{:S(2)}, u32[]{:S(2)}) collective-permute-start(bf16[3,4,48,384]{3,2,1,0:T(8,128)(2,1)S(1)} %pad_maximum_fusion.12), channel_id=1, source_target_pairs={{0,24},{4,28},{8,16},{12,20},{16,8},{20,12},{24,0},{28,4},{1,25},{... | collective-permute-start | bytes 1327112 | tf_op jit(solution)/shard_map/ppermute | solution.py:947
  62.4 71.8 %collective-permute-start.13 = (bf16[2,8,48,384]{3,2,1,0:T(8,128)(2,1)}, bf16[2,8,48,384]{3,2,1,0:T(8,128)(2,1)}, u32[]{:S(2)}, u32[]{:S(2)}) collective-permute-start(bf16[2,8,48,384]{3,2,1,0:T(8,128)(2,1)} %get-tuple-element.159), channel_id=1, source_target_pairs={{0,1},{1,2},{2,3},{3,0},{4,5},{5,6},{6,7},{7,4},{8,9},{9,10},{10,1... | collective-permute-start | bytes 1769480 | tf_op jit(solution)/shard_map/ppermute | solution.py:952
  62.4 71.8 %collective-permute-start.14 = (bf16[2,8,48,384]{3,2,1,0:T(8,128)(2,1)}, bf16[2,8,48,384]{3,2,1,0:T(8,128)(2,1)}, u32[]{:S(2)}, u32[]{:S(2)}) collective-permute-start(bf16[2,8,48,384]{3,2,1,0:T(8,128)(2,1)} %get-tuple-element.159), channel_id=1, source_target_pairs={{0,2},{1,3},{2,0},{3,1},{4,6},{5,7},{6,4},{7,5},{8,10},{9,11},{10,... | collective-permute-start | bytes 1769480 | tf_op jit(solution)/shard_map/ppermute | solution.py:952
  62.7 71.5 %collective-permute-start.15 = (bf16[2,8,48,384]{3,2,1,0:T(8,128)(2,1)}, bf16[2,8,48,384]{3,2,1,0:T(8,128)(2,1)}, u32[]{:S(2)}, u32[]{:S(2)}) collective-permute-start(bf16[2,8,48,384]{3,2,1,0:T(8,128)(2,1)} %get-tuple-element.159), channel_id=1, source_target_pairs={{0,3},{1,0},{2,1},{3,2},{4,7},{5,4},{6,5},{7,6},{8,11},{9,8},{10,9... | collective-permute-start | bytes 1769480 | tf_op jit(solution)/shard_map/ppermute | solution.py:952
  66.8 45.2 %collective-permute-start.12 = (bf16[4,3,4,48,384]{4,3,2,1,0:T(8,128)(2,1)S(1)}, bf16[4,3,4,48,384]{4,3,2,1,0:T(8,128)(2,1)S(1)}, u32[]{:S(2)}, u32[]{:S(2)}) collective-permute-start(bf16[4,3,4,48,384]{4,3,2,1,0:T(8,128)(2,1)S(1)} %pad_maximum_fusion.2.fetched), channel_id=1, source_target_pairs={{0,4},{4,0},{8,12},{12,8},{16,20},{20,16},{24,28},{28,24},{1,5},{5... | collective-permute-start | bytes 5308424 | tf_op jit(solution)/shard_map/ppermute | solution.py:947
  160.0 35.5 %collective-permute-start.18 = (bf16[4,3,8,48,384]{4,3,2,1,0:T(8,128)(2,1)S(1)}, bf16[4,3,8,48,384]{4,3,2,1,0:T(8,128)(2,1)}, u32[]{:S(2)}, u32[]{:S(2)}) collective-permute-start(bf16[4,3,8,48,384]{4,3,2,1,0:T(8,128)(2,1)S(1)} %pad_maximum_fusion.fetched), channel_id=1, source_target_pairs={{0,4},{4,0},{8,12},{12,8},{16,20},{20,16},{24,28},{28,24},{1,5},{5... | collective-permute-start | bytes 10616840 | tf_op jit(solution)/shard_map/ppermute | solution.py:947
  167.3 27.6 %collective-permute-start.19 = (bf16[6,48,384]{2,1,0:T(8,128)(2,1)}, bf16[6,48,384]{2,1,0:T(8,128)(2,1)S(1)}, u32[]{:S(2)}, u32[]{:S(2)}) collective-permute-start(bf16[6,48,384]{2,1,0:T(8,128)(2,1)} %get-tuple-element.177), channel_id=1, source_target_pairs={{0,1},{1,2},{2,3},{3,0},{4,5},{5,6},{6,7},{7,4},{8,9},{9,10},{10,1... | collective-permute-start | bytes 663560 | tf_op jit(solution)/shard_map/ppermute | solution.py:952
  167.8 27.6 %collective-permute-start.20 = (bf16[6,48,384]{2,1,0:T(8,128)(2,1)}, bf16[6,48,384]{2,1,0:T(8,128)(2,1)S(1)}, u32[]{:S(2)}, u32[]{:S(2)}) collective-permute-start(bf16[6,48,384]{2,1,0:T(8,128)(2,1)} %get-tuple-element.177), channel_id=1, source_target_pairs={{0,2},{1,3},{2,0},{3,1},{4,6},{5,7},{6,4},{7,5},{8,10},{9,11},{10,... | collective-permute-start | bytes 663560 | tf_op jit(solution)/shard_map/ppermute | solution.py:952
  169.3 26.2 %collective-permute-start.21 = (bf16[6,48,384]{2,1,0:T(8,128)(2,1)}, bf16[6,48,384]{2,1,0:T(8,128)(2,1)S(1)}, u32[]{:S(2)}, u32[]{:S(2)}) collective-permute-start(bf16[6,48,384]{2,1,0:T(8,128)(2,1)} %get-tuple-element.177), channel_id=1, source_target_pairs={{0,3},{1,0},{2,1},{3,2},{4,7},{5,4},{6,5},{7,6},{8,11},{9,8},{10,9... | collective-permute-start | bytes 663560 | tf_op jit(solution)/shard_map/ppermute | solution.py:952
  194.9 29.0 %collective-permute-start.22 = (bf16[768,1536]{1,0:T(8,128)(2,1)}, bf16[768,1536]{1,0:T(8,128)(2,1)S(1)}, u32[]{:S(2)}, u32[]{:S(2)}) collective-permute-start(bf16[768,1536]{1,0:T(8,128)(2,1)} %get-tuple-element.184), channel_id=1, source_target_pairs={{0,4},{4,0},{8,12},{12,8},{16,20},{20,16},{24,28},{28,24},{1,5},{5... | collective-permute-start | bytes 7077896 | tf_op jit(solution)/shard_map/ppermute | solution.py:947
  195.0 28.9 %collective-permute-start.23 = (bf16[1536,768]{1,0:T(8,128)(2,1)}, bf16[1536,768]{1,0:T(8,128)(2,1)}, u32[]{:S(2)}, u32[]{:S(2)}) collective-permute-start(bf16[1536,768]{1,0:T(8,128)(2,1)} %get-tuple-element.185), channel_id=1, source_target_pairs={{0,4},{4,0},{8,12},{12,8},{16,20},{20,16},{24,28},{28,24},{1,5},{5... | collective-permute-start | bytes 7077896 | tf_op jit(solution)/shard_map/ppermute | solution.py:947
  195.6 28.3 %collective-permute-start.24 = (bf16[3,6,48,384]{3,2,1,0:T(8,128)(2,1)S(1)}, bf16[3,6,48,384]{3,2,1,0:T(8,128)(2,1)S(1)}, u32[]{:S(2)}, u32[]{:S(2)}) collective-permute-start(bf16[3,6,48,384]{3,2,1,0:T(8,128)(2,1)S(1)} %pad_maximum_fusion.7), channel_id=1, source_target_pairs={{0,8},{4,12},{8,0},{12,4},{16,24},{20,28},{24,16},{28,20},{1,9},{5... | collective-permute-start | bytes 1990664 | tf_op jit(solution)/shard_map/ppermute | solution.py:947
  197.3 30.8 %collective-permute-start.25 = (bf16[3,6,48,384]{3,2,1,0:T(8,128)(2,1)S(1)}, bf16[3,6,48,384]{3,2,1,0:T(8,128)(2,1)S(1)}, u32[]{:S(2)}, u32[]{:S(2)}) collective-permute-start(bf16[3,6,48,384]{3,2,1,0:T(8,128)(2,1)S(1)} %pad_maximum_fusion.7), channel_id=1, source_target_pairs={{0,16},{4,20},{8,24},{12,28},{16,0},{20,4},{24,8},{28,12},{1,17},{... | collective-permute-start | bytes 1990664 | tf_op jit(solution)/shard_map/ppermute | solution.py:947
  197.6 30.5 %collective-permute-start.26 = (bf16[3,6,48,384]{3,2,1,0:T(8,128)(2,1)S(1)}, bf16[3,6,48,384]{3,2,1,0:T(8,128)(2,1)S(1)}, u32[]{:S(2)}, u32[]{:S(2)}) collective-permute-start(bf16[3,6,48,384]{3,2,1,0:T(8,128)(2,1)S(1)} %pad_maximum_fusion.7), channel_id=1, source_target_pairs={{0,24},{4,28},{8,16},{12,20},{16,8},{20,12},{24,0},{28,4},{1,25},{... | collective-permute-start | bytes 1990664 | tf_op jit(solution)/shard_map/ppermute | solution.py:947
  231.9 40.3 %collective-permute-start.27 = (bf16[4,96,1536]{2,1,0:T(8,128)(2,1)}, bf16[4,96,1536]{2,1,0:T(8,128)(2,1)S(1)}, u32[]{:S(2)}, u32[]{:S(2)}) collective-permute-start(bf16[4,96,1536]{2,1,0:T(8,128)(2,1)} %add_convert_fusion.1), channel_id=1, source_target_pairs={{0,8},{4,12},{8,0},{12,4},{16,24},{20,28},{24,16},{28,20},{1,9},{5... | collective-permute-start | bytes 3538952 | tf_op jit(solution)/shard_map/ppermute | solution.py:947
  234.9 37.3 %collective-permute-start.28 = (bf16[4,192,768]{2,1,0:T(8,128)(2,1)}, bf16[4,192,768]{2,1,0:T(8,128)(2,1)S(1)}, u32[]{:S(2)}, u32[]{:S(2)}) collective-permute-start(bf16[4,192,768]{2,1,0:T(8,128)(2,1)} %add_convert_fusion), channel_id=1, source_target_pairs={{0,16},{4,20},{8,24},{12,28},{16,0},{20,4},{24,8},{28,12},{1,17},{... | collective-permute-start | bytes 3538952 | tf_op jit(solution)/shard_map/ppermute | solution.py:947
  250.9 44.0 %collective-permute-start.33 = (bf16[768,384]{1,0:T(8,128)(2,1)}, bf16[768,384]{1,0:T(8,128)(2,1)}, u32[]{:S(2)}, u32[]{:S(2)}) collective-permute-start(bf16[768,384]{1,0:T(8,128)(2,1)} %get-tuple-element.218), channel_id=1, source_target_pairs={{0,4},{4,0},{8,12},{12,8},{16,20},{20,16},{24,28},{28,24},{1,5},{5... | collective-permute-start | bytes 1769480 | tf_op jit(solution)/shard_map/ppermute | solution.py:947
  310.1 31.8 %collective-permute-start.36 = (bf16[4,96,768]{2,1,0:T(8,128)(2,1)S(1)}, bf16[4,96,768]{2,1,0:T(8,128)(2,1)S(1)}, u32[]{:S(2)}, u32[]{:S(2)}) collective-permute-start(bf16[4,96,768]{2,1,0:T(8,128)(2,1)S(1)} %pad_maximum_fusion.10), channel_id=1, source_target_pairs={{0,16},{4,20},{8,24},{12,28},{16,0},{20,4},{24,8},{28,12},{1,17},{... | collective-permute-start | bytes 1769480 | tf_op jit(solution)/shard_map/ppermute | solution.py:947
  316.3 25.6 %collective-permute-start.35 = (bf16[4,104,768]{2,1,0:T(8,128)(2,1)S(1)}, bf16[4,104,768]{2,1,0:T(8,128)(2,1)S(1)}, u32[]{:S(2)}, u32[]{:S(2)}) collective-permute-start(bf16[4,104,768]{2,1,0:T(8,128)(2,1)S(1)} %pad_maximum_fusion.8), channel_id=1, source_target_pairs={{0,8},{4,12},{8,0},{12,4},{16,24},{20,28},{24,16},{28,20},{1,9},{5... | collective-permute-start | bytes 1916936 | tf_op jit(solution)/shard_map/ppermute | solution.py:947
  317.5 24.3 %collective-permute-start.37 = (bf16[192,768]{1,0:T(8,128)(2,1)S(1)}, bf16[192,768]{1,0:T(8,128)(2,1)}, u32[]{:S(2)}, u32[]{:S(2)}) collective-permute-start(bf16[192,768]{1,0:T(8,128)(2,1)S(1)} %get-tuple-element.271), channel_id=1, source_target_pairs={{0,1},{1,2},{2,3},{3,0},{4,5},{5,6},{6,7},{7,4},{8,9},{9,10},{10,1... | collective-permute-start | bytes 884744 | tf_op jit(solution)/shard_map/ppermute | solution.py:952
  317.6 24.3 %collective-permute-start.38 = (bf16[192,768]{1,0:T(8,128)(2,1)S(1)}, bf16[192,768]{1,0:T(8,128)(2,1)}, u32[]{:S(2)}, u32[]{:S(2)}) collective-permute-start(bf16[192,768]{1,0:T(8,128)(2,1)S(1)} %get-tuple-element.270), channel_id=1, source_target_pairs={{0,2},{1,3},{2,0},{3,1},{4,6},{5,7},{6,4},{7,5},{8,10},{9,11},{10,... | collective-permute-start | bytes 884744 | tf_op jit(solution)/shard_map/ppermute | solution.py:952
  368.0 36.7 %collective-permute-start.55 = (bf16[4,192,768]{2,1,0:T(8,128)(2,1)}, bf16[4,192,768]{2,1,0:T(8,128)(2,1)}, u32[]{:S(2)}, u32[]{:S(2)}) collective-permute-start(bf16[4,192,768]{2,1,0:T(8,128)(2,1)} %pad_maximum_fusion.4.mine_ref), channel_id=1, source_target_pairs={{0,4},{4,0},{8,12},{12,8},{16,20},{20,16},{24,28},{28,24},{1,5},{5... | collective-permute-start | bytes 3538952 | tf_op jit(solution)/shard_map/ppermute | solution.py:947
  (68 other events, 731.6 us)

commit v3 on v2

--- a/solution.py
+++ b/solution.py
@@ -84,27 +84,66 @@
             )
 
 
-def pick_entry_body(idx_ref, w_ref, proj_ref, own_ref, piece_ref):
-    spot, core = idx_ref[1], idx_ref[2]
+def pick_entry_body(idx_ref, step_ref, label_ref, w_ref, proj_ref, cond_ref, bias_ref, rel_ref, own_ref, out_ref):
+    me, spot, core = idx_ref[0], idx_ref[1], idx_ref[2]
     for n, half in enumerate((1 - core, core)):
         for u in range(3):
             column = pl.multiple_of((2 * u + half) * HALF, HALF)
             own_ref[n, u] = w_ref[:, pl.ds(column, HALF)].reshape(4, UR, HALF)
         own_ref[n, 3] = proj_ref[:, pl.ds(pl.multiple_of(half * HALF, HALF), HALF)].reshape(4, UR, HALF)
-    for u in range(4):
-        piece_ref[u] = own_ref[0, u, spot]
-
-
-def pick_entry(idx, w, proj):
+    for n, q in enumerate((spot, lax.bitwise_xor(spot, 3))):
+        for u in range(4):
+            out_ref[4 * n + u] = own_ref[0, u, q]
+    slots = MICRO * NSEG
+    cond = cond_ref[...]
+    act = cond / (1.0 + jnp.exp(-cond))
+    row = lax.broadcasted_iota(jnp.int32, (slots, HALF), 0)
+    lane = lax.broadcasted_iota(jnp.int32, (slots, HALF), 1)
+    digits = jnp.zeros((slots, HALF), jnp.int32)
+    for n in range(slots):
+        step, label = step_ref[n // NSEG, n % NSEG], label_ref[n // NSEG, n % NSEG]
+        values = (step // 32, step % 32, label // 32, label % 32)
+        for m, value in enumerate(values):
+            digits = jnp.where((row == n) & (lane == m), value, digits)
+    rel = rel_ref[...].astype(f32)
+    rel = jnp.concatenate([rel, jnp.zeros((3, 1), f32)], axis=1)
+    bias = bias_ref[...].astype(f32)
+    pair = jnp.broadcast_to(bias[3:4], (8, HALF))
+    lane = lax.broadcasted_iota(jnp.int32, (8, HALF), 1)
+    blank = jnp.zeros((8, HALF), f32)
+    proj_b = jnp.concatenate([jnp.where(lane < 192, pair, 0.0), blank], axis=1)
+    fc2_b = jnp.concatenate([jnp.where(lane < 192, 0.0, pair), blank], axis=1)
+    proj_b = pltpu.roll(proj_b, me * 192, 1)
+    fc2_b = pltpu.roll(fc2_b, lax.rem(me + 3, 4) * 192, 1)
+    out_ref[8] = jnp.concatenate(
+        [
+            act[:, :HALF],
+            act[:, HALF:],
+            digits.astype(f32),
+            rel[:, :HALF],
+            rel[:, HALF : 2 * HALF],
+            jnp.concatenate([rel[:, 2 * HALF :], jnp.zeros((3, 128), f32)], axis=1),
+            bias[0:3],
+            proj_b[0:1, :HALF],
+            proj_b[0:1, HALF:],
+            fc2_b[0:1, :HALF],
+            fc2_b[0:1, HALF:],
+            jnp.zeros((8, HALF), f32),
+        ],
+        axis=0,
+    ).astype(bf16)
+
+
+def pick_entry(idx, steps, labels, w, proj, cond, bias, rel):
     return pl.pallas_call(
         pick_entry_body,
-        in_specs=[SMEM, VMEM, VMEM],
+        in_specs=[SMEM, SMEM, SMEM, VMEM, VMEM, VMEM, VMEM, VMEM],
         out_specs=[VMEM, VMEM],
-        out_shape=[jax.ShapeDtypeStruct((2, 4, 4, UR, HALF), bf16), jax.ShapeDtypeStruct((4, UR, HALF), bf16)],
+        out_shape=[jax.ShapeDtypeStruct((2, 4, 4, UR, HALF), bf16), jax.ShapeDtypeStruct((9, UR, HALF), bf16)],
         compiler_params=params(),
         cost_estimate=SHORT,
         name="pick_entry",
-    )(idx, w, proj)
+    )(idx, steps, labels, w, proj, cond, bias, rel)
 
 
 def pick_ff_body(idx_ref, fc1_ref, fc2_ref, own1_ref, own2_ref, piece_ref):
@@ -191,8 +230,8 @@
 
 
 def ada_copies(idx_ref, own, half, sources, held):
-    return [(own.at[half, pl.ds(2 * c, 2)], held.at[idx_ref[0], c]) for c in range(3)] + [
-        (ref.at[pl.ds(2 * c, 2)], held.at[z, c, :, q]) for ref, z, q in quarters(idx_ref, sources) for c in range(3)
+    return [(own.at[half], held.at[:, idx_ref[0]])] + [
+        (ref, held.at[:, z, q]) for ref, z, q in quarters(idx_ref, sources)
     ]
 
 
@@ -205,6 +244,96 @@
 
 
 ENTRY_HELD = (3, 4, 4, UR, HALF)
+
+
+def columns_body(w_ref, b_ref, p0, p1, p2, p3, c0, c1, c2, c3, held, sems):
+    copies = bring([(p.at[8], held.at[k]) for k, p in enumerate((p0, p1, p2, p3))], sems)
+    go(copies)
+    ready(copies)
+    slots = MICRO * NSEG
+    units = [held[k].astype(f32) for k in range(4)]
+    act = jnp.concatenate(
+        [jnp.concatenate([u[:slots], u[slots : 2 * slots]], axis=1) for u in units], axis=0
+    ).astype(bf16)
+    out = dot(act, w_ref[...]) + b_ref[...].astype(f32)
+    for k, c in enumerate((c0, c1, c2, c3)):
+        c[...] = out[k * slots : (k + 1) * slots]
+
+
+def mod_columns(w, b, payloads):
+    return pl.pallas_call(
+        columns_body,
+        in_specs=[VMEM, VMEM] + [ANY] * 4,
+        out_specs=[VMEM] * 4,
+        out_shape=[jax.ShapeDtypeStruct((MICRO * NSEG, 3 * HALF), f32)] * 4,
+        scratch_shapes=[pltpu.VMEM((4, UR, HALF), bf16), pltpu.SemaphoreType.DMA((4,))],
+        compiler_params=params(),
+        cost_estimate=SHORT,
+        name="mod_columns",
+    )(w, b, *payloads)
+
+
+def prepare_body(idx_ref, long_ref, valid_ref, c0, c1, c2, c3, p0, p1, p2, p3,
+                 mod_ref, qb1, qb2, pb_ref, ub1, ub2, fb_ref, r1, r2, cols, held, rows, sems):
+    me, core = idx_ref[0], idx_ref[2]
+    copies = bring([(p.at[8], held.at[lax.rem(me + 4 - k, 4)]) for k, p in enumerate((p0, p1, p2, p3))], sems)
+    go(copies)
+    for k, c in enumerate((c0, c1, c2, c3)):
+        cols[lax.rem(me + k, 4)] = c[...]
+    ready(copies)
+    rows[...] = held[...].astype(f32)
+    slots = MICRO * NSEG
+    row = lax.broadcasted_iota(jnp.int32, (slots, 1), 0)
+    upper = row < NSEG
+    is_long = jnp.where(upper, long_ref[0], long_ref[1]) > 0
+    valid = jnp.zeros((slots, 1), f32)
+    for n in range(slots):
+        valid = jnp.where(row == n, valid_ref[n // NSEG, n % NSEG].astype(f32), valid)
+    for g in range(12):
+        value = cols[g // 3, :, (g % 3) * HALF : (g % 3 + 1) * HALF]
+        value = jnp.where(is_long, jnp.where(upper, value[0:1], value[NSEG : NSEG + 1]), value)
+        if (g // 2) % 3 == 2:
+            value = value * valid
+        mod_ref[g // 2, :, (g % 2) * HALF : (g % 2 + 1) * HALF] = value
+    for half, qb, ub, r in ((1 - core, qb1, ub1, r1), (core, qb2, ub2, r2)):
+        qb[:, :HALF] = rows[half, 33:34, :]
+        qb[:, HALF : 2 * HALF] = jnp.zeros((1, HALF), f32)
+        qb[:, 2 * HALF :] = rows[2 + half, 33:34, :]
+        for z in range(4):
+            ub[:, z * HALF : (z + 1) * HALF] = jnp.where(half > 0, rows[z, 35:36, :], rows[z, 34:35, :])
+        for n in range(6):
+            z, t, to = 2 * half + n // 3, n % 3, slice(n % 2, n % 2 + 1)
+            r[n // 2, to, :HALF] = rows[z, 24 + t : 25 + t, :]
+            r[n // 2, to, HALF : 2 * HALF] = rows[z, 27 + t : 28 + t, :]
+            r[n // 2, to, 2 * HALF :] = rows[z, 30 + t : 31 + t, :256]
+    for ref, at in ((pb_ref, 36), (fb_ref, 38)):
+        for n in range(2):
+            ref[:, n * HALF : (n + 1) * HALF] = (
+                rows[0, at + n : at + n + 1, :]
+                + rows[1, at + n : at + n + 1, :]
+                + rows[2, at + n : at + n + 1, :]
+                + rows[3, at + n : at + n + 1, :]
+            )
+
+
+def prepare(idx, long_flag, valid_seg, columns, payloads):
+    shapes = [(6, MICRO * NSEG, D), (1, 3 * HALF), (1, 3 * HALF), (1, D), (1, FH), (1, FH), (1, D),
+              (3, 2, 2 * L), (3, 2, 2 * L)]
+    return pl.pallas_call(
+        prepare_body,
+        in_specs=[SMEM] * 3 + [VMEM] * 4 + [ANY] * 4,
+        out_specs=[VMEM] * 9,
+        out_shape=[jax.ShapeDtypeStruct(shape, f32) for shape in shapes],
+        scratch_shapes=[
+            pltpu.VMEM((4, MICRO * NSEG, 3 * HALF), f32),
+            pltpu.VMEM((4, UR, HALF), bf16),
+            pltpu.VMEM((4, UR, HALF), f32),
+            pltpu.SemaphoreType.DMA((4,)),
+        ],
+        compiler_params=params(),
+        cost_estimate=SHORT,
+        name="prepare",
+    )(idx, long_flag, valid_seg, *columns, *payloads)
 
 
 def qkv_first_body(idx_ref, x_ref, mod_ref, b_ref, own, fetched, a_ref, qkv_ref, held, sems):
@@ -721,35 +850,42 @@
     )(qkv, qkv, qkv, p, dout, out)
 
 
-def qkv_weight_body(a_ref, dq_ref, dk_ref, dv_ref, out_ref):
+def qkv_weight_body(a_ref, dq_ref, dk_ref, dv_ref, proj_ref, out_ref):
     a = a_ref[...]
-    out_ref[:, 0:HALF] = dot(a, dq_ref[...], 0, 0).astype(bf16)
-    out_ref[:, HALF : 2 * HALF] = dot(a, dk_ref[...], 0, 0).astype(bf16)
-    out_ref[:, 2 * HALF : 3 * HALF] = dot(a, dv_ref[...], 0, 0).astype(bf16)
-
-
-def qkv_weight(a, dq, dk, dv, cost):
+    grads = jnp.concatenate([dq_ref[...], dk_ref[...]], axis=1)
+    out_ref[0] = dot(a, grads, 0, 0).astype(bf16)
+    out_ref[1, :, :HALF] = dot(a, dv_ref[...], 0, 0).astype(bf16)
+    out_ref[1, :, HALF:] = proj_ref[...]
+
+
+def qkv_weight(a, dq, dk, dv, proj, cost):
     return pl.pallas_call(
         qkv_weight_body,
-        out_shape=jax.ShapeDtypeStruct((D, 3 * HALF), bf16),
+        out_shape=jax.ShapeDtypeStruct((2, D, D), bf16),
         compiler_params=params(),
         cost_estimate=cost,
         name="qkv_weight",
-    )(a, dq, dk, dv)
-
-
-def back_entry_body(idx_ref, dq1, dk1, dv1, dq2, dk2, dv2, x_ref, dh_ref, mod_ref, own, fetched, peer,
-                    dx_ref, dmod_ref, held1, held2, sems):
+    )(a, dq, dk, dv, proj)
+
+
+def back_entry_body(idx_ref, long_ref, valid_ref, dq1, dk1, dv1, dq2, dk2, dv2, x_ref, dh_ref, mod_ref, mid_ref, cond_ref,
+                    own, fetched, peer, own_c, fetched_c, peer_c,
+                    dx_ref, out_ref, held1, held2, held3, held4, entry_ref, sems, sems_c):
     i = pl.program_id(0)
+    core = idx_ref[2]
+    copies_c = bring(
+        ada_copies(idx_ref, own_c, 0, stacked(fetched_c), held3) + ada_copies(idx_ref, own_c, 1, stacked(peer_c), held4),
+        sems_c,
+    )
 
     @pl.when(i == 0)
     def _():
         copies = bring(
-            entry_copies(idx_ref, own, 0, stacked(fetched), held1)
-            + entry_copies(idx_ref, own, 1, stacked(peer), held2),
+            entry_copies(idx_ref, own, 0, stacked(fetched), held1) + entry_copies(idx_ref, own, 1, stacked(peer), held2),
             sems,
         )
         go(copies)
+        go(copies_c)
         ready(copies)
 
     one = jnp.concatenate([dq1[...], dk1[...], dv1[...]], axis=1)
@@ -760,32 +896,89 @@
         at = pl.ds(i * NSEG + s, 1)
         piece = da[s * SEG : (s + 1) * SEG, :]
         norm, inverse = norm_of(x_ref[rows, :].astype(f32))
-        dmod_ref[0, at, :] = jnp.sum(piece, axis=0, keepdims=True)
-        dmod_ref[1, at, :] = jnp.sum(piece * norm, axis=0, keepdims=True)
+        entry_ref[0, at, :] = jnp.sum(piece, axis=0, keepdims=True)
+        entry_ref[1, at, :] = jnp.sum(piece * norm, axis=0, keepdims=True)
         dx_ref[rows, :] = (
             dh_ref[rows, :] + norm_back(piece * (1.0 + mod_ref[1, at, :]), norm, inverse)
         ).astype(bf16)
 
-
-def back_entry(idx, parts, x, dh, mods, own, near, peer):
+    @pl.when(i == MICRO - 1)
+    def _():
+        ready(copies_c)
+        slots = MICRO * NSEG
+        row = lax.broadcasted_iota(jnp.int32, (slots, 1), 0)
+        upper = row < NSEG
+        is_long = jnp.where(upper, long_ref[0], long_ref[1]) > 0
+        valid = jnp.zeros((slots, 1), f32)
+        for n in range(slots):
+            valid = jnp.where(row == n, valid_ref[n // NSEG, n % NSEG].astype(f32), valid)
+        lead = (row == 0) | (row == NSEG)
+        blocks = []
+        for j in range(6):
+            value = entry_ref[j] if j < 2 else mid_ref[j]
+            if j % 3 == 2:
+                value = value * valid
+            total = jnp.where(
+                upper,
+                jnp.sum(value[:NSEG], axis=0, keepdims=True),
+                jnp.sum(value[NSEG:], axis=0, keepdims=True),
+            )
+            value = jnp.where(is_long, jnp.where(lead, total, 0.0), value)
+            blocks += [value[:, :HALF], value[:, HALF:]]
+        low = [block.astype(bf16) for block in blocks]
+        sides = []
+        for held in (held3, held4):
+            grad = jnp.zeros((slots, HALF), f32)
+            for c in range(3):
+                for z in range(4):
+                    weight = jnp.concatenate([held[2 * c + n, z].reshape(192, HALF) for n in range(2)], axis=0)
+                    grad += dot(low[3 * z + c], weight, 1, 1)
+            sides.append(grad)
+        swapped = core > 0
+        d_act = jnp.concatenate(
+            [jnp.where(swapped, sides[0], sides[1]), jnp.where(swapped, sides[1], sides[0])], axis=1
+        )
+        cond = cond_ref[...]
+        sigma = 1.0 / (1.0 + jnp.exp(-cond))
+        d_cond = d_act * (sigma * (1.0 + cond * (1.0 - sigma)))
+        blank = jnp.zeros((slots, HALF), f32)
+        for z in range(4):
+            out_ref[z] = jnp.concatenate(
+                [
+                    jnp.concatenate(blocks[3 * z : 3 * z + 2], axis=1),
+                    jnp.concatenate([blocks[3 * z + 2], blank], axis=1),
+                    d_cond,
+                    jnp.zeros((slots, D), f32),
+                ],
+                axis=0,
+            ).astype(bf16)
+
+
+def back_entry(idx, long_flag, valid_seg, parts, x, dh, mods, mid, cond, own, near, peer, own_c, near_c, peer_c):
     row = lambda i: (i, 0)
     full = pl.BlockSpec((L, D), row)
     part = pl.BlockSpec((L, HALF), row)
+    slots = MICRO * NSEG
     return pl.pallas_call(
         back_entry_body,
         grid=(MICRO,),
-        in_specs=[SMEM] + [part] * 6 + [full, full, whole((6, MICRO * NSEG, D))] + [ANY] * 3,
-        out_specs=[full, whole((2, MICRO * NSEG, D))],
-        out_shape=[jax.ShapeDtypeStruct((T, D), bf16), jax.ShapeDtypeStruct((2, MICRO * NSEG, D), f32)],
+        in_specs=[SMEM] * 3 + [part] * 6 + [full, full, whole((6, slots, D)), whole((6, slots, D)), whole((slots, D))]
+        + [ANY] * 6,
+        out_specs=[full, whole((4, 4 * slots, D))],
+        out_shape=[jax.ShapeDtypeStruct((T, D), bf16), jax.ShapeDtypeStruct((4, 4 * slots, D), bf16)],
         scratch_shapes=[
             pltpu.VMEM(ENTRY_HELD, bf16),
             pltpu.VMEM(ENTRY_HELD, bf16),
+            pltpu.VMEM((6, 4, 4, UR, HALF), bf16),
+            pltpu.VMEM((6, 4, 4, UR, HALF), bf16),
+            pltpu.VMEM((2, slots, D), f32),
             pltpu.SemaphoreType.DMA((26,)),
+            pltpu.SemaphoreType.DMA((26,)),
         ],
         compiler_params=params("arbitrary"),
-        cost_estimate=SHORT,
+        cost_estimate=LONG,
         name="back_entry",
-    )(idx, *parts, x, dh, mods, own, near, peer)
+    )(idx, long_flag, valid_seg, *parts, x, dh, mods, mid, cond, own, near, peer, own_c, near_c, peer_c)
 
 
 def pack_small_body(idx_ref, q1, q2, proj_ref, u1, u2, fc2_ref, t1, t2, out_ref):
@@ -821,80 +1014,18 @@
     )(idx, *arrays)
 
 
-def back_cond_body(idx_ref, long_ref, valid_ref, mid_ref, entry_ref, slope_ref, own, fetched, peer,
-                   out_ref, held1, held2, sems):
-    copies = bring(
-        ada_copies(idx_ref, own, 0, stacked(fetched), held1)
-        + ada_copies(idx_ref, own, 1, stacked(peer), held2),
-        sems,
-    )
-    go(copies)
-    core = idx_ref[2]
-    slots = MICRO * NSEG
-    row = lax.broadcasted_iota(jnp.int32, (slots, 1), 0)
-    upper = row < NSEG
-    is_long = jnp.where(upper, long_ref[0], long_ref[1]) > 0
-    valid = jnp.zeros((slots, 1), f32)
-    for n in range(slots):
-        valid = jnp.where(row == n, valid_ref[n // NSEG, n % NSEG].astype(f32), valid)
-    lead = (row == 0) | (row == NSEG)
-    blocks = []
-    for j in range(6):
-        value = entry_ref[j] if j < 2 else mid_ref[j]
-        if j % 3 == 2:
-            value = value * valid
-        total = jnp.where(
-            upper,
-            jnp.sum(value[:NSEG], axis=0, keepdims=True),
-            jnp.sum(value[NSEG:], axis=0, keepdims=True),
-        )
-        value = jnp.where(is_long, jnp.where(lead, total, 0.0), value).astype(bf16)
-        blocks += [value[:, :HALF], value[:, HALF:]]
-    ready(copies)
-    for held, half in ((held1, 1 - core), (held2, core)):
-        grad = jnp.zeros((slots, HALF), f32)
-        for z in range(4):
-            for c in range(3):
-                grad += dot(blocks[3 * z + c], held[z, c].reshape(HALF, HALF), 1, 1)
-        at = pl.ds(pl.multiple_of(half * HALF, HALF), HALF)
-        out_ref[0, :, pl.ds(pl.multiple_of(3 * HALF + half * HALF, HALF), HALF)] = grad * slope_ref[:, at]
-    for z in range(4):
-        if z:
-            out_ref[z, :, 3 * HALF :] = out_ref[0, :, 3 * HALF :]
-        for c in range(3):
-            out_ref[z, :, c * HALF : (c + 1) * HALF] = blocks[3 * z + c].astype(f32)
-
-
-def back_cond(idx, long_flag, valid_seg, mid, entry, slope, own, near, peer):
-    return pl.pallas_call(
-        back_cond_body,
-        in_specs=[SMEM, SMEM, SMEM, VMEM, VMEM, VMEM] + [ANY] * 3,
-        out_specs=VMEM,
-        out_shape=jax.ShapeDtypeStruct((4, MICRO * NSEG, 5 * HALF), f32),
-        scratch_shapes=[
-            pltpu.VMEM((4, 3, 2, 4, UR, HALF), bf16),
-            pltpu.VMEM((4, 3, 2, 4, UR, HALF), bf16),
-            pltpu.SemaphoreType.DMA((78,)),
-        ],
-        compiler_params=params(),
-        cost_estimate=SHORT,
-        name="back_cond",
-    )(idx, long_flag, valid_seg, mid, entry, slope, own, near, peer)
-
-
 def finish_ff_body(idx_ref, mine_ref, peer_ref, fc1_ref, fc2_ref):
     spot, core = idx_ref[1], idx_ref[2]
     for source, half in ((mine_ref, core), (peer_ref, 1 - core)):
         for j in range(4):
             place_at = lax.bitwise_xor(spot, j)
-            low, high = lax.rem(place_at, 2), lax.div(place_at, 2)
-            row = pl.multiple_of((2 * low + high) * 48, 16)
+            row = pl.multiple_of(place_at * 48, 16)
             for z in range(4):
                 source_rows = pl.ds(48 * (z // 2), 48)
                 block = source[j, source_rows, (z % 2) * HALF : (z % 2 + 1) * HALF]
                 column = pl.multiple_of((2 * z + half) * HALF, 128)
                 fc1_ref[pl.ds(row, 48), pl.ds(column, HALF)] = block.astype(f32)
-            row = pl.multiple_of(half * HALF + (2 * high + low) * 96, 16)
+            row = pl.multiple_of(half * HALF + place_at * 96, 16)
             fc2_ref[pl.ds(row, 96), :] = source[j, 96:192, :].astype(f32)
 
 
@@ -917,12 +1048,9 @@
         column = half * HALF
         for j in range(4):
             place_at = lax.bitwise_xor(spot, j)
-            low, high = lax.rem(place_at, 2), lax.div(place_at, 2)
-            row0 = pl.multiple_of((2 * low + high) * 48, 16)
-            row1 = pl.multiple_of((2 * high + low) * 48, 16)
+            row = pl.multiple_of(place_at * 48, 16)
             for t in range(4):
                 block = source[j, 48 * (t // 2) : 48 * (t // 2 + 1), (t % 2) * HALF : (t % 2 + 1) * HALF].astype(f32)
-                row = row0 if t < 2 else row1
                 if t < 3:
                     qkv_ref[pl.ds(row, 48), pl.ds(pl.multiple_of(t * D + column, 128), HALF)] = block
                 else:
@@ -1017,187 +1145,163 @@
     core = lax.axis_index("dp") % 2
     spot = (lax.axis_index("dp") // 2) % 4
     idx = jnp.stack([me, spot, core]).astype(jnp.int32)
-    first = 1 - core
     slots_n = MICRO * NSEG
-
-    own_a, piece_a = pick_entry(idx, w_qkv, w_proj)
+    x = block_input.reshape(T, D)
+    dy = grad_out.reshape(T, D)
+    long_one = long_flag.reshape(MICRO)
+    valid_seg = valid_mask.reshape(MICRO, NSEG, SEG)[:, :, 0]
+
     step_flat = tsteps.reshape(slots_n)
     label_flat = labels.reshape(slots_n)
     cond = time_table[step_flat].astype(f32) + class_table[label_flat].astype(f32)
-    sigma = jax.nn.sigmoid(cond)
-    act = (cond * sigma).astype(bf16)
-    slope = sigma * (1.0 + cond * (1.0 - sigma))
-    digits = jnp.stack([step_flat // 32, step_flat % 32, label_flat // 32, label_flat % 32], axis=1).astype(bf16)
-    digits = jnp.pad(digits, ((0, 0), (0, 124)))
-    rel_shape = rel_table.shape
-    small = jnp.concatenate(
-        [qv_bias, proj_bias, fc1_bias, fc2_bias, jnp.pad(rel_table, ((0, 0), (0, 1))).reshape(-1)]
-    ).reshape(slots_n, -1)
-    packet = jnp.concatenate([act, digits, small], axis=1)
-    group = jnp.stack([packet] + [shift(packet, k) for k in range(1, mods_n)])
-    near_a = jnp.stack(around(piece_a))
-    group_act = group[:, :, :D].reshape(mods_n * slots_n, D)
-    columns = jnp.dot(group_act, w_ada, preferred_element_type=f32) + b_ada.astype(f32)
-    columns = columns.reshape(mods_n, slots_n, -1)
+    biases = jnp.concatenate([qv_bias, fc1_bias, proj_bias, fc2_bias]).reshape(4, HALF)
+    own_a, payload = pick_entry(
+        idx, tsteps.reshape(MICRO, NSEG), labels.reshape(MICRO, NSEG), w_qkv, w_proj, cond, biases, rel_table
+    )
+    payloads = [payload] + around(payload)
     own_1, own_2, piece_b = pick_ff(idx, w_fc1, w_fc2)
-    near_a, columns, piece_b, group = fence(near_a, columns, piece_b, group)
-    set_a = three(near_a)
+    own_c, piece_c = pick_ada(idx, w_ada)
+    piece_b, piece_c, payloads[0], *payloads[1:] = fence(piece_b, piece_c, *payloads)
+
+    def sides(got, also_x=None, also_y=None):
+        near = jnp.concatenate([g[0] for g in got])
+        units = near.shape[0]
+        outs = []
+        for bit, also in ((2, also_x), (4, also_y)):
+            outs.append(swap(near if also is None else jnp.concatenate([near, also]), bit))
+        return near, outs, jnp.concatenate([g[1] for g in got]), units
+
+    def assemble(near, outs, diag, units):
+        return jnp.stack([near, outs[0][:units], outs[1][:units], diag]).reshape(4, 3, units // 3, UR, HALF)
+
+    packets = jnp.stack([p[8] for p in payloads])
+    set_a = list(sides([p[:8].reshape(2, 4, UR, HALF) for p in payloads[1:]], packets, packets))
+    columns = mod_columns(w_ada, b_ada.reshape(1, -1), payloads)
+    back = [columns[0]] + [shift(columns[k], mods_n - k) for k in range(1, mods_n)]
     got_b = around(piece_b)
-    back = [columns[0]] + [shift(columns[k], mods_n - k) for k in range(1, mods_n)]
-    act_all = lax.all_gather(
-        group[:, :, : D + 128].reshape(mods_n * slots_n, D + 128), "dp", axis=0, tiled=True
-    )
-    act_all, *rest = fence(act_all, *set_a, *back)
-    set_a, back = jnp.stack(rest[:4]), rest[4:]
-    turn = (mods_n - me) % mods_n
-    modulation = lax.dynamic_slice_in_dim(jnp.stack(back + back), turn, mods_n, 0)
-    modulation = modulation.transpose(1, 0, 2).reshape(MICRO, NSEG, 6, D)
-    long_one = long_flag.reshape(MICRO)
-    is_long = long_one[:, None, None, None] > 0
-    seg_mod = jnp.where(is_long, modulation[:, :1], modulation)
-    valid_seg = valid_mask.reshape(MICRO, NSEG, SEG)[:, :, 0]
-    valid = valid_seg.astype(f32)[:, :, None, None]
-    is_gate = (jnp.arange(6) % 3 == 2)[None, None, :, None]
-    mods = jnp.where(is_gate, seg_mod * valid, seg_mod).reshape(slots_n, 6, D).transpose(1, 0, 2)
-
-    rows_small = group[:, :, D + 128 :][::-1]
-    rows_small = lax.dynamic_slice_in_dim(jnp.concatenate([rows_small, rows_small]), (mods_n - 1 - me) % mods_n, mods_n, 0)
-    rows_small = rows_small.reshape(mods_n, -1).astype(f32)
-    cuts = [0]
-    for bias in (qv_bias, proj_bias, fc1_bias, fc2_bias):
-        cuts.append(cuts[-1] + bias.shape[0])
-    full_qv = rows_small[:, cuts[0] : cuts[1]].reshape(-1)
-    full_proj_b = rows_small[:, cuts[1] : cuts[2]].reshape(1, -1)
-    full_fc1_b = rows_small[:, cuts[2] : cuts[3]].reshape(mods_n, 2, HALF)
-    full_fc2_b = rows_small[:, cuts[3] : cuts[4]].reshape(1, -1)
-    full_rel = rows_small[:, cuts[4] :].reshape(2, H // 4, 2, 2 * L)
-    bias_thirds = jnp.concatenate([full_qv[:D], jnp.zeros((D,), f32), full_qv[D:]]).reshape(3, 2, HALF)
-
-    def by_half(array, axis):
-        one, two = (lax.index_in_dim(array, n, axis, keepdims=False) for n in (0, 1))
-        return jnp.where(core > 0, one, two), jnp.where(core > 0, two, one)
-
-    qkv_b = [b.reshape(1, 3 * HALF) for b in by_half(bias_thirds, 1)]
-    fc1_b = [b.reshape(1, FH) for b in by_half(full_fc1_b, 1)]
-    rel = by_half(full_rel, 0)
-
-    x = block_input.reshape(T, D)
-    dy = grad_out.reshape(T, D)
+    mods, qkv_b1, qkv_b2, proj_b, fc1_b1, fc1_b2, fc2_b, rel_1, rel_2 = prepare(
+        idx, long_one, valid_seg, back, payloads
+    )
+    mods, *set_a[1] = fence(mods, *set_a[1])
+    units = set_a[3]
+    plane = [packets, set_a[1][0][units:], set_a[1][1][units:]]
+    set_a = assemble(*set_a)
     peer_a = swap(set_a, 1)
-    a, qkv1 = qkv_first(idx, x, mods, qkv_b[0], own_a, set_a)
-    o1, p1 = attend(qkv1, rel[0], long_one, valid_seg)
+    a, qkv1 = qkv_first(idx, x, mods, qkv_b1, own_a, set_a)
+    o1, p1 = attend(qkv1, rel_1, long_one, valid_seg)
     a, o1, peer_a = fence(a, o1, peer_a)
-    qkv2 = qkv_second(idx, a, qkv_b[1], own_a, peer_a)
-    o2, p2 = attend(qkv2, rel[1], long_one, valid_seg)
-    o2, *got_b = fence(o2, *got_b)
-    near_b = jnp.stack([g[0] for g in got_b])
-    diag_b = jnp.stack([g[1] for g in got_b])
-    side_b = [swap(near_b, 2), swap(near_b, 4)]
-    hidden, m_in, attn, d_mlp, db_fc2 = middle(idx, o1, o2, full_proj_b, x, dy, mods, own_a, set_a, peer_a)
-    m_in, near_b, diag_b, *side_b = fence(m_in, near_b, diag_b, *side_b)
-    set_b = jnp.stack([near_b, *side_b, diag_b])
+    qkv2 = qkv_second(idx, a, qkv_b2, own_a, peer_a)
+    o2, p2 = attend(qkv2, rel_2, long_one, valid_seg)
+    hidden, m_in, attn, d_mlp, db_fc2 = middle(idx, o1, o2, proj_b, x, dy, mods, own_a, set_a, peer_a)
+    m_in, *got_b = fence(m_in, *got_b)
+    set_b = list(sides(got_b, None, plane[1]))
+    m_in, piece_c, *set_b[1] = fence(m_in, piece_c, *set_b[1])
+    plane = jnp.stack(plane + [set_b[1][1][set_b[3] :]])
+    set_b = assemble(*set_b)
     peer_b = swap(set_b, 1)
-    own_c, piece_c = pick_ada(idx, w_ada)
-    piece_c, m_in = fence(piece_c, m_in)
     got_c = around(piece_c)
-    acc_o, acc_d, dw1_send, dw2_send, db1_first = mlp(idx, m_in, d_mlp, fc1_b[0], own_1, own_2, set_b)
+    acc_o, acc_d, dw1_send, dw2_send, db1_first = mlp(idx, m_in, d_mlp, fc1_b1, own_1, own_2, set_b)
     acc_o, peer_b, *got_c = fence(acc_o, peer_b, *got_c)
-    near_c = jnp.stack(got_c)
-    set_c = three(near_c)
+    set_c = three(jnp.stack(got_c))
     from_core = [swap(dw1_send, 1), swap(dw2_send, 1)]
     ff, dm, dw1_keep, dw2_keep, db1_second = mlp(
-        idx, m_in, d_mlp, fc1_b[1], own_1, own_2, peer_b, (acc_o, acc_d)
+        idx, m_in, d_mlp, fc1_b2, own_1, own_2, peer_b, (acc_o, acc_d)
     )
     ff, dw1_keep, dw2_keep, *rest = fence(ff, dw1_keep, dw2_keep, *from_core, *set_c)
-    from_core, set_c = rest[:2], jnp.stack(rest[2:])
-
-    side_x, side_y = spot % 2, spot // 2
-
-    def cut(terms, side):
-        size = terms[0].shape[1] // 2
-        return [take(term, side, size, 1) for term in terms]
-
-    terms_1 = [g.reshape(mods_n, D // mods_n, FH) for g in (dw1_keep, from_core[0])]
-    terms_2 = [g.reshape(mods_n, HALF, D) for g in (dw2_keep, from_core[1])]
-    in_1 = swap(add(*cut(terms_1, 1 - side_x)), 2)
-    in_2 = swap(add(*cut(terms_2, 1 - side_y)), 4)
+    from_core, set_c = rest[:2], rest[2:]
+
+    def quarters_of(grads):
+        return [g.reshape(g.shape[0], mods_n, 4, -1, g.shape[-1]) for g in grads]
+
+    def mine(grads, other):
+        return add(*[lax.dynamic_index_in_dim(g, lax.bitwise_xor(spot, other), 2, keepdims=False) for g in grads])
+
+    dw1 = quarters_of([g[None] for g in (dw1_keep, from_core[0])])
+    dw2 = quarters_of([g[None] for g in (dw2_keep, from_core[1])])
+
+    def ff_quarter(other):
+        one, two = mine(dw1, other)[0], mine(dw2, other)[0]
+        return jnp.concatenate([one[:, :, :D], one[:, :, D:], two], axis=1)
+
+    ff_plane = [swap(ff_quarter(n), 2 * n) for n in (1, 2, 3)]
     y, d_h, do1, do2, dwp_send, dwp_keep, dmod_mid, db_proj = back_middle(
-        idx, hidden, dy, ff, full_fc2_b, dm, attn, mods, o1, o2, own_a, set_a, peer_a
+        idx, hidden, dy, ff, fc2_b, dm, attn, mods, o1, o2, own_a, set_a, peer_a
     )
     dq1, dk1, dv1, dt1, dbq1 = attend_back(qkv1, p1, do1, o1, SHORT)
-    dwq_send = qkv_weight(a, dq1, dk1, dv1, SHORT)
-    in_1, in_2, dwq_send, do2, set_c = fence(in_1, in_2, dwq_send, do2, set_c)
-    terms_1 = cut(terms_1, side_x) + [in_1]
-    terms_2 = cut(terms_2, side_y) + [in_2]
-    far_in_1 = swap(add(*cut(terms_1, 1 - side_y)), 4)
-    far_in_2 = swap(add(*cut(terms_2, 1 - side_x)), 2)
+    dw_send = qkv_weight(a, dq1, dk1, dv1, dwp_send, SHORT)
+    dq2, dk2, dv2, dt2, dbq2 = attend_back(qkv2, p2, after(do2, dw_send), o2, SHORT)
+    dq2, dk2, dv2, dt2, dbq2, dw_send, dwp_keep, *ff_plane = fence(
+        dq2, dk2, dv2, dt2, dbq2, dw_send, dwp_keep, *ff_plane
+    )
+    ff_parts = spread_chips(add(ff_quarter(0), *ff_plane))
+    set_c = jnp.stack(set_c)
     peer_c = swap(set_c, 1)
-    dwq_in = swap(dwq_send, 1)
-    dwp_in = swap(dwp_send, 1)
-    dq2, dk2, dv2, dt2, dbq2 = attend_back(qkv2, p2, do2, o2, LONG)
-    dq2, dk2, dv2, dt2, dbq2, far_in_1, far_in_2, peer_c, dwq_in, dwp_in = fence(
-        dq2, dk2, dv2, dt2, dbq2, far_in_1, far_in_2, peer_c, dwq_in, dwp_in
-    )
-    kept_1 = spread_chips(add(*cut(terms_1, side_y), far_in_1))
-    kept_2 = spread_chips(add(*cut(terms_2, side_x), far_in_2))
-    ff_parts = jnp.concatenate([kept_1[:, :, :D], kept_1[:, :, D:], kept_2], axis=1)
-
-    def scatter_send(grad):
-        return [shift(pick_mod(grad, (me + k) % mods_n), k) for k in range(1, mods_n)]
-
-    ff_in = scatter_send(ff_parts)
-    dwq_keep = qkv_weight(a, dq2, dk2, dv2, LONG)
+    dw_in = swap(dw_send, 1)
+    plane_peer = swap(plane, 1)
+
+    def ring(step, total):
+        block = pick_mod(ff_parts, (me + 2 * mods_n - 1 - step) % mods_n)
+        return block if total is None else add(block, total)
+
+    ff_ring = shift(ring(0, None), 1)
+    dw_keep = qkv_weight(a, dq2, dk2, dv2, dwp_keep, LONG)
+    dw_keep, dt2, dbq2, ff_ring, dw_in, peer_c, plane_peer = fence(
+        dw_keep, dt2, dbq2, ff_ring, dw_in, peer_c, plane_peer
+    )
     packed = pack_small(idx, dbq1, dbq2, db_proj, db1_first, db1_second, db_fc2, dt1, dt2).astype(bf16)
     packed = add(packed, swap(packed, 1))
-
-    dwq = [dwq_keep, dwq_in]
-    dwp = [g.reshape(mods_n, D // mods_n, HALF) for g in (dwp_keep, dwp_in)]
-    left = [g[:, :D].reshape(mods_n, D // mods_n, D) for g in dwq]
-    right = [g[:, D:].reshape(mods_n, D // mods_n, HALF) for g in dwq]
-
-    def right_add(side):
-        return jnp.concatenate([add(*cut(right, side)), add(*cut(dwp, side))], axis=2)
-
-    in_l = swap(jnp.concatenate([add(*cut(left, 1 - side_x)), packed], axis=1), 2)
-    in_r = swap(right_add(1 - side_y), 4)
-    dx, dmod_entry = back_entry(
-        idx, (dq1, dk1, dv1, dq2, dk2, dv2), x, after(d_h, dwq_keep), mods, own_a, set_a, peer_a
-    )
-    d_cond = back_cond(idx, long_one, valid_seg, dmod_mid, dmod_entry, slope, own_c, set_c, peer_c).astype(bf16)
-    in_l, in_r, d_cond, dx, *ff_in = fence(in_l, in_r, d_cond, dx, *ff_in)
-    rows = left[0].shape[1] // 2
-    left = cut(left, side_x) + [in_l[:, :rows]]
-    packed = add(packed, in_l[:, rows:])
-    right_mid = [right_add(side_y), in_r]
-    far_l = swap(jnp.concatenate([add(*cut(left, 1 - side_y)), packed], axis=1), 4)
-    far_r = swap(add(*cut(right_mid, 1 - side_x)), 2)
-    cond_in = scatter_send(d_cond)
-    far_l, far_r, *cond_in = fence(far_l, far_r, *cond_in)
-    packed = add(packed, far_l[:, rows // 2 :])
-    attn_parts = spread_chips(
-        jnp.concatenate(
-            [add(*cut(left, side_y), far_l[:, : rows // 2]), add(*cut(right_mid, side_x), far_r), packed], axis=1
-        )
-    )
-    attn_in = scatter_send(attn_parts)
-    everyone = lax.all_gather(jnp.concatenate([pick_mod(d_cond, me), *cond_in]), "dp", axis=0, tiled=True)
-    ff_part = add(pick_mod(ff_parts, me), *ff_in)
-    attn_in[0], everyone = fence(attn_in[0], everyone)
-    attn_part = add(pick_mod(attn_parts, me), *attn_in)
-
+    ff_ring = shift(ring(1, ff_ring), 1)
+    d_h, ff_ring = fence(d_h, ff_ring)
+    ff_ring = shift(ring(2, ff_ring), 1)
+
+    dw = quarters_of([dw_keep, dw_in])
+
+    def quarter(other):
+        total = mine(dw, other)
+        return jnp.concatenate([total[0], total[1], packed], axis=1)
+
+    from_plane = [swap(quarter(n), 2 * n) for n in (1, 2, 3)]
+    dx, d_cond = back_entry(
+        idx, long_one, valid_seg, (dq1, dk1, dv1, dq2, dk2, dv2), x, d_h, mods, dmod_mid, cond,
+        own_a, set_a, peer_a, own_c, set_c, peer_c
+    )
+    d_cond, dx, ff_ring, *from_plane = fence(d_cond, dx, ff_ring, *from_plane)
+    parts = spread_chips(add(quarter(0), *from_plane))
+    tail_parts = jnp.concatenate([parts, d_cond], axis=1)
+    tail_in = [shift(pick_mod(tail_parts, (me + k) % mods_n), k) for k in range(1, mods_n)]
+    ff_part = ring(3, ff_ring)
+    ff_set = [ff_part, swap(ff_part, 2), swap(ff_part, 4)]
     def gather_chips(piece):
         mine = jnp.stack(three(piece))
         return mine, swap(mine, 1)
 
-    grad_fc1, grad_fc2 = finish_ff(idx, *gather_chips(ff_part))
-    grad_qkv, grad_proj = finish_attn(idx, *gather_chips(attn_part[:D // 8]))
-    small_all = attn_part[D // 8 :].astype(f32)
-
+    *ff_set, tail_in[0], tail_in[1], tail_in[2] = fence(*ff_set, *tail_in)
+    count = parts.shape[1]
+    arrived = [pick_mod(tail_parts, me)] + tail_in
+    part = add(*[t[:count] for t in arrived])
+    rows = D // 8
+    conds = [t[count : count + 3 * slots_n] for t in arrived]
+    gathered = gather_chips(jnp.concatenate([part[:rows]] + conds))
+    small_all = part[rows:].astype(f32)
+    ff_set = jnp.stack(ff_set + [swap(ff_part, 6)])
+    grad_fc1, grad_fc2 = finish_ff(idx, ff_set, swap(ff_set, 1))
+    grad_qkv, grad_proj = finish_attn(idx, *gathered)
+
+    conds = jnp.stack([g[:, rows:] for g in gathered]).reshape(-1, 3, slots_n, D)
+    acts = jnp.stack([plane, plane_peer]).reshape(-1, UR, HALF)
+    bit = 8
+    while bit < lax.axis_size("dp"):
+        conds = jnp.concatenate([conds, swap(conds, bit)])
+        acts = jnp.concatenate([acts, swap(acts, bit)])
+        bit *= 2
     width = w_ada.shape[1]
-    d_mod_all = everyone[:, :width]
-    d_cond_all = everyone[:, width:]
-    digits_all = act_all[:, D : D + 4].astype(jnp.int32)
-    grad_ada = lax.dot_general(act_all[:, :D], d_mod_all, (((0,), (0,)), ((), ())), preferred_element_type=f32)
+    d_mod_all = jnp.concatenate([conds[:, 0].reshape(-1, D), conds[:, 1].reshape(-1, D)[:, : width - D]], axis=1)
+    d_cond_all = conds[:, 2].reshape(-1, D)
+    act_all = jnp.concatenate(
+        [acts[:, n * slots_n : (n + 1) * slots_n].reshape(-1, HALF) for n in range(2)], axis=1
+    )
+    digits_all = acts[:, 2 * slots_n : 3 * slots_n, :4].reshape(-1, 4).astype(jnp.int32)
+    grad_ada = lax.dot_general(act_all, d_mod_all, (((0,), (0,)), ((), ())), preferred_element_type=f32)
     grad_ada_b = jnp.sum(d_mod_all.astype(f32), axis=0)
 
     def table_grad(high, low, rows):
@@ -1222,7 +1326,7 @@
         small_all[4],
         grad_fc2,
         take(small_all[7], me, fc2_bias.shape[0]),
-        grad_rel[:, : rel_shape[1]],
+        grad_rel[:, : rel_table.shape[1]],
     )
 
 

time: 415 us -> 391 us (0.942)
  waiting for transfers between devices: 35.5 us -> 88.2 us
  blocking collectives: 28.3 us -> 0 us
  local copies, waits for them, and re-layouts: 50.4 us -> 27.9 us
  starting transfers between devices: 66.9 us -> 48 us
  other arithmetic: 32.3 us -> 23.3 us
    ppermute x24 -> x18, waiting for transfers between devices: 14.2 us -> 43.2 us  [shift(): lax.ppermute(array, 'mod', [(i, (i + step) % count) for i in range(count)])]
    all_gather x2 -> x0, blocking collectives: 28.3 us -> none  [the longest x1 18.1 us: local(): lax.all_gather(group[:, :, :D + 128].reshape(mods_n * slots_n, D + 128),...]
    ppermute x32 -> x29, waiting for transfers between devices: 21.3 us -> 45 us  [swap(): return lax.ppermute(array, 'dp', [(i, i ^ bit) for i in range(count)])]
    ppermute x24 -> x18, starting transfers between devices: 40.6 us -> 25.1 us  [shift(): lax.ppermute(array, 'mod', [(i, (i + step) % count) for i in range(count)])]
    convert_element_type x18 -> x10, other arithmetic: 18 us -> 11.4 us  [add(): return total.astype(bf16)]
    slice x13 -> x16, local copies, waits for them, and re-layouts: 9.75 us -> 3.77 us  [the longest x4 3.25 us: local(): packets = jnp.stack([p[8] for p in payloads])]
    ppermute x32 -> x29, starting transfers between devices: 26.3 us -> 22.9 us  [swap(): return lax.ppermute(array, 'dp', [(i, i ^ bit) for i in range(count)])]
    pallas_call x5 -> x6, Pallas kernels: 33.3 us -> 36.3 us  [the longest x1 16.1 us: back_entry(): pl.pallas_call(back_entry_body, grid=(MICRO,), in_specs=[SMEM] * 3 + [par...]
  transfers between devices with their start and end apart: 56 -> 47, of which waited for: 10 -> 16; matrix products, arithmetic and copies ran while one was open for 16% -> 7% of each run, Pallas kernels for 43% -> 48%
where the time goes in v3:
time: 391 us; the launch traced here: 386 us
  Pallas kernels  191 us (49%)
  waiting for transfers between devices  88.2 us (23%)
  starting transfers between devices  48 us (12%)
  local copies, waits for them, and re-layouts  27.9 us (7%)
  other arithmetic  23.3 us (6%)
  matrix products  4.89 us (1%)
    pallas_call x2, Pallas kernels, mlp(): pl.pallas_call(partial(mlp_body, acc is not None), grid=(FH // FB,), in_s...  47 us
    ppermute x29, waiting for transfers between devices, swap(): return lax.ppermute(array, 'dp', [(i, i ^ bit) for i in range(count)])  45 us
    ppermute x18, waiting for transfers between devices, shift(): lax.ppermute(array, 'mod', [(i, (i + step) % count) for i in range(count)])  43.2 us
    pallas_call x2, Pallas kernels, attend(): pl.pallas_call(attend_body, grid_spec=pltpu.PrefetchScalarGridSpec(num_sc...  28.2 us
    pallas_call x2, Pallas kernels, attend_back(): pl.pallas_call(attend_back_body, grid=(3, MICRO), in_specs=[part, pl.Bloc...  27.6 us
    ppermute x18, starting transfers between devices, shift(): lax.ppermute(array, 'mod', [(i, (i + step) % count) for i in range(count)])  25.1 us
    ppermute x29, starting transfers between devices, swap(): return lax.ppermute(array, 'dp', [(i, i ^ bit) for i in range(count)])  22.9 us
    pallas_call x1, Pallas kernels, back_entry(): pl.pallas_call(back_entry_body, grid=(MICRO,), in_specs=[SMEM] * 3 + [par...  16.1 us
  transfers between devices with their start and end apart: 47, of which 16 were waited for; matrix products, arithmetic and copies ran while one was open for 7% of the time, Pallas kernels for 48%

profile of v3, /device:TPU:0, one launch (start us, length us, event | category | flops | bytes accessed | tf_op | source)
XLA Modules:
  0.0 385.8 jit_solution(16005896012341867268)
XLA Ops:
  12.3 5.0 %collective-permute-start.2 = (bf16[9,48,384]{2,1,0:T(8,128)(2,1)}, bf16[9,48,384]{2,1,0:T(8,128)(2,1)S(1)}, u32[]{:S(2)}, u32[]{:S(2)}) collective-permute-start(bf16[9,48,384]{2,1,0:T(8,128)(2,1)} %get-tuple-element.149.p0), channel_id=1, source_target_pairs={{0,3},{1,0},{2,1},{3,2},{4,7},{5,4},{6,5},{7,6},{8,11},{9,8},{10,9... | collective-permute-start | bytes 995336 | tf_op jit(solution)/shard_map/ppermute | solution.py:1080
  26.0 19.9 %collective-permute-done.1.p2 = bf16[9,48,384]{2,1,0:T(8,128)(2,1)S(1)} collective-permute-done((bf16[9,48,384]{2,1,0:T(8,128)(2,1)}, bf16[9,48,384]{2,1,0:T(8,128)(2,1)S(1)}, u32[]{:S(2)}, u32[]{:S(2)}) %collective-permute-start.1) | collective-permute-done | bytes 331808 | tf_op jit(solution)/shard_map/ppermute | solution.py:1080
  73.2 7.3 %qkv_first.1 = (bf16[1024,768]{1,0:T(8,128)(2,1)}, bf16[1024,1152]{1,0:T(8,128)(2,1)}) custom-call(s32[3]{0:T(128)} %pad_add_fusion.idx_ref, bf16[1024,768]{1,0:T(8,128)(2,1)} %bitcast.213, f32[6,8,768]{2,1,0:T(8,128)} %get-tuple-element.158.mod_ref, f32[1,1152]{1,0:T(1,128)} %get-tuple-element.159.b_ref, ...), custom_call_target="tpu_custom_call" | custom-call | flops 1 | bytes 1 | tf_op jit(solution)/shard_map/qkv_first/pallas_call | solution.py:361
  80.5 14.1 %attend.2 = (bf16[1024,384]{1,0:T(8,128)(2,1)}, bf16[2,6,512,512]{3,2,1,0:T(8,128)(2,1)}) custom-call(s32[2]{0:T(128)} %bitcast.237, s32[2,4]{1,0:T(2,128)} %bitcast.233, bf16[1024,1152]{1,0:T(8,128)(2,1)} %get-tuple-element.164.q_ref.k_ref.v_ref, bf16[1024,1152]{1,0:T(8,128)(2,1)} %get-tuple-element.164.q_ref.k_ref.v_ref, ...), custom_call_target="tpu_custom_call" | custom-call | flops 1 | bytes 1 | tf_op jit(solution)/shard_map/attend/pallas_call | solution.py:464
  96.5 6.2 %qkv_second.1.q_ref.k_ref.v_ref = bf16[1024,1152]{1,0:T(8,128)(2,1)} custom-call(s32[3]{0:T(128)} %pad_add_fusion.idx_ref, bf16[1024,768]{1,0:T(8,128)(2,1)} %get-tuple-element.168.a_ref, f32[1,1152]{1,0:T(1,128)} %get-tuple-element.169.b_ref, bf16[2,4,4,48,384]{4,3,2,1,0:T(8,128)(2,1)} %get-tuple-element.160.own, bf16[4,3,4,48,384]{4,3,2,1,0:T(8,128)(2,1)} %copy-done.15), custom_call_target="tpu_custom_call" | custom-call | flops 1 | bytes 1 | tf_op jit(solution)/shard_map/qkv_second/pallas_call | solution.py:398
  102.6 14.1 %attend.3 = (bf16[1024,384]{1,0:T(8,128)(2,1)}, bf16[2,6,512,512]{3,2,1,0:T(8,128)(2,1)}) custom-call(s32[2]{0:T(128)} %bitcast.238, s32[2,4]{1,0:T(2,128)} %bitcast.234, bf16[1024,1152]{1,0:T(8,128)(2,1)} %qkv_second.1.q_ref.k_ref.v_ref, bf16[1024,1152]{1,0:T(8,128)(2,1)} %qkv_second.1.q_ref.k_ref.v_ref, bf16[1024,1152]{1,0:T(8,128)(2,1)} %qkv_second.1.q_ref.k_ref.v_ref, ...), custom_call_target="tpu_custom_call" | custom-call | flops 1 | bytes 1 | tf_op jit(solution)/shard_map/attend/pallas_call | solution.py:464
  116.8 8.9 %middle.1 = (f32[1024,768]{1,0:T(8,128)}, bf16[1024,768]{1,0:T(8,128)(2,1)}, bf16[1024,768]{1,0:T(8,128)(2,1)}, bf16[1024,768]{1,0:T(8,128)(2,1)}, f32[8,768]{1,0:T(8,128)}) custom-call(s32[3]{0:T(128)} %pad_add_fusion.idx_ref, bf16[1024,384]{1,0:T(8,128)(2,1)} %get-tuple-element.167.o1_ref.o_ref, bf16[1024,384]{1,0:T(8,128)(2,1)} %get-tuple-element.172.o2_ref.o_ref, ...), custom_call_target="tpu_custom_call" | custom-call | flops 30000001024 | bytes 1000000 | tf_op jit(solution)/shard_map/middle/pallas_call | solution.py:533
  127.5 19.9 %collective-permute-done.12 = bf16[24,48,384]{2,1,0:T(8,128)(2,1)S(1)} collective-permute-done((bf16[24,48,384]{2,1,0:T(8,128)(2,1)S(1)}, bf16[24,48,384]{2,1,0:T(8,128)(2,1)S(1)}, u32[]{:S(2)}, u32[]{:S(2)}) %collective-permute-start.12) | collective-permute-done | bytes 884768 | tf_op jit(solution)/shard_map/ppermute | solution.py:1075
  159.1 22.5 %mlp.2 = (f32[1024,768]{1,0:T(8,128)}, f32[1024,768]{1,0:T(8,128)}, bf16[768,1536]{1,0:T(8,128)(2,1)}, bf16[1536,768]{1,0:T(8,128)(2,1)}, f32[8,1536]{1,0:T(8,128)}) custom-call(s32[3]{0:T(128)} %pad_add_fusion.idx_ref, bf16[1024,768]{1,0:T(8,128)(2,1)} %get-tuple-element.182.m_ref, bf16[1024,768]{1,0:T(8,128)(2,1)} %get-tuple-element.183.dmlp_ref, ...), custom_call_target="tpu_custom_call" | custom-call | flops 30000001024 | bytes 1000000 | tf_op jit(solution)/shard_map/mlp/pallas_call | solution.py:643
  187.9 24.5 %mlp.3 = (f32[1024,768]{1,0:T(8,128)}, f32[1024,768]{1,0:T(8,128)}, bf16[768,1536]{1,0:T(8,128)(2,1)}, bf16[1536,768]{1,0:T(8,128)(2,1)}, f32[8,1536]{1,0:T(8,128)}) custom-call(s32[3]{0:T(128)} %pad_add_fusion.idx_ref, bf16[1024,768]{1,0:T(8,128)(2,1)} %get-tuple-element.182.m_ref, bf16[1024,768]{1,0:T(8,128)(2,1)} %get-tuple-element.183.dmlp_ref, ...), custom_call_target="tpu_custom_call" | custom-call | flops 30000001024 | bytes 1000000 | tf_op jit(solution)/shard_map/mlp/pallas_call | solution.py:643
  215.7 3.5 fusion.6
  226.5 14.4 %back_middle.1 = (bf16[1024,768]{1,0:T(8,128)(2,1)}, f32[1024,768]{1,0:T(8,128)}, bf16[1024,384]{1,0:T(8,128)(2,1)}, bf16[1024,384]{1,0:T(8,128)(2,1)}, bf16[768...) custom-call(s32[3]{0:T(128)} %pad_add_fusion.idx_ref, ...), custom_call_target="tpu_custom_call" | custom-call | flops 30000001024 | bytes 1000000 | tf_op jit(solution)/shard_map/back_middle/pallas_call | solution.py:742
  240.9 13.4 %attend_back.2 = (bf16[1024,384]{1,0:T(8,128)(2,1)}, bf16[1024,384]{1,0:T(8,128)(2,1)}, bf16[1024,384]{1,0:T(8,128)(2,1)}, f32[3,8,1024]{2,1,0:T(8,128)}, f32[8,384]{1,0:T(8,128)}) custom-call(bf16[1024,1152]{1,0:T(8,128)(2,1)} %get-tuple-element.164.q_ref.k_ref.v_ref, bf16[1024,1152]{1,0:T(8,128)(2,1)} %get-tuple-element.164.q_ref.k_ref.v_ref, ...), custom_call_target="tpu_custom_call" | custom-call | flops 1 | bytes 1 | tf_op jit(solution)/shard_map/attend_back/pallas_call | solution.py:831
  254.3 5.9 %qkv_weight.2 = bf16[2,768,768]{2,1,0:T(8,128)(2,1)} custom-call(bf16[1024,768]{1,0:T(8,128)(2,1)} %get-tuple-element.168.a_ref, bf16[1024,384]{1,0:T(8,128)(2,1)} %get-tuple-element.210.dq_ref.dq1, bf16[1024,384]{1,0:T(8,128)(2,1)} %get-tuple-element.211.dk_ref.dk1, bf16[1024,384]{1,0:T(8,128)(2,1)} %get-tuple-element.212.dv_ref.dv1, ...), custom_call_target="tpu_custom_call" | custom-call | flops 1 | bytes 1 | tf_op jit(solution)/shard_map/qkv_weight/pallas_call | solution.py:862
  262.0 14.2 %attend_back.3 = (bf16[1024,384]{1,0:T(8,128)(2,1)}, bf16[1024,384]{1,0:T(8,128)(2,1)}, bf16[1024,384]{1,0:T(8,128)(2,1)}, f32[3,8,1024]{2,1,0:T(8,128)}, f32[8,384]{1,0:T(8,128)}) custom-call(bf16[1024,1152]{1,0:T(8,128)(2,1)} %qkv_second.1.q_ref.k_ref.v_ref, bf16[1024,1152]{1,0:T(8,128)(2,1)} %qkv_second.1.q_ref.k_ref.v_ref, ...), custom_call_target="tpu_custom_call" | custom-call | flops 1 | bytes 1 | tf_op jit(solution)/shard_map/attend_back/pallas_call | solution.py:831
  281.3 5.9 %qkv_weight.3 = bf16[2,768,768]{2,1,0:T(8,128)(2,1)} custom-call(bf16[1024,768]{1,0:T(8,128)(2,1)} %get-tuple-element.168.a_ref, bf16[1024,384]{1,0:T(8,128)(2,1)} %get-tuple-element.227.dq_ref.dq2, bf16[1024,384]{1,0:T(8,128)(2,1)} %get-tuple-element.228.dk_ref.dk2, bf16[1024,384]{1,0:T(8,128)(2,1)} %get-tuple-element.229.dv_ref.dv2, ...), custom_call_target="tpu_custom_call" | custom-call | flops 30000001024 | bytes 1000000 | tf_op jit(solution)/shard_map/qkv_weight/pallas_call | solution.py:862
  303.8 16.1 %back_entry.1 = (bf16[1024,768]{1,0:T(8,128)(2,1)}, bf16[4,32,768]{2,1,0:T(8,128)(2,1)}) custom-call(s32[3]{0:T(128)} %pad_add_fusion.idx_ref, s32[2]{0:T(128)} %bitcast.239, s32[2,4]{1,0:T(2,128)} %bitcast.235, bf16[1024,384]{1,0:T(8,128)(2,1)} %get-tuple-element.210.dq_ref.dq1, bf16[1024,384]{1,0:T(8,128)(2,1)} %get-tuple-element.211.dk_ref.dk1, ...), custom_call_target="tpu_custom_call" | custom-call | flops 30000001024 | bytes 1000000 | tf_op jit(solution)/shard_map/back_entry/pallas_call | solution.py:962
  320.0 8.1 %collective-permute-done.34 = bf16[4,104,768]{2,1,0:T(8,128)(2,1)S(1)} collective-permute-done((bf16[4,104,768]{2,1,0:T(8,128)(2,1)S(1)}, bf16[4,104,768]{2,1,0:T(8,128)(2,1)S(1)}, u32[]{:S(2)}, u32[]{:S(2)}) %collective-permute-start.34) | collective-permute-done | bytes 639008 | tf_op jit(solution)/shard_map/ppermute | solution.py:1075
  331.0 3.6 collective-permute-start.40
  336.9 6.4 %collective-permute-done.40 = bf16[136,768]{1,0:T(8,128)(2,1)S(1)} collective-permute-done((bf16[136,768]{1,0:T(8,128)(2,1)S(1)}, bf16[136,768]{1,0:T(8,128)(2,1)S(1)}, u32[]{:S(2)}, u32[]{:S(2)}) %collective-permute-start.40) | collective-permute-done | bytes 208928 | tf_op jit(solution)/shard_map/ppermute | solution.py:1080
  344.9 5.8 %collective-permute-done.39 = bf16[136,768]{1,0:T(8,128)(2,1)} collective-permute-done((bf16[136,768]{1,0:T(8,128)(2,1)S(1)}, bf16[136,768]{1,0:T(8,128)(2,1)}, u32[]{:S(2)}, u32[]{:S(2)}) %collective-permute-start.39) | collective-permute-done | bytes 208928 | tf_op jit(solution)/shard_map/ppermute | solution.py:1080
  356.3 7.1 %collective-permute-done.43 = bf16[192,768]{1,0:T(8,128)(2,1)S(1)} collective-permute-done((bf16[192,768]{1,0:T(8,128)(2,1)S(1)}, bf16[192,768]{1,0:T(8,128)(2,1)S(1)}, u32[]{:S(2)}, u32[]{:S(2)}) %collective-permute-start.43) | collective-permute-done | bytes 294944 | tf_op jit(solution)/shard_map/ppermute | solution.py:1075
  363.4 3.9 %collective-permute-done.42 = bf16[192,768]{1,0:T(8,128)(2,1)S(1)} collective-permute-done((bf16[192,768]{1,0:T(8,128)(2,1)S(1)}, bf16[192,768]{1,0:T(8,128)(2,1)S(1)}, u32[]{:S(2)}, u32[]{:S(2)}) %collective-permute-start.42) | collective-permute-done | bytes 294944 | tf_op jit(solution)/shard_map/ppermute | solution.py:1075
  371.1 4.1 %finish_ff.1 = (f32[192,3072]{1,0:T(8,128)}, f32[768,768]{1,0:T(8,128)}) custom-call(s32[3]{0:T(128)} %pad_add_fusion.idx_ref, bf16[4,192,768]{2,1,0:T(8,128)(2,1)} %copy-done.4, bf16[4,192,768]{2,1,0:T(8,128)(2,1)} %collective-permute-done.46.peer_ref), custom_call_target="tpu_custom_call" | custom-call | flops 1 | bytes 1 | tf_op jit(solution)/shard_map/finish_ff/pallas_call | solution.py:1034
  (247 shorter events, 128.9 us)
Async XLA Ops:
  17.4 28.5 %collective-permute-start.1 = (bf16[9,48,384]{2,1,0:T(8,128)(2,1)}, bf16[9,48,384]{2,1,0:T(8,128)(2,1)S(1)}, u32[]{:S(2)}, u32[]{:S(2)}) collective-permute-start(bf16[9,48,384]{2,1,0:T(8,128)(2,1)} %get-tuple-element.149.p0), channel_id=1, source_target_pairs={{0,2},{1,3},{2,0},{3,1},{4,6},{5,7},{6,4},{7,5},{8,10},{9,11},{10,... | collective-permute-start | bytes 995336 | tf_op jit(solution)/shard_map/ppermute | solution.py:1080
  17.4 28.5 %collective-permute-start = (bf16[9,48,384]{2,1,0:T(8,128)(2,1)}, bf16[9,48,384]{2,1,0:T(8,128)(2,1)S(1)}, u32[]{:S(2)}, u32[]{:S(2)}) collective-permute-start(bf16[9,48,384]{2,1,0:T(8,128)(2,1)} %get-tuple-element.149.p0), channel_id=1, source_target_pairs={{0,1},{1,2},{2,3},{3,0},{4,5},{5,6},{6,7},{7,4},{8,9},{9,10},{10,1... | collective-permute-start | bytes 995336 | tf_op jit(solution)/shard_map/ppermute | solution.py:1080
  70.1 25.2 %collective-permute-start.8 = (bf16[4,3,4,48,384]{4,3,2,1,0:T(8,128)(2,1)S(1)}, bf16[4,3,4,48,384]{4,3,2,1,0:T(8,128)(2,1)S(1)}, u32[]{:S(2)}, u32[]{:S(2)}) collective-permute-start(bf16[4,3,4,48,384]{4,3,2,1,0:T(8,128)(2,1)S(1)} %pad_maximum_fusion.2.fetched), channel_id=1, source_target_pairs={{0,4},{4,0},{8,12},{12,8},{16,20},{20,16},{24,28},{28,24},{1,5},{5... | collective-permute-start | bytes 5308424 | tf_op jit(solution)/shard_map/ppermute | solution.py:1075
  70.8 54.8 %collective-permute-start.11 = (bf16[2,8,48,384]{3,2,1,0:T(8,128)(2,1)S(1)}, bf16[2,8,48,384]{3,2,1,0:T(8,128)(2,1)S(1)}, u32[]{:S(2)}, u32[]{:S(2)}) collective-permute-start(bf16[2,8,48,384]{3,2,1,0:T(8,128)(2,1)S(1)} %copy-done.28), channel_id=1, source_target_pairs={{0,3},{1,0},{2,1},{3,2},{4,7},{5,4},{6,5},{7,6},{8,11},{9,8},{10,9... | collective-permute-start | bytes 1769480 | tf_op jit(solution)/shard_map/ppermute | solution.py:1080
  71.3 54.3 %collective-permute-start.10 = (bf16[2,8,48,384]{3,2,1,0:T(8,128)(2,1)S(1)}, bf16[2,8,48,384]{3,2,1,0:T(8,128)(2,1)S(1)}, u32[]{:S(2)}, u32[]{:S(2)}) collective-permute-start(bf16[2,8,48,384]{3,2,1,0:T(8,128)(2,1)S(1)} %copy-done.28), channel_id=1, source_target_pairs={{0,2},{1,3},{2,0},{3,1},{4,6},{5,7},{6,4},{7,5},{8,10},{9,11},{10,... | collective-permute-start | bytes 1769480 | tf_op jit(solution)/shard_map/ppermute | solution.py:1080
  72.5 53.2 %collective-permute-start.9 = (bf16[2,8,48,384]{3,2,1,0:T(8,128)(2,1)S(1)}, bf16[2,8,48,384]{3,2,1,0:T(8,128)(2,1)S(1)}, u32[]{:S(2)}, u32[]{:S(2)}) collective-permute-start(bf16[2,8,48,384]{3,2,1,0:T(8,128)(2,1)S(1)} %copy-done.28), channel_id=1, source_target_pairs={{0,1},{1,2},{2,3},{3,0},{4,5},{5,6},{6,7},{7,4},{8,9},{9,10},{10,1... | collective-permute-start | bytes 1769480 | tf_op jit(solution)/shard_map/ppermute | solution.py:1080
  126.1 24.0 %collective-permute-start.13 = (bf16[28,48,384]{2,1,0:T(8,128)(2,1)S(1)}, bf16[28,48,384]{2,1,0:T(8,128)(2,1)S(1)}, u32[]{:S(2)}, u32[]{:S(2)}) collective-permute-start(bf16[28,48,384]{2,1,0:T(8,128)(2,1)S(1)} %pad_maximum_fusion.14), channel_id=1, source_target_pairs={{0,16},{4,20},{8,24},{12,28},{16,0},{20,4},{24,8},{28,12},{1,17},{... | collective-permute-start | bytes 3096584 | tf_op jit(solution)/shard_map/ppermute | solution.py:1075
  151.6 32.6 %collective-permute-start.14 = (bf16[4,3,8,48,384]{4,3,2,1,0:T(8,128)(2,1)S(1)}, bf16[4,3,8,48,384]{4,3,2,1,0:T(8,128)(2,1)}, u32[]{:S(2)}, u32[]{:S(2)}) collective-permute-start(bf16[4,3,8,48,384]{4,3,2,1,0:T(8,128)(2,1)S(1)} %pad_maximum_fusion.fetched), channel_id=1, source_target_pairs={{0,4},{4,0},{8,12},{12,8},{16,20},{20,16},{24,28},{28,24},{1,5},{5... | collective-permute-start | bytes 10616840 | tf_op jit(solution)/shard_map/ppermute | solution.py:1075
  153.8 29.9 %collective-permute-start.17 = (bf16[6,48,384]{2,1,0:T(8,128)(2,1)}, bf16[6,48,384]{2,1,0:T(8,128)(2,1)S(1)}, u32[]{:S(2)}, u32[]{:S(2)}) collective-permute-start(bf16[6,48,384]{2,1,0:T(8,128)(2,1)} %get-tuple-element.191), channel_id=1, source_target_pairs={{0,3},{1,0},{2,1},{3,2},{4,7},{5,4},{6,5},{7,6},{8,11},{9,8},{10,9... | collective-permute-start | bytes 663560 | tf_op jit(solution)/shard_map/ppermute | solution.py:1080
  157.0 27.2 %collective-permute-start.16 = (bf16[6,48,384]{2,1,0:T(8,128)(2,1)}, bf16[6,48,384]{2,1,0:T(8,128)(2,1)S(1)}, u32[]{:S(2)}, u32[]{:S(2)}) collective-permute-start(bf16[6,48,384]{2,1,0:T(8,128)(2,1)} %get-tuple-element.191), channel_id=1, source_target_pairs={{0,2},{1,3},{2,0},{3,1},{4,6},{5,7},{6,4},{7,5},{8,10},{9,11},{10,... | collective-permute-start | bytes 663560 | tf_op jit(solution)/shard_map/ppermute | solution.py:1080
  157.0 27.2 %collective-permute-start.15 = (bf16[6,48,384]{2,1,0:T(8,128)(2,1)}, bf16[6,48,384]{2,1,0:T(8,128)(2,1)S(1)}, u32[]{:S(2)}, u32[]{:S(2)}) collective-permute-start(bf16[6,48,384]{2,1,0:T(8,128)(2,1)} %get-tuple-element.191), channel_id=1, source_target_pairs={{0,1},{1,2},{2,3},{3,0},{4,5},{5,6},{6,7},{7,4},{8,9},{9,10},{10,1... | collective-permute-start | bytes 663560 | tf_op jit(solution)/shard_map/ppermute | solution.py:1080
  182.5 29.9 %collective-permute-start.18 = (bf16[768,1536]{1,0:T(8,128)(2,1)}, bf16[768,1536]{1,0:T(8,128)(2,1)}, u32[]{:S(2)}, u32[]{:S(2)}) collective-permute-start(bf16[768,1536]{1,0:T(8,128)(2,1)} %get-tuple-element.198), channel_id=1, source_target_pairs={{0,4},{4,0},{8,12},{12,8},{16,20},{20,16},{24,28},{28,24},{1,5},{5... | collective-permute-start | bytes 7077896 | tf_op jit(solution)/shard_map/ppermute | solution.py:1075
  183.7 28.8 %collective-permute-start.19 = (bf16[1536,768]{1,0:T(8,128)(2,1)}, bf16[1536,768]{1,0:T(8,128)(2,1)S(1)}, u32[]{:S(2)}, u32[]{:S(2)}) collective-permute-start(bf16[1536,768]{1,0:T(8,128)(2,1)} %get-tuple-element.199), channel_id=1, source_target_pairs={{0,4},{4,0},{8,12},{12,8},{16,20},{20,16},{24,28},{28,24},{1,5},{5... | collective-permute-start | bytes 7077896 | tf_op jit(solution)/shard_map/ppermute | solution.py:1075
  184.3 28.2 %collective-permute-start.22 = (bf16[3,6,48,384]{3,2,1,0:T(8,128)(2,1)S(1)}, bf16[3,6,48,384]{3,2,1,0:T(8,128)(2,1)S(1)}, u32[]{:S(2)}, u32[]{:S(2)}) collective-permute-start(bf16[3,6,48,384]{3,2,1,0:T(8,128)(2,1)S(1)} %pad_maximum_fusion.17), channel_id=1, source_target_pairs={{0,24},{4,28},{8,16},{12,20},{16,8},{20,12},{24,0},{28,4},{1,25},{... | collective-permute-start | bytes 1990664 | tf_op jit(solution)/shard_map/ppermute | solution.py:1075
  184.9 30.8 %collective-permute-start.21 = (bf16[3,6,48,384]{3,2,1,0:T(8,128)(2,1)S(1)}, bf16[3,6,48,384]{3,2,1,0:T(8,128)(2,1)S(1)}, u32[]{:S(2)}, u32[]{:S(2)}) collective-permute-start(bf16[3,6,48,384]{3,2,1,0:T(8,128)(2,1)S(1)} %pad_maximum_fusion.17), channel_id=1, source_target_pairs={{0,16},{4,20},{8,24},{12,28},{16,0},{20,4},{24,8},{28,12},{1,17},{... | collective-permute-start | bytes 1990664 | tf_op jit(solution)/shard_map/ppermute | solution.py:1075
  186.4 29.3 %collective-permute-start.20 = (bf16[3,6,48,384]{3,2,1,0:T(8,128)(2,1)S(1)}, bf16[3,6,48,384]{3,2,1,0:T(8,128)(2,1)S(1)}, u32[]{:S(2)}, u32[]{:S(2)}) collective-permute-start(bf16[3,6,48,384]{3,2,1,0:T(8,128)(2,1)S(1)} %pad_maximum_fusion.17), channel_id=1, source_target_pairs={{0,8},{4,12},{8,0},{12,4},{16,24},{20,28},{24,16},{28,20},{1,9},{5... | collective-permute-start | bytes 1990664 | tf_op jit(solution)/shard_map/ppermute | solution.py:1075
  212.4 74.7 %collective-permute-start.29 = (bf16[4,4,48,384]{3,2,1,0:T(8,128)(2,1)}, bf16[4,4,48,384]{3,2,1,0:T(8,128)(2,1)}, u32[]{:S(2)}, u32[]{:S(2)}) collective-permute-start(bf16[4,4,48,384]{3,2,1,0:T(8,128)(2,1)} %get-tuple-element.300), channel_id=1, source_target_pairs={{0,4},{4,0},{8,12},{12,8},{16,20},{20,16},{24,28},{28,24},{1,5},{5... | collective-permute-start | bytes 1769480 | tf_op jit(solution)/shard_map/ppermute | solution.py:1075
  221.7 54.5 %collective-permute-start.23 = (bf16[4,192,768]{2,1,0:T(8,128)(2,1)S(1)}, bf16[4,192,768]{2,1,0:T(8,128)(2,1)}, u32[]{:S(2)}, u32[]{:S(2)}) collective-permute-start(bf16[4,192,768]{2,1,0:T(8,128)(2,1)S(1)} %pad_maximum_fusion.7), channel_id=1, source_target_pairs={{0,8},{4,12},{8,0},{12,4},{16,24},{20,28},{24,16},{28,20},{1,9},{5... | collective-permute-start | bytes 3538952 | tf_op jit(solution)/shard_map/ppermute | solution.py:1075
  223.1 53.2 %collective-permute-start.24 = (bf16[4,192,768]{2,1,0:T(8,128)(2,1)S(1)}, bf16[4,192,768]{2,1,0:T(8,128)(2,1)}, u32[]{:S(2)}, u32[]{:S(2)}) collective-permute-start(bf16[4,192,768]{2,1,0:T(8,128)(2,1)S(1)} %pad_maximum_fusion.8), channel_id=1, source_target_pairs={{0,16},{4,20},{8,24},{12,28},{16,0},{20,4},{24,8},{28,12},{1,17},{... | collective-permute-start | bytes 3538952 | tf_op jit(solution)/shard_map/ppermute | solution.py:1075
  224.8 51.5 %collective-permute-start.25 = (bf16[4,192,768]{2,1,0:T(8,128)(2,1)}, bf16[4,192,768]{2,1,0:T(8,128)(2,1)}, u32[]{:S(2)}, u32[]{:S(2)}) collective-permute-start(bf16[4,192,768]{2,1,0:T(8,128)(2,1)} %pad_maximum_fusion.9), channel_id=1, source_target_pairs={{0,24},{4,28},{8,16},{12,20},{16,8},{20,12},{24,0},{28,4},{1,25},{... | collective-permute-start | bytes 3538952 | tf_op jit(solution)/shard_map/ppermute | solution.py:1075
  261.9 27.8 %collective-permute-start.28 = (bf16[4,3,6,48,384]{4,3,2,1,0:T(8,128)(2,1)S(1)}, bf16[4,3,6,48,384]{4,3,2,1,0:T(8,128)(2,1)}, u32[]{:S(2)}, u32[]{:S(2)}) collective-permute-start(bf16[4,3,6,48,384]{4,3,2,1,0:T(8,128)(2,1)S(1)} %pad_maximum_fusion.1.fetched_c), channel_id=1, source_target_pairs={{0,4},{4,0},{8,12},{12,8},{16,20},{20,16},{24,28},{28,24},{1,5},{5... | collective-permute-start | bytes 7962632 | tf_op jit(solution)/shard_map/ppermute | solution.py:1075
  296.7 23.2 %collective-permute-start.35 = (bf16[4,104,768]{2,1,0:T(8,128)(2,1)S(1)}, bf16[4,104,768]{2,1,0:T(8,128)(2,1)S(1)}, u32[]{:S(2)}, u32[]{:S(2)}) collective-permute-start(bf16[4,104,768]{2,1,0:T(8,128)(2,1)S(1)} %get-tuple-element.342), channel_id=1, source_target_pairs={{0,24},{4,28},{8,16},{12,20},{16,8},{20,12},{24,0},{28,4},{1,25},{... | collective-permute-start | bytes 1916936 | tf_op jit(solution)/shard_map/ppermute | solution.py:1075
  298.0 30.1 %collective-permute-start.34 = (bf16[4,104,768]{2,1,0:T(8,128)(2,1)S(1)}, bf16[4,104,768]{2,1,0:T(8,128)(2,1)S(1)}, u32[]{:S(2)}, u32[]{:S(2)}) collective-permute-start(bf16[4,104,768]{2,1,0:T(8,128)(2,1)S(1)} %get-tuple-element.343), channel_id=1, source_target_pairs={{0,16},{4,20},{8,24},{12,28},{16,0},{20,4},{24,8},{28,12},{1,17},{... | collective-permute-start | bytes 1916936 | tf_op jit(solution)/shard_map/ppermute | solution.py:1075
  299.5 28.5 %collective-permute-start.33 = (bf16[4,104,768]{2,1,0:T(8,128)(2,1)S(1)}, bf16[4,104,768]{2,1,0:T(8,128)(2,1)S(1)}, u32[]{:S(2)}, u32[]{:S(2)}) collective-permute-start(bf16[4,104,768]{2,1,0:T(8,128)(2,1)S(1)} %get-tuple-element.344), channel_id=1, source_target_pairs={{0,8},{4,12},{8,0},{12,4},{16,24},{20,28},{24,16},{28,20},{1,9},{5... | collective-permute-start | bytes 1916936 | tf_op jit(solution)/shard_map/ppermute | solution.py:1075
  (52 other events, 453.5 us)
